TPU v7x, 32 devices: a whole 2x2x4 slice. The times are simulated.
32 devices in a mesh: user: 8 (over z, x), grp: 4 (over y, core).
Axes of the slice: x: 2, y: 2, z: 4, core: 2. Of those that a mesh axis runs over, the one named last changes fastest.
Arguments:
- user_factors: bfloat16 [32768, 128], P(('user', 'grp')), may hold values from -0.4 to 0.4
- tile_user: int32 [32, 384, 128], P(('user', 'grp')), may hold values from 0 to 1023
- tile_count: int32 [32, 384, 128], P(('user', 'grp')), may hold values from 1 to 8
- tile_valid: int32 [32, 384], P(('user', 'grp')), may hold values from 1 to 128
- tile_item: int32 [32, 384], P(('user', 'grp')), may hold values from 0 to 127, never falling along the last dimension, each value on 1 to 32 neighbouring positions
- prev_items: float32 [128, 128], P(('user', 'grp')), may hold values from -2 to 2
Outputs:
- item_factors: float32 [128, 128], P(('user', 'grp'))
- user_rhs: float32 [32768, 128], P(('user', 'grp'))
Inputs may be any that keep to these rules, and one draw needn't show every extreme that they name: `tile_item`: within the tiles of one user block the item ids never fall, and every item has 1 to 32 tiles in every user block.
All inputs are finite; a program needn't handle non-finite values.
Results may differ from a plain program's by a relative error of at most 0.0021.
Values may be sent and summed in bfloat16 or wider, within the bound.
No kernel may reach another device: no remote copies, remote signals or barrier semaphores. Data moves between devices by JAX's collectives and lax.ppermute only.
A program may use at most 128 MiB of HBM per device.

v0:
```python
import jax
import jax.numpy as jnp
from jax import lax
from jax.sharding import PartitionSpec as P

CG_STEPS = 4


confidence_rate = 0.5
ridge_weight = 1.0
block_tiles = 64


def tile_weights(counts, valid):
    positions = lax.broadcasted_iota(jnp.int32, counts.shape, counts.ndim - 1)
    live_rows = positions < valid[..., None]
    excess = jnp.where(live_rows, confidence_rate * counts.astype(jnp.float32), jnp.float32(0.0))
    confidence = jnp.where(live_rows, 1.0 + excess, jnp.float32(0.0))
    return (excess, confidence)


def accumulate(user_factors, users, excess, confidence, item_ids, num_items):
    num_tiles, tile_rows = users.shape
    block_users, factor_rank = user_factors.shape
    block_count = num_tiles // block_tiles

    def block_step(totals, scanned):
        slab_gram, slab_rhs, weights = totals
        users_blk, excess_blk, conf_blk, items_blk = scanned
        user_pick = (
            users_blk[..., None] == lax.broadcasted_iota(jnp.int32, (1, 1, block_users), 2)
        ).astype(jnp.bfloat16)
        gathered = jnp.einsum(
            "tru,ua->tra", user_pick, user_factors, preferred_element_type=jnp.float32
        ).astype(jnp.bfloat16)
        weighted = (excess_blk[..., None] * gathered).astype(jnp.bfloat16)
        part_gram = jnp.einsum(
            "tra,trb->tab", gathered, weighted, preferred_element_type=jnp.float32
        )
        conf_half = conf_blk.astype(jnp.bfloat16)
        part_rhs = jnp.einsum("tr,tra->ta", conf_half, gathered, preferred_element_type=jnp.float32)
        tile_users = jnp.einsum(
            "tru,tr->tu", user_pick, conf_half, preferred_element_type=jnp.float32
        )
        item_pick = (
            items_blk[:, None] == lax.broadcasted_iota(jnp.int32, (1, num_items), 1)
        ).astype(jnp.float32)
        slab_gram = slab_gram + jnp.dot(
            item_pick.T,
            part_gram.reshape(block_tiles, factor_rank * factor_rank),
            precision=lax.Precision.HIGHEST,
        ).reshape(num_items, factor_rank, factor_rank)
        slab_rhs = slab_rhs + jnp.dot(item_pick.T, part_rhs, precision=lax.Precision.HIGHEST)
        weights = weights + jnp.dot(tile_users.T, item_pick, precision=lax.Precision.HIGHEST)
        return ((slab_gram, slab_rhs, weights), None)

    initial = (
        jnp.zeros((num_items, factor_rank, factor_rank), jnp.float32),
        jnp.zeros((num_items, factor_rank), jnp.float32),
        jnp.zeros((block_users, num_items), jnp.float32),
    )
    scanned = (
        users.reshape(block_count, block_tiles, tile_rows),
        excess.reshape(block_count, block_tiles, tile_rows),
        confidence.reshape(block_count, block_tiles, tile_rows),
        item_ids.reshape(block_count, block_tiles),
    )
    (slab_gram, slab_rhs, weights), _ = lax.scan(block_step, initial, scanned)
    return (slab_gram, slab_rhs, weights)


def conjugate(system, rhs_total, start):

    def apply_system(vector):
        return jnp.einsum("iab,ib->ia", system, vector, precision=lax.Precision.HIGHEST)

    solution = start
    residual = rhs_total - apply_system(solution)
    direction = residual
    norm_now = jnp.sum(residual * residual, axis=1, keepdims=True)
    for iteration in range(CG_STEPS):
        product_vec = apply_system(direction)
        step_size = norm_now / jnp.sum(direction * product_vec, axis=1, keepdims=True)
        solution = solution + step_size * direction
        residual = residual - step_size * product_vec
        norm_next = jnp.sum(residual * residual, axis=1, keepdims=True)
        direction = residual + norm_next / norm_now * direction
        norm_now = norm_next
    return solution


def shards(user_factors, tile_user, tile_count, tile_valid, tile_item, prev_items):
    user_devices = lax.axis_size("user")
    group_devices = lax.axis_size("grp")
    item_dev, factor_rank = prev_items.shape
    num_items = item_dev * user_devices * group_devices
    users = tile_user[0]
    item_ids = tile_item[0]
    excess, confidence = tile_weights(tile_count[0], tile_valid[0])
    local_gram = lax.dot_general(
        user_factors, user_factors, (((0,), (0,)), ((), ())), preferred_element_type=jnp.float32
    )
    user_gram = lax.psum(local_gram, ("user", "grp"))
    slab_gram, slab_rhs, weights = accumulate(
        user_factors, users, excess, confidence, item_ids, num_items
    )
    system, rhs_total = (
        lax.psum_scatter(slab_gram, ("user", "grp"), scatter_dimension=0, tiled=True),
        lax.psum_scatter(slab_rhs, ("user", "grp"), scatter_dimension=0, tiled=True),
    )
    system = system + user_gram[None]
    identity = jnp.eye(factor_rank, dtype=jnp.float32)
    system = system + ridge_weight * identity[None]
    solution = conjugate(system, rhs_total, prev_items)
    returned = lax.all_gather(solution.astype(jnp.bfloat16), ("user", "grp"), axis=0, tiled=True)
    user_rhs = jnp.dot(weights, returned.astype(jnp.float32), precision=lax.Precision.HIGHEST)
    return (solution, user_rhs)


def solution(mesh):
    return jax.shard_map(
        shards,
        mesh=mesh,
        in_specs=(
            P(("user", "grp"), None),
            P(("user", "grp"), None, None),
            P(("user", "grp"), None, None),
            P(("user", "grp"), None),
            P(("user", "grp"), None),
            P(("user", "grp"), None),
        ),
        out_specs=(P(("user", "grp"), None), P(("user", "grp"), None)),
        check_vma=False,
    )
```

profile of v0, /device:TPU:0, one launch (start us, length us, event | category | flops | bytes accessed | tf_op | source)
XLA Modules:
  0.0 530.1 jit_solution(12085113631159364440)
XLA Ops:
  7.2 0.9 convert_multiply_fusion
  10.0 1.9 fusion.42
  11.9 187.1 %while.15 = (s32[]{:T(128)}, f32[128,128,128]{2,0,1:T(8,128)}, f32[128,128]{1,0:T(8,128)S(1)}, f32[1024,128]{1,0:T(8,128)S(1)}, s32[6,64]{1,0:T(8,128)S(1)}, /*i...) while((s32[]{:T(128)}, f32[128,128,128]{2,0,1:T(8,128)}, ...), condition=%wide.region_1.2_spmd.clone, body=%wide.region_0.1_spmd.clone.sunk | while | flops 4184137728 | bytes 100894144 | solution.py:68
  12.7 7.7 %fusion.81 = bf16[64,128,128]{2,1,0:T(8,128)(2,1)S(1)} fusion(s32[64,128]{1,0:T(8,128)S(1)} %dynamic-slice_bitcast_fusion.4, bf16[1024,128]{1,0:T(8,128)(2,1)} %get-tuple-element.193), kind=kOutput, calls=%fused_computation.13.clone.1 | convolution fusion | flops 2156920832 | bytes 2392064 | tf_op jit(solution)/shard_map/while/body/eval_jaxpr/tru,ua->tra/dot_general | solution.py:33
  21.4 2.5 fusion.82
  23.9 0.8 copy-done
  24.8 11.1 %select_add_fusion.2 = f32[128,128,128]{2,0,1:T(8,128)S(1)} fusion(f32[128,128,128]{2,0,1:T(8,128)S(1)} %copy-done, pred[]{:T(512)S(6)} %compare.3, s32[64]{0:T(128)S(1)} %fusion.80, f32[8,8,128,128]{3,2,1,0:T(8,128)S(1)} %bitcast.107), kind=kOutput, calls=%fused_computation.5.clone.1 | convolution fusion | flops 1614815232 | bytes 20971776 | tf_op jit(solution)/shard_map/while/body/eval_jaxpr/dot_general | solution.py:48
  35.9 6.4 %fusion.85 = f32[64,1,1024]{2,1,0:T(1,128)S(1)} fusion(s32[64,128]{1,0:T(8,128)S(1)} %dynamic-slice_bitcast_fusion.4, bf16[64,128,1]{1,0,2:T(8,128)(2,1)S(1)} %fusion.83), kind=kOutput, calls=%fused_computation.1.clone.1 | convolution fusion | flops 25165824 | bytes 311296 | tf_op jit(solution)/shard_map/while/body/eval_jaxpr/tru,tr->tu/dot_general | solution.py:42
  42.3 0.8 convolution_add_fusion.5
  43.8 7.7 %fusion.81 = bf16[64,128,128]{2,1,0:T(8,128)(2,1)S(1)} fusion(s32[64,128]{1,0:T(8,128)S(1)} %dynamic-slice_bitcast_fusion.4, bf16[1024,128]{1,0:T(8,128)(2,1)} %get-tuple-element.193), kind=kOutput, calls=%fused_computation.13.clone.1 | convolution fusion | flops 2156920832 | bytes 2392064 | tf_op jit(solution)/shard_map/while/body/eval_jaxpr/tru,ua->tra/dot_general | solution.py:33
  52.5 2.5 fusion.82
  55.1 0.8 copy-done
  55.9 11.1 %select_add_fusion.2 = f32[128,128,128]{2,0,1:T(8,128)S(1)} fusion(f32[128,128,128]{2,0,1:T(8,128)S(1)} %copy-done, pred[]{:T(512)S(6)} %compare.3, s32[64]{0:T(128)S(1)} %fusion.80, f32[8,8,128,128]{3,2,1,0:T(8,128)S(1)} %bitcast.107), kind=kOutput, calls=%fused_computation.5.clone.1 | convolution fusion | flops 1614815232 | bytes 20971776 | tf_op jit(solution)/shard_map/while/body/eval_jaxpr/dot_general | solution.py:48
  67.0 6.4 %fusion.85 = f32[64,1,1024]{2,1,0:T(1,128)S(1)} fusion(s32[64,128]{1,0:T(8,128)S(1)} %dynamic-slice_bitcast_fusion.4, bf16[64,128,1]{1,0,2:T(8,128)(2,1)S(1)} %fusion.83), kind=kOutput, calls=%fused_computation.1.clone.1 | convolution fusion | flops 25165824 | bytes 311296 | tf_op jit(solution)/shard_map/while/body/eval_jaxpr/tru,tr->tu/dot_general | solution.py:42
  73.4 0.8 convolution_add_fusion.5
  75.0 7.7 %fusion.81 = bf16[64,128,128]{2,1,0:T(8,128)(2,1)S(1)} fusion(s32[64,128]{1,0:T(8,128)S(1)} %dynamic-slice_bitcast_fusion.4, bf16[1024,128]{1,0:T(8,128)(2,1)} %get-tuple-element.193), kind=kOutput, calls=%fused_computation.13.clone.1 | convolution fusion | flops 2156920832 | bytes 2392064 | tf_op jit(solution)/shard_map/while/body/eval_jaxpr/tru,ua->tra/dot_general | solution.py:33
  83.7 2.5 fusion.82
  86.2 0.8 copy-done
  87.1 11.1 %select_add_fusion.2 = f32[128,128,128]{2,0,1:T(8,128)S(1)} fusion(f32[128,128,128]{2,0,1:T(8,128)S(1)} %copy-done, pred[]{:T(512)S(6)} %compare.3, s32[64]{0:T(128)S(1)} %fusion.80, f32[8,8,128,128]{3,2,1,0:T(8,128)S(1)} %bitcast.107), kind=kOutput, calls=%fused_computation.5.clone.1 | convolution fusion | flops 1614815232 | bytes 20971776 | tf_op jit(solution)/shard_map/while/body/eval_jaxpr/dot_general | solution.py:48
  98.2 6.4 %fusion.85 = f32[64,1,1024]{2,1,0:T(1,128)S(1)} fusion(s32[64,128]{1,0:T(8,128)S(1)} %dynamic-slice_bitcast_fusion.4, bf16[64,128,1]{1,0,2:T(8,128)(2,1)S(1)} %fusion.83), kind=kOutput, calls=%fused_computation.1.clone.1 | convolution fusion | flops 25165824 | bytes 311296 | tf_op jit(solution)/shard_map/while/body/eval_jaxpr/tru,tr->tu/dot_general | solution.py:42
  104.6 0.8 convolution_add_fusion.5
  106.1 7.7 %fusion.81 = bf16[64,128,128]{2,1,0:T(8,128)(2,1)S(1)} fusion(s32[64,128]{1,0:T(8,128)S(1)} %dynamic-slice_bitcast_fusion.4, bf16[1024,128]{1,0:T(8,128)(2,1)} %get-tuple-element.193), kind=kOutput, calls=%fused_computation.13.clone.1 | convolution fusion | flops 2156920832 | bytes 2392064 | tf_op jit(solution)/shard_map/while/body/eval_jaxpr/tru,ua->tra/dot_general | solution.py:33
  114.9 2.5 fusion.82
  117.4 0.8 copy-done
  118.2 11.1 %select_add_fusion.2 = f32[128,128,128]{2,0,1:T(8,128)S(1)} fusion(f32[128,128,128]{2,0,1:T(8,128)S(1)} %copy-done, pred[]{:T(512)S(6)} %compare.3, s32[64]{0:T(128)S(1)} %fusion.80, f32[8,8,128,128]{3,2,1,0:T(8,128)S(1)} %bitcast.107), kind=kOutput, calls=%fused_computation.5.clone.1 | convolution fusion | flops 1614815232 | bytes 20971776 | tf_op jit(solution)/shard_map/while/body/eval_jaxpr/dot_general | solution.py:48
  129.4 6.4 %fusion.85 = f32[64,1,1024]{2,1,0:T(1,128)S(1)} fusion(s32[64,128]{1,0:T(8,128)S(1)} %dynamic-slice_bitcast_fusion.4, bf16[64,128,1]{1,0,2:T(8,128)(2,1)S(1)} %fusion.83), kind=kOutput, calls=%fused_computation.1.clone.1 | convolution fusion | flops 25165824 | bytes 311296 | tf_op jit(solution)/shard_map/while/body/eval_jaxpr/tru,tr->tu/dot_general | solution.py:42
  135.7 0.8 convolution_add_fusion.5
  137.3 7.7 %fusion.81 = bf16[64,128,128]{2,1,0:T(8,128)(2,1)S(1)} fusion(s32[64,128]{1,0:T(8,128)S(1)} %dynamic-slice_bitcast_fusion.4, bf16[1024,128]{1,0:T(8,128)(2,1)} %get-tuple-element.193), kind=kOutput, calls=%fused_computation.13.clone.1 | convolution fusion | flops 2156920832 | bytes 2392064 | tf_op jit(solution)/shard_map/while/body/eval_jaxpr/tru,ua->tra/dot_general | solution.py:33
  146.0 2.5 fusion.82
  148.6 0.8 copy-done
  149.4 11.1 %select_add_fusion.2 = f32[128,128,128]{2,0,1:T(8,128)S(1)} fusion(f32[128,128,128]{2,0,1:T(8,128)S(1)} %copy-done, pred[]{:T(512)S(6)} %compare.3, s32[64]{0:T(128)S(1)} %fusion.80, f32[8,8,128,128]{3,2,1,0:T(8,128)S(1)} %bitcast.107), kind=kOutput, calls=%fused_computation.5.clone.1 | convolution fusion | flops 1614815232 | bytes 20971776 | tf_op jit(solution)/shard_map/while/body/eval_jaxpr/dot_general | solution.py:48
  160.5 6.4 %fusion.85 = f32[64,1,1024]{2,1,0:T(1,128)S(1)} fusion(s32[64,128]{1,0:T(8,128)S(1)} %dynamic-slice_bitcast_fusion.4, bf16[64,128,1]{1,0,2:T(8,128)(2,1)S(1)} %fusion.83), kind=kOutput, calls=%fused_computation.1.clone.1 | convolution fusion | flops 25165824 | bytes 311296 | tf_op jit(solution)/shard_map/while/body/eval_jaxpr/tru,tr->tu/dot_general | solution.py:42
  166.9 0.8 convolution_add_fusion.5
  168.4 7.7 %fusion.81 = bf16[64,128,128]{2,1,0:T(8,128)(2,1)S(1)} fusion(s32[64,128]{1,0:T(8,128)S(1)} %dynamic-slice_bitcast_fusion.4, bf16[1024,128]{1,0:T(8,128)(2,1)} %get-tuple-element.193), kind=kOutput, calls=%fused_computation.13.clone.1 | convolution fusion | flops 2156920832 | bytes 2392064 | tf_op jit(solution)/shard_map/while/body/eval_jaxpr/tru,ua->tra/dot_general | solution.py:33
  177.2 2.5 fusion.82
  179.7 0.8 copy-done
  180.5 11.1 %select_add_fusion.2 = f32[128,128,128]{2,0,1:T(8,128)S(1)} fusion(f32[128,128,128]{2,0,1:T(8,128)S(1)} %copy-done, pred[]{:T(512)S(6)} %compare.3, s32[64]{0:T(128)S(1)} %fusion.80, f32[8,8,128,128]{3,2,1,0:T(8,128)S(1)} %bitcast.107), kind=kOutput, calls=%fused_computation.5.clone.1 | convolution fusion | flops 1614815232 | bytes 20971776 | tf_op jit(solution)/shard_map/while/body/eval_jaxpr/dot_general | solution.py:48
  191.7 6.4 %fusion.85 = f32[64,1,1024]{2,1,0:T(1,128)S(1)} fusion(s32[64,128]{1,0:T(8,128)S(1)} %dynamic-slice_bitcast_fusion.4, bf16[64,128,1]{1,0,2:T(8,128)(2,1)S(1)} %fusion.83), kind=kOutput, calls=%fused_computation.1.clone.1 | convolution fusion | flops 25165824 | bytes 311296 | tf_op jit(solution)/shard_map/while/body/eval_jaxpr/tru,tr->tu/dot_general | solution.py:42
  199.7 11.5 %copy.13 = f32[128,128,128]{2,1,0:T(8,128)} copy(f32[128,128,128]{2,0,1:T(8,128)} %get-tuple-element.52) | data formatting | bytes 16777216 | tf_op jit(solution)/shard_map/while | solution.py:68
  211.2 114.1 %all-reduce.4.cloned.1.call-done = (f32[128,128]{1,0:T(8,128)}, f32[128,128]{1,0:T(8,128)}) async-done(((f32[128,128]{1,0:T(8,128)}, f32[128,128]{1,0:T(8,128)}), (f32[128,128]{1,0:T(8,128)}, f32[128,128]{1,0:T(8,128)})) %all-reduce.4.cloned.1.call-update) | async-done | bytes 131088 | tf_op jit(solution)/shard_map/psum | solution.py:103
  325.3 150.3 %reduce-scatter.2.cloned.1.call-done = f32[4,128,128]{2,1,0:T(8,128)} async-done(((f32[128,128,128]{2,1,0:T(8,128)}), f32[4,128,128]{2,1,0:T(8,128)}) %reduce-scatter.2.cloned.1.call-update) | async-done | bytes 262160 | tf_op jit(solution)/shard_map/reduce_scatter | solution.py:108
  475.6 1.5 fusion.30
  477.8 1.5 fusion.29
  479.7 1.5 fusion.28
  481.6 1.5 fusion.27
  483.5 1.5 fusion.26
  485.8 36.4 %all-gather = bf16[32,4,128]{2,1,0:T(4,128)(2,1)S(1)} all-gather(bf16[1,4,128]{2,1,0:T(4,128)(2,1)S(1)} %get-tuple-element.106), channel_id=1, replica_groups=mesh['user'=8,'grp'=4] {'user','grp'}, dimensions={0}, use_global_device_ids=true | all-gather | bytes 33792 | tf_op jit(solution)/shard_map/all_gather | solution.py:115
  522.1 1.2 fusion.43
  (92 shorter events, 16.8 us)
Async XLA Ops:
  7.2 318.1 %all-reduce.4.cloned.1.call-start = ((), (), s32[]{:S(2)}) async-start(), calls=%async_computation.2 | async-start | bytes 262144 | tf_op jit(solution)/shard_map/psum | solution.py:103
  21.4 3.4 copy-start
  35.9 6.4 %copy-start.1 = (f32[128,128,128]{2,0,1:T(8,128)}, f32[128,128,128]{2,0,1:T(8,128)S(1)}, u32[]{:S(2)}) copy-start(f32[128,128,128]{2,0,1:T(8,128)S(1)} %select_add_fusion.2) | copy-start | bytes 25165828 | tf_op jit(solution)/shard_map/while
  52.5 3.4 copy-start
  67.0 6.4 %copy-start.1 = (f32[128,128,128]{2,0,1:T(8,128)}, f32[128,128,128]{2,0,1:T(8,128)S(1)}, u32[]{:S(2)}) copy-start(f32[128,128,128]{2,0,1:T(8,128)S(1)} %select_add_fusion.2) | copy-start | bytes 25165828 | tf_op jit(solution)/shard_map/while
  83.7 3.4 copy-start
  98.2 6.4 %copy-start.1 = (f32[128,128,128]{2,0,1:T(8,128)}, f32[128,128,128]{2,0,1:T(8,128)S(1)}, u32[]{:S(2)}) copy-start(f32[128,128,128]{2,0,1:T(8,128)S(1)} %select_add_fusion.2) | copy-start | bytes 25165828 | tf_op jit(solution)/shard_map/while
  114.8 3.4 copy-start
  129.3 6.4 %copy-start.1 = (f32[128,128,128]{2,0,1:T(8,128)}, f32[128,128,128]{2,0,1:T(8,128)S(1)}, u32[]{:S(2)}) copy-start(f32[128,128,128]{2,0,1:T(8,128)S(1)} %select_add_fusion.2) | copy-start | bytes 25165828 | tf_op jit(solution)/shard_map/while
  146.0 3.4 copy-start
  160.5 6.4 %copy-start.1 = (f32[128,128,128]{2,0,1:T(8,128)}, f32[128,128,128]{2,0,1:T(8,128)S(1)}, u32[]{:S(2)}) copy-start(f32[128,128,128]{2,0,1:T(8,128)S(1)} %select_add_fusion.2) | copy-start | bytes 25165828 | tf_op jit(solution)/shard_map/while
  177.2 3.4 copy-start
  191.7 6.4 %copy-start.1 = (f32[128,128,128]{2,0,1:T(8,128)}, f32[128,128,128]{2,0,1:T(8,128)S(1)}, u32[]{:S(2)}) copy-start(f32[128,128,128]{2,0,1:T(8,128)S(1)} %select_add_fusion.2) | copy-start | bytes 25165828 | tf_op jit(solution)/shard_map/while
  199.0 0.6 copy-start.2
  199.7 276.0 %reduce-scatter.2.cloned.1.call-start = ((), (), s32[]{:S(2)}) async-start(), calls=%async_computation.1 | async-start | bytes 8650752 | tf_op jit(solution)/shard_map/reduce_scatter | solution.py:108
  211.2 264.5 %copy-start.3 = (f32[4,128]{1,0:T(4,128)S(1)}, f32[4,128]{1,0:T(4,128)}, u32[]{:S(2)}) copy-start(f32[4,128]{1,0:T(4,128)} %param.13) | copy-start | bytes 6148
Sparse Core Ops, SparseCore 0:
  199.8 125.4 all-reduce.3
  327.6 148.0 reduce-scatter.1
where the time goes:
time: 531 us; the launch traced here: 530 us
  waiting for transfers between devices  264 us (50%)
  matrix products  187 us (35%)
  blocking collectives  36.4 us (7%)
  local copies, waits for them, and re-layouts  22 us (4%)
  between operations  14.2 us (3%)
    reduce_scatter x1, waiting for transfers between devices, shards(): lax.psum_scatter(slab_gram, ('user', 'grp'), scatter_dimension=0, tiled=T...  150 us
    psum x1, waiting for transfers between devices, shards(): user_gram = lax.psum(local_gram, ('user', 'grp'))  114 us
    dot_general x6, matrix products, block_step(): jnp.dot(item_pick.T, part_gram.reshape(block_tiles, factor_rank * factor_...  66.7 us
    dot_general x6, matrix products, block_step(): jnp.einsum('tru,ua->tra', user_pick, user_factors, preferred_element_type...  45.9 us
    dot_general x6, matrix products, block_step(): jnp.einsum('tru,tr->tu', user_pick, conf_half, preferred_element_type=jnp...  38.2 us
    all_gather x1, blocking collectives, shards(): lax.all_gather(solution.astype(jnp.bfloat16), ('user', 'grp'), axis=0, ti...  36.4 us
    dot_general x6, matrix products, block_step(): jnp.einsum('tra,trb->tab', gathered, weighted, preferred_element_type=jnp...  15.2 us
    while x1, local copies, waits for them, and re-layouts, accumulate(): (slab_gram, slab_rhs, weights), _ = lax.scan(block_step, initial, scanned)  11.5 us
  transfers between devices with their start and end apart: 2, of which 2 were waited for; matrix products, arithmetic and copies ran while one was open for 2% of the time, Pallas kernels for 0%

commit v1 on v0

v1 whole, which is shorter than its diff:
```python
import functools

import jax
import jax.numpy as jnp
from jax import lax
from jax.experimental import pallas as pl
from jax.experimental.pallas import tpu as pltpu
from jax.sharding import PartitionSpec as P

CG_STEPS = 4
bf16, f32, i32 = jnp.bfloat16, jnp.float32, jnp.int32
AXES = ("user", "grp")
VMEM = pl.BlockSpec(memory_space=pltpu.VMEM)
SMEM = pl.BlockSpec(memory_space=pltpu.SMEM)
struct = jax.ShapeDtypeStruct

confidence_rate = 0.5
ridge_weight = 1.0


def log2(n):
    k = n.bit_length() - 1
    assert 1 << k == n
    return k


def params(mib):
    return pltpu.CompilerParams(vmem_limit_bytes=mib << 20)


def slot_of(item, me, item_dev, n_grp, n_user):
    rel = (item >> log2(item_dev)) ^ me
    slot = item & (item_dev - 1)
    w = rel >> log2(n_grp)
    per, left = n_user * item_dev, n_user
    k = (rel & (n_grp - 1)) * per
    while left > 4:
        per, left = per // 2, left // 2
        k = k + (w & 1) * per
        w = w >> 1
    return k + w * item_dev + slot


def owner_of(group, item_dev, n_grp, n_user):
    k, w = divmod(group, n_user)
    bits, left, at = 0, n_user, 0
    while left > 4:
        left //= 2
        bits |= (w // left) << at
        w %= left
        at += 1
    return (bits | (w << at)) * n_grp + k


def histogram_kernel(step, item_dev, n_grp, n_user, me_s, valid_s, item_s, users, counts, u, *rest):
    eouts = rest[:n_grp]
    c_hi, c_lo, acc = rest[n_grp:]
    tiles, rows = users.shape[1:]
    num_items = c_hi.shape[0]
    block_users = u.shape[0]
    his = block_users // 128
    me = me_s[0]
    acc[...] = jnp.zeros_like(acc)
    lane = lax.broadcasted_iota(i32, (8, rows), 1)
    sub = lax.broadcasted_iota(i32, (8, rows), 0)
    iota = lax.broadcasted_iota(i32, (128, rows), 0).astype(f32).astype(bf16)
    zero = jnp.zeros((16, rows), bf16)
    one, nil = jnp.ones((128, rows), bf16), jnp.zeros((128, rows), bf16)

    def body(b, _):
        base = pl.multiple_of(b * step, step)
        blk = users[0, pl.ds(base, step), :]
        cnt = counts[0, pl.ds(base, step), :].astype(f32) * confidence_rate
        lo = (blk & 127).astype(f32)
        hi = blk >> 7
        for t in range(0, step, 2):
            oh, lhs = [], []
            for j in (t, t + 1):
                lob = jnp.broadcast_to(lo[j : j + 1], (16, rows)).astype(bf16)
                oh.append(jnp.where(jnp.concatenate([lob] * 8, 0) == iota, one, nil))
                on = (lane < valid_s[0, base + j]) & (jnp.broadcast_to(hi[j : j + 1], (8, rows)) == sub)
                ex = jnp.broadcast_to(cnt[j : j + 1], (8, rows))
                lhs.append(
                    jnp.concatenate([jnp.where(on, ex, 0.0), jnp.where(on, 1.0 + ex, 0.0)], 0).astype(bf16)
                )
            left = jnp.concatenate(
                [jnp.concatenate([lhs[0], zero], 1), jnp.concatenate([zero, lhs[1]], 1)], 0
            )
            out = lax.dot_general(
                left, jnp.concatenate(oh, 1), (((1,), (1,)), ((), ())), preferred_element_type=f32
            )
            for q, j in enumerate((t, t + 1)):
                p = slot_of(item_s[0, base + j], me, item_dev, n_grp, n_user)
                acc[pl.ds(pl.multiple_of(p * 16, 16), 16), :] += out[16 * q : 16 * q + 16]
        return 0

    lax.fori_loop(0, tiles // step, body, 0)
    per = num_items // n_grp
    for h in range(his):
        e = (acc[pl.ds(h, num_items, stride=16), :] + 1.0).astype(bf16)
        for k in range(n_grp):
            eouts[k][:, h * 128 : (h + 1) * 128] = e[k * per : (k + 1) * per]
        c = acc[pl.ds(8 + h, num_items, stride=16), :]
        ch = c.astype(bf16)
        c_hi[:, h * 128 : (h + 1) * 128] = ch
        c_lo[:, h * 128 : (h + 1) * 128] = (c - ch.astype(f32)).astype(bf16)
    uu = u[...]
    r = jnp.dot(c_hi[...], uu, preferred_element_type=f32) + jnp.dot(c_lo[...], uu, preferred_element_type=f32)
    rh = r.astype(bf16)
    rl = (r - rh.astype(f32)).astype(bf16)
    for k in range(n_grp):
        eouts[k][:, block_users : block_users + 128] = rh[k * per : (k + 1) * per]
        eouts[k][:, block_users + 128 :] = rl[k * per : (k + 1) * per]


def histogram(me, valid, item, users, counts, u, num_items, item_dev, n_grp, n_user):
    block_users, rank = u.shape
    step = 16
    return pl.pallas_call(
        functools.partial(histogram_kernel, step, item_dev, n_grp, n_user),
        in_specs=[SMEM, SMEM, SMEM, VMEM, VMEM, VMEM],
        out_specs=[VMEM] * (n_grp + 2),
        out_shape=[struct((num_items // n_grp, block_users + 2 * rank), bf16)] * n_grp
        + [struct((num_items, block_users), bf16)] * 2,
        scratch_shapes=[pltpu.VMEM((num_items * 16, 128), f32)],
        compiler_params=params(32),
        name="histogram",
    )(me, valid, item, users, counts, u)


def transpose_kernel(*refs):
    *us, ut = refs
    block_users = us[0].shape[0]
    for b, u in enumerate(us):
        for c in range(block_users // 128):
            at = b * block_users + c * 128
            ut[:, at : at + 128] = u[c * 128 : (c + 1) * 128, :].T


def transposed(us):
    block_users, rank = us[0].shape
    return pl.pallas_call(
        transpose_kernel,
        in_specs=[VMEM] * len(us),
        out_specs=VMEM,
        out_shape=struct((rank, block_users * len(us)), bf16),
        compiler_params=params(16),
        name="transpose",
    )(*us)


def chunk_rows(item_dev):
    return 64 * item_dev + -(-4 * item_dev // 16) * 16


def systems_kernel(first, n_items, item_dev, keep, n_grp, *refs):
    es, us, ut, out, ef = refs[:n_grp], refs[n_grp : 2 * n_grp], refs[2 * n_grp], refs[2 * n_grp + 1], refs[-1]
    block_users, rank = us[0].shape
    span = slice(first, first + n_items)
    for b in range(n_grp):
        e = es[b][span, :block_users].astype(f32)
        for c in range(n_items // item_dev):
            ef[c, :, b * block_users : (b + 1) * block_users] = e[c * item_dev : (c + 1) * item_dev]
    rhs = jnp.zeros((n_items, rank), f32)
    for b in range(n_grp):
        rhs = rhs + es[b][span, block_users : block_users + rank].astype(f32)
        rhs = rhs + es[b][span, block_users + rank :].astype(f32)
    for c in range(n_items // item_dev):
        ef[c, :, n_grp * block_users :] = rhs[c * item_dev : (c + 1) * item_dev]
    row = lax.broadcasted_iota(i32, (64, rank), 0)
    lane = lax.broadcasted_iota(i32, (64, rank), 1)
    eye = lax.broadcasted_iota(i32, (rank, rank), 0) == lax.broadcasted_iota(i32, (rank, rank), 1)
    above = (lane < 64) & (lane > row)
    base = 64 * item_dev

    def body(c, _):
        total = None
        for b in range(n_grp):
            cols = slice(b * block_users, (b + 1) * block_users)
            w = []
            for j in range(item_dev):
                e = ef[c, j : j + 1, cols]
                e = jnp.broadcast_to(e, (16, block_users)).astype(bf16)
                w.append(jnp.concatenate([e] * (rank // 16), 0) * ut[:, cols])
            g = jnp.dot(jnp.concatenate(w, 0), us[b][...], preferred_element_type=f32)
            total = g if total is None else total + g
        diag = []
        for j in range(item_dev):
            g = total[j * rank : (j + 1) * rank]
            packed = jnp.where(above, pltpu.roll(g[64:], 64, 1), g[:64])
            out[c, 64 * j : 64 * j + 64, :] = packed.astype(out.dtype)
            diag.append(jnp.sum(jnp.where(eye, g, 0.0), axis=0, keepdims=True))
        diag = jnp.concatenate(diag, 0)
        side = ef[c, :, n_grp * block_users :]
        put_extras(lambda a, n, v: out.__setitem__((c, slice(base + a, base + a + n)), v), diag, side, keep, item_dev)
        return 0

    lax.fori_loop(0, n_items // item_dev, body, 0)


def put_extras(put, diag, side, keep, item_dev):
    if keep:
        nil = jnp.zeros_like(diag)
        rows = [diag, nil, side, nil]
    else:
        rows = []
        for v in (diag, side):
            high = v.astype(bf16).astype(f32)
            rows += [high, v - high]
    pad = -4 * item_dev % 16
    if pad:
        rows.append(jnp.zeros((pad, diag.shape[1]), f32))
    value = jnp.concatenate(rows, 0)
    put(0, value.shape[0], value if keep else value.astype(bf16))


def systems(es, us, ut, first, n_items, item_dev, keep):
    n_grp = len(es)
    block_users, rank = us[0].shape
    return pl.pallas_call(
        functools.partial(systems_kernel, first, n_items, item_dev, keep, n_grp),
        in_specs=[VMEM] * (2 * n_grp + 1),
        out_specs=VMEM,
        out_shape=struct((n_items // item_dev, chunk_rows(item_dev), rank), f32 if keep else bf16),
        scratch_shapes=[pltpu.VMEM((n_items // item_dev, item_dev, n_grp * block_users + rank), f32)],
        compiler_params=params(40),
        name="systems",
    )(*es, *us, ut)


def extras(value, item_dev):
    base = 64 * item_dev
    part = [value[base + n * item_dev : base + (n + 1) * item_dev] for n in range(4)]
    return part[0] + part[1], part[2] + part[3]


def merge_kernel(item_dev, n_keep, own, got, kept, *sent):
    base = 64 * item_dev
    for c in range(own.shape[0]):
        value = own[c] + got[c].astype(f32)
        diag, side = extras(value, item_dev)
        if c < n_keep:
            kept[c, :base, :] = value[:base]
            put_extras(lambda a, n, v, c=c: kept.__setitem__((c, slice(base + a, base + a + n)), v), diag, side, True, item_dev)
        else:
            ref = sent[0] if len(sent) == 1 else sent[c - n_keep]
            lead = (c - n_keep,) if len(sent) == 1 else ()
            ref[lead + (slice(0, base),)] = value[:base].astype(bf16)
            put_extras(
                lambda a, n, v, ref=ref, lead=lead: ref.__setitem__(lead + (slice(base + a, base + a + n),), v),
                diag, side, False, item_dev,
            )


def merged(own, got, item_dev, n_keep, apart):
    chunks, rows, rank = own.shape
    n_sent = chunks - n_keep
    shapes = [struct((rows, rank), bf16)] * n_sent if apart else [struct((n_sent, rows, rank), bf16)]
    return pl.pallas_call(
        functools.partial(merge_kernel, item_dev, n_keep),
        in_specs=[VMEM] * 2,
        out_specs=[VMEM] * (1 + len(shapes)),
        out_shape=[struct((n_keep, rows, rank), f32)] + shapes,
        compiler_params=params(16),
        name="merge",
    )(own, got)


def gradients_kernel(item_dev, own, *refs):
    *got, prev, out, half = refs
    value = own[0]
    for g in got:
        value = value + g[...].astype(f32)
    rank = value.shape[1]
    diag, side = extras(value, item_dev)
    row = lax.broadcasted_iota(i32, (64, 64), 0)
    col = lax.broadcasted_iota(i32, (64, 64), 1)
    eye = lax.broadcasted_iota(i32, (rank, rank), 0) == lax.broadcasted_iota(i32, (rank, rank), 1)
    matrices = []
    for j in range(item_dev):
        m = value[64 * j : 64 * j + 64]
        t = m.T
        mix, mix_t = m[:, :64], t[:64]
        a = jnp.where(col < row, mix, mix_t)
        c = jnp.where(col > row, mix, mix_t)
        full = jnp.concatenate(
            [jnp.concatenate([a, m[:, 64:]], 1), jnp.concatenate([t[64:], c], 1)], 0
        )
        matrices.append(jnp.where(eye, diag[j : j + 1] + ridge_weight, full))

    def apply(vector):
        rows = []
        for j in range(item_dev):
            s = jnp.sum(matrices[j] * vector[j : j + 1], axis=1, keepdims=True)
            rows.append(jnp.sum(jnp.where(eye, s, 0.0), axis=0, keepdims=True))
        return jnp.concatenate(rows, 0)

    solution = prev[...]
    residual = side - apply(solution)
    direction = residual
    norm_now = jnp.sum(residual * residual, axis=1, keepdims=True)
    for _ in range(CG_STEPS):
        image = apply(direction)
        step = norm_now / jnp.sum(direction * image, axis=1, keepdims=True)
        solution = solution + step * direction
        residual = residual - step * image
        norm_next = jnp.sum(residual * residual, axis=1, keepdims=True)
        direction = residual + norm_next / norm_now * direction
        norm_now = norm_next
    out[...] = solution
    half[...] = solution.astype(bf16)


def gradients(own, got, prev):
    item_dev, rank = prev.shape
    return pl.pallas_call(
        functools.partial(gradients_kernel, item_dev),
        in_specs=[VMEM] * (2 + len(got)),
        out_specs=[VMEM] * 2,
        out_shape=[struct(prev.shape, f32), struct(prev.shape, bf16)],
        compiler_params=params(16),
        name="gradients",
    )(own, *got, prev)


def user_side_kernel(item_dev, n_grp, n_user, me_s, returned, c_hi, c_lo, out, rows, order):
    num_items = returned.shape[0]
    rows[...] = returned[...].astype(f32)
    me = me_s[0]
    for group in range(num_items // item_dev):
        owner = owner_of(group, item_dev, n_grp, n_user) ^ me
        order[group * item_dev : (group + 1) * item_dev, :] = rows[pl.ds(owner * item_dev, item_dev), :]
    ret = order[...].astype(bf16)
    dims = (((0,), (0,)), ((), ()))
    out[...] = lax.dot_general(c_hi[...], ret, dims, preferred_element_type=f32) + lax.dot_general(
        c_lo[...], ret, dims, preferred_element_type=f32
    )


def user_side(me, returned, c_hi, c_lo, item_dev, n_grp, n_user):
    num_items, rank = returned.shape
    return pl.pallas_call(
        functools.partial(user_side_kernel, item_dev, n_grp, n_user),
        in_specs=[SMEM, VMEM, VMEM, VMEM],
        out_specs=VMEM,
        out_shape=struct((c_hi.shape[1], rank), f32),
        scratch_shapes=[pltpu.VMEM((num_items, rank), f32)] * 2,
        compiler_params=params(16),
        name="user_side",
    )(me, returned, c_hi, c_lo)


def shards(user_factors, tile_user, tile_count, tile_valid, tile_item, prev_items):
    n_user = lax.axis_size("user")
    n_grp = lax.axis_size("grp")
    devices = n_user * n_grp
    item_dev, rank = prev_items.shape
    num_items = item_dev * devices
    assert n_grp == 4 and n_user >= 4 and rank == 128 and user_factors.shape[0] == 1024
    me = lax.axis_index(AXES).astype(i32).reshape(1)

    def swap(value, bit):
        return lax.ppermute(value, AXES, [(d, d ^ bit) for d in range(devices)])

    u0 = user_factors
    u2 = swap(u0, 2)
    u1 = swap(u0, 1)
    *es, c_hi, c_lo = histogram(
        me, tile_valid, tile_item, tile_user, tile_count, u0, num_items, item_dev, n_grp, n_user
    )
    u3 = swap(u2, 1)
    got = [es[0], swap(es[1], 1), swap(es[2], 2), swap(es[3], 3)]
    us = [u0, u1, u2, u3]
    ut = transposed(us)
    n_items = num_items // n_grp
    left, bit = n_user, n_grp
    n_half = n_items // 2
    sent = systems(got, us, ut, n_half, n_half, item_dev, False)
    other = swap(sent, bit)
    own = systems(got, us, ut, 0, n_half, item_dev, True)
    left, bit = left // 2, bit * 2
    while left > 4:
        own, sent = merged(own, other, item_dev, left // 2, False)
        other = swap(sent, bit)
        left, bit = left // 2, bit * 2
    own, *sent = merged(own, other, item_dev, 1, True)
    parts = [swap(value, bit * (n + 1)) for n, value in enumerate(sent)]
    solved, half = gradients(own, parts, prev_items)
    spread = jnp.broadcast_to(half[None], (devices, item_dev, rank))
    returned = lax.all_to_all(spread, AXES, 0, 0, tiled=True).reshape(num_items, rank)
    return solved, user_side(me, returned, c_hi, c_lo, item_dev, n_grp, n_user)


def solution(mesh):
    return jax.shard_map(
        shards,
        mesh=mesh,
        in_specs=(
            P(AXES, None),
            P(AXES, None, None),
            P(AXES, None, None),
            P(AXES, None),
            P(AXES, None),
            P(AXES, None),
        ),
        out_specs=(P(AXES, None), P(AXES, None)),
        check_vma=False,
    )
```

time: 531 us -> 68.3 us (0.13)
  waiting for transfers between devices: 264 us -> 18.6 us
  matrix products: 187 us -> 0 us
  blocking collectives: 36.4 us -> 11 us
  Pallas kernels: 0 us -> 22.9 us
  local copies, waits for them, and re-layouts: 22 us -> 3.51 us
  between operations: 14.2 us -> 0.69 us
  starting transfers between devices: 0.08 us -> 11.4 us
    dot_general x49 -> x0, matrix products: 187 us -> none  [the longest x6 66.7 us: block_step(): jnp.dot(item_pick.T, part_gram.reshape(block_tiles, factor_rank * factor_...]
    reduce_scatter x1 -> x0, waiting for transfers between devices: 150 us -> none  [shards(): lax.psum_scatter(slab_gram, ('user', 'grp'), scatter_dimension=0, tiled=T...]
    psum x1 -> x0, waiting for transfers between devices: 114 us -> none  [shards(): user_gram = lax.psum(local_gram, ('user', 'grp'))]
    all_gather x1 -> x0, blocking collectives: 36.4 us -> none  [shards(): lax.all_gather(solution.astype(jnp.bfloat16), ('user', 'grp'), axis=0, ti...]
    pallas_call x0 -> x7, Pallas kernels: none -> 22.9 us  [the longest x2 10.6 us: systems(): pl.pallas_call(functools.partial(systems_kernel, first, n_items, item_dev...]
    ppermute x0 -> x10, waiting for transfers between devices: none -> 18.6 us  [swap(): return lax.ppermute(value, AXES, [(d, d ^ bit) for d in range(devices)])]
    while x25 -> x0, local copies, waits for them, and re-layouts: 16.5 us -> none  [the longest x1 11.5 us: accumulate(): (slab_gram, slab_rhs, weights), _ = lax.scan(block_step, initial, scanned)]
    ppermute x0 -> x10, starting transfers between devices: none -> 11.4 us  [swap(): return lax.ppermute(value, AXES, [(d, d ^ bit) for d in range(devices)])]
  transfers between devices with their start and end apart: 2 -> 10, of which waited for: 2 -> 7; matrix products, arithmetic and copies ran while one was open for 2% -> 0% of each run, Pallas kernels for 0% -> 21%
where the time goes in v1:
time: 68.3 us; the launch traced here: 68.1 us
  Pallas kernels  22.9 us (34%)
  waiting for transfers between devices  18.6 us (27%)
  starting transfers between devices  11.4 us (17%)
  blocking collectives  11 us (16%)
  local copies, waits for them, and re-layouts  3.51 us (5%)
  between operations  0.69 us (1%)
    ppermute x10, waiting for transfers between devices, swap(): return lax.ppermute(value, AXES, [(d, d ^ bit) for d in range(devices)])  18.6 us
    ppermute x10, starting transfers between devices, swap(): return lax.ppermute(value, AXES, [(d, d ^ bit) for d in range(devices)])  11.4 us
    all_to_all x1, blocking collectives, shards(): lax.all_to_all(spread, AXES, 0, 0, tiled=True).reshape(num_items, rank)  11 us
    pallas_call x2, Pallas kernels, systems(): pl.pallas_call(functools.partial(systems_kernel, first, n_items, item_dev...  10.6 us
    pallas_call x1, Pallas kernels, histogram(): pl.pallas_call(functools.partial(histogram_kernel, step, item_dev, n_grp,...  8.65 us
    unnamed x14, local copies, waits for them, and re-layouts  3.51 us
    pallas_call x1, Pallas kernels, gradients(): pl.pallas_call(functools.partial(gradients_kernel, item_dev), in_specs=[V...  2.08 us
  transfers between devices with their start and end apart: 10, of which 7 were waited for; matrix products, arithmetic and copies ran while one was open for 0% of the time, Pallas kernels for 21%

profile of v1, /device:TPU:0, one launch (start us, length us, event | category | flops | bytes accessed | tf_op | source)
XLA Modules:
  0.0 68.1 jit_solution(15188360335927066325)
XLA Ops:
  0.6 3.0 %collective-permute-start.4 = (bf16[1024,128]{1,0:T(8,128)(2,1)}, bf16[1024,128]{1,0:T(8,128)(2,1)S(1)}, u32[]{:S(2)}, u32[]{:S(2)}) collective-permute-start(bf16[1024,128]{1,0:T(8,128)(2,1)} %refs_4_.3), channel_id=1, source_target_pairs={{0,2},{1,3},{2,0},{3,1},{4,6},{5,7},{6,4},{7,5},{8,10},{9,11},{10,... | collective-permute-start | bytes 786440 | tf_op jit(solution)/shard_map/ppermute | solution.py:363
  3.7 0.0 collective-permute-start.3
  3.7 6.5 %collective-permute-done.4.refs_2_.refs_6_ = bf16[1024,128]{1,0:T(8,128)(2,1)S(1)} collective-permute-done((bf16[1024,128]{1,0:T(8,128)(2,1)}, bf16[1024,128]{1,0:T(8,128)(2,1)S(1)}, u32[]{:S(2)}, u32[]{:S(2)}) %collective-permute-start.4) | collective-permute-done | bytes 262176 | tf_op jit(solution)/shard_map/ppermute | solution.py:363
  10.2 0.0 collective-permute-start.5
  10.2 0.0 copy-start.5
  10.2 0.0 copy-start.6
  10.2 0.7 copy-done.5
  10.9 0.0 copy-done.6
  10.9 0.0 copy-start
  10.9 0.9 %copy-done = bf16[1024,128]{1,0:T(8,128)(2,1)S(1)} copy-done((bf16[1024,128]{1,0:T(8,128)(2,1)S(1)}, bf16[1024,128]{1,0:T(8,128)(2,1)}, u32[]{:S(2)}) %copy-start) | copy-done | bytes 262168
  11.8 0.0 copy-start.2
  11.8 0.9 %copy-done.2 = s32[1,384,128]{2,1,0:T(8,128)S(1)} copy-done((s32[1,384,128]{2,1,0:T(8,128)S(1)}, s32[1,384,128]{2,1,0:T(8,128)}, u32[]{:S(2)}) %copy-start.2) | copy-done | bytes 196632
  12.8 0.0 copy-start.3
  12.8 0.9 %copy-done.3 = s32[1,384,128]{2,1,0:T(8,128)S(1)} copy-done((s32[1,384,128]{2,1,0:T(8,128)S(1)}, s32[1,384,128]{2,1,0:T(8,128)}, u32[]{:S(2)}) %copy-start.3) | copy-done | bytes 196632
  13.7 8.6 %histogram.1 = (bf16[32,1280]{1,0:T(8,128)(2,1)S(1)}, bf16[32,1280]{1,0:T(8,128)(2,1)S(1)}, bf16[32,1280]{1,0:T(8,128)(2,1)S(1)}, bf16[32,1280]{1,0:T(8,128)(2,1...) custom-call(s32[1]{0:T(128)} %bitcast.me_s, s32[1,384]{1,0:T(1,128)S(1)} %copy-done.5, ...), custom_call_target="tpu_custom_call" | custom-call | tf_op jit(solution)/shard_map/histogram/pallas_call | solution.py:119
  22.3 0.6 collective-permute-start
  22.9 1.7 %collective-permute-start.1 = (bf16[32,1280]{1,0:T(8,128)(2,1)S(1)}, bf16[32,1280]{1,0:T(8,128)(2,1)S(1)}, u32[]{:S(2)}, u32[]{:S(2)}) collective-permute-start(bf16[32,1280]{1,0:T(8,128)(2,1)S(1)} %get-tuple-element.16), channel_id=1, source_target_pairs={{0,2},{1,3},{2,0},{3,1},{4,6},{5,7},{6,4},{7,5},{8,10},{9,11},{10,... | collective-permute-start | bytes 245768 | tf_op jit(solution)/shard_map/ppermute | solution.py:363
  24.6 0.0 copy-start.1
  24.6 0.0 collective-permute-start.2
  24.7 0.0 collective-permute-done.3.refs_1_.refs_5_
  24.7 0.0 collective-permute-done.5.refs_3_.refs_7_
  24.7 0.3 transpose.2.refs_8_
  25.0 0.0 collective-permute-done.refs_1_
  25.0 2.5 %collective-permute-done.1.refs_2_ = bf16[32,1280]{1,0:T(8,128)(2,1)S(1)} collective-permute-done((bf16[32,1280]{1,0:T(8,128)(2,1)S(1)}, bf16[32,1280]{1,0:T(8,128)(2,1)S(1)}, u32[]{:S(2)}, u32[]{:S(2)}) %collective-permute-start.1) | collective-permute-done | bytes 81952 | tf_op jit(solution)/shard_map/ppermute | solution.py:363
  27.5 1.9 %collective-permute-done.2.refs_3_ = bf16[32,1280]{1,0:T(8,128)(2,1)S(1)} collective-permute-done((bf16[32,1280]{1,0:T(8,128)(2,1)S(1)}, bf16[32,1280]{1,0:T(8,128)(2,1)S(1)}, u32[]{:S(2)}, u32[]{:S(2)}) %collective-permute-start.2) | collective-permute-done | bytes 81952 | tf_op jit(solution)/shard_map/ppermute | solution.py:363
  29.4 0.0 copy-done.1
  29.4 5.3 %systems.3 = bf16[4,272,128]{2,1,0:T(8,128)(2,1)S(1)} custom-call(bf16[32,1280]{1,0:T(8,128)(2,1)S(1)} %get-tuple-element.14.refs_0_, bf16[32,1280]{1,0:T(8,128)(2,1)S(1)} %collective-permute-done.refs_1_, bf16[32,1280]{1,0:T(8,128)(2,1)S(1)} %collective-permute-done.1.refs_2_, bf16[32,1280]{1,0:T(8,128)(2,1)S(1)} %collective-permute-done.2.refs_3_, ...), custom_call_target="tpu_custom_call" | custom-call | tf_op jit(solution)/shard_map/systems/pallas_call | solution.py:220
  34.7 1.6 %collective-permute-start.6 = (bf16[4,272,128]{2,1,0:T(8,128)(2,1)S(1)}, bf16[4,272,128]{2,1,0:T(8,128)(2,1)S(1)}, u32[]{:S(2)}, u32[]{:S(2)}) collective-permute-start(bf16[4,272,128]{2,1,0:T(8,128)(2,1)S(1)} %systems.3), channel_id=1, source_target_pairs={{0,4},{1,5},{2,6},{3,7},{4,0},{5,1},{6,2},{7,3},{8,12},{9,13},{10,... | collective-permute-start | bytes 835592 | tf_op jit(solution)/shard_map/ppermute | solution.py:363
  36.2 5.3 %systems.2.own = f32[4,272,128]{2,1,0:T(8,128)S(1)} custom-call(bf16[32,1280]{1,0:T(8,128)(2,1)S(1)} %get-tuple-element.14.refs_0_, bf16[32,1280]{1,0:T(8,128)(2,1)S(1)} %collective-permute-done.refs_1_, bf16[32,1280]{1,0:T(8,128)(2,1)S(1)} %collective-permute-done.1.refs_2_, bf16[32,1280]{1,0:T(8,128)(2,1)S(1)} %collective-permute-done.2.refs_3_, ...), custom_call_target="tpu_custom_call" | custom-call | tf_op jit(solution)/shard_map/systems/pallas_call | solution.py:220
  41.5 1.9 %collective-permute-done.6.got = bf16[4,272,128]{2,1,0:T(8,128)(2,1)S(1)} collective-permute-done((bf16[4,272,128]{2,1,0:T(8,128)(2,1)S(1)}, bf16[4,272,128]{2,1,0:T(8,128)(2,1)S(1)}, u32[]{:S(2)}, u32[]{:S(2)}) %collective-permute-start.6) | collective-permute-done | bytes 278560 | tf_op jit(solution)/shard_map/ppermute | solution.py:363
  43.4 0.1 merge.1
  43.5 1.6 %collective-permute-start.7 = (bf16[272,128]{1,0:T(8,128)(2,1)S(1)}, bf16[272,128]{1,0:T(8,128)(2,1)S(1)}, u32[]{:S(2)}, u32[]{:S(2)}) collective-permute-start(bf16[272,128]{1,0:T(8,128)(2,1)S(1)} %get-tuple-element.19), channel_id=1, source_target_pairs={{0,8},{1,9},{2,10},{3,11},{4,12},{5,13},{6,14},{7,15},{8,0},{9,1},... | collective-permute-start | bytes 208904 | tf_op jit(solution)/shard_map/ppermute | solution.py:363
  45.1 0.0 copy-start.4
  45.1 2.6 %collective-permute-start.8 = (bf16[272,128]{1,0:T(8,128)(2,1)S(1)}, bf16[272,128]{1,0:T(8,128)(2,1)S(1)}, u32[]{:S(2)}, u32[]{:S(2)}) collective-permute-start(bf16[272,128]{1,0:T(8,128)(2,1)S(1)} %get-tuple-element.20), channel_id=1, source_target_pairs={{0,16},{1,17},{2,18},{3,19},{4,20},{5,21},{6,22},{7,23},{8,24},{9,... | collective-permute-start | bytes 208904 | tf_op jit(solution)/shard_map/ppermute | solution.py:363
  47.7 0.2 collective-permute-start.9
  47.9 0.6 collective-permute-done.7.refs_0_
  48.5 3.6 %collective-permute-done.8.refs_1_ = bf16[272,128]{1,0:T(8,128)(2,1)S(1)} collective-permute-done((bf16[272,128]{1,0:T(8,128)(2,1)S(1)}, bf16[272,128]{1,0:T(8,128)(2,1)S(1)}, u32[]{:S(2)}, u32[]{:S(2)}) %collective-permute-start.8) | collective-permute-done | bytes 69664 | tf_op jit(solution)/shard_map/ppermute | solution.py:363
  52.1 1.8 %collective-permute-done.9.refs_2_ = bf16[272,128]{1,0:T(8,128)(2,1)S(1)} collective-permute-done((bf16[272,128]{1,0:T(8,128)(2,1)S(1)}, bf16[272,128]{1,0:T(8,128)(2,1)S(1)}, u32[]{:S(2)}, u32[]{:S(2)}) %collective-permute-start.9) | collective-permute-done | bytes 69664 | tf_op jit(solution)/shard_map/ppermute | solution.py:363
  53.8 0.0 copy-done.4
  53.8 2.1 %gradients.1 = (f32[4,128]{1,0:T(4,128)}, bf16[4,128]{1,0:T(4,128)(2,1)S(1)}) custom-call(f32[1,272,128]{2,1,0:T(8,128)S(1)} %get-tuple-element.18.own, bf16[272,128]{1,0:T(8,128)(2,1)S(1)} %collective-permute-done.7.refs_0_, bf16[272,128]{1,0:T(8,128)(2,1)S(1)} %collective-permute-done.8.refs_1_, bf16[272,128]{1,0:T(8,128)(2,1)S(1)} %collective-permute-done.9.refs_2_, ...), custom_call_target="tpu_custom_call" | custom-call | tf_op jit(solution)/shard_map/gradients/pallas_call | solution.py:316
  55.9 11.0 %all_to_all.5 = bf16[32,4,128]{2,1,0:T(4,128)(2,1)S(1)} all-to-all(bf16[32,4,128]{2,1,0:T(4,128)(2,1)S(1)} %broadcast_in_dim.2), channel_id=1, replica_groups=mesh['user'=8,'grp'=4] {'user','grp'}, dimensions={0} | all-to-all | bytes 65536 | tf_op jit(solution)/shard_map/all_to_all | solution.py:390
  66.9 1.2 %user_side.1 = f32[1024,128]{1,0:T(8,128)} custom-call(s32[1]{0:T(128)} %bitcast.me_s, bf16[128,128]{1,0:T(8,128)(2,1)S(1)} %bitcast.2, bf16[128,1024]{1,0:T(8,128)(2,1)S(1)} %get-tuple-element.24.c_hi, bf16[128,1024]{1,0:T(8,128)(2,1)S(1)} %get-tuple-element.25.c_lo), custom_call_target="tpu_custom_call" | custom-call | tf_op jit(solution)/shard_map/user_side/pallas_call | solution.py:342
  (1 shorter events, 0.0 us)
Async XLA Ops:
  0.6 9.6 %collective-permute-start.4 = (bf16[1024,128]{1,0:T(8,128)(2,1)}, bf16[1024,128]{1,0:T(8,128)(2,1)S(1)}, u32[]{:S(2)}, u32[]{:S(2)}) collective-permute-start(bf16[1024,128]{1,0:T(8,128)(2,1)} %refs_4_.3), channel_id=1, source_target_pairs={{0,2},{1,3},{2,0},{3,1},{4,6},{5,7},{6,4},{7,5},{8,10},{9,11},{10,... | collective-permute-start | bytes 786440 | tf_op jit(solution)/shard_map/ppermute | solution.py:363
  3.7 21.0 %collective-permute-start.3 = (bf16[1024,128]{1,0:T(8,128)(2,1)}, bf16[1024,128]{1,0:T(8,128)(2,1)S(1)}, u32[]{:S(2)}, u32[]{:S(2)}) collective-permute-start(bf16[1024,128]{1,0:T(8,128)(2,1)} %refs_4_.3), channel_id=1, source_target_pairs={{0,1},{1,0},{2,3},{3,2},{4,5},{5,4},{6,7},{7,6},{8,9},{9,8},{10,11... | collective-permute-start | bytes 786440 | tf_op jit(solution)/shard_map/ppermute | solution.py:363
  10.2 14.5 %collective-permute-start.5 = (bf16[1024,128]{1,0:T(8,128)(2,1)S(1)}, bf16[1024,128]{1,0:T(8,128)(2,1)S(1)}, u32[]{:S(2)}, u32[]{:S(2)}) collective-permute-start(bf16[1024,128]{1,0:T(8,128)(2,1)S(1)} %collective-permute-done.4.refs_2_.refs_6_), channel_id=1, source_target_pairs={{0,1},{1,0},{2,3},{3,2},{4,5},{5,4},{6,7},{7,6},{8,9},{9,8},{10,11... | collective-permute-start | bytes 786440 | tf_op jit(solution)/shard_map/ppermute | solution.py:363
  10.2 0.7 %copy-start.5 = (s32[1,384]{1,0:T(1,128)S(1)}, s32[1,384]{1,0:T(1,128)}, u32[]{:S(2)}) copy-start(s32[1,384]{1,0:T(1,128)} %valid_s.1) | copy-start | bytes 4612
  10.2 0.7 %copy-start.6 = (s32[1,384]{1,0:T(1,128)S(1)}, s32[1,384]{1,0:T(1,128)}, u32[]{:S(2)}) copy-start(s32[1,384]{1,0:T(1,128)} %item_s.1) | copy-start | bytes 4612
  10.9 0.9 %copy-start = (bf16[1024,128]{1,0:T(8,128)(2,1)S(1)}, bf16[1024,128]{1,0:T(8,128)(2,1)}, u32[]{:S(2)}) copy-start(bf16[1024,128]{1,0:T(8,128)(2,1)} %refs_4_.3) | copy-start | bytes 786436
  11.8 0.9 %copy-start.2 = (s32[1,384,128]{2,1,0:T(8,128)S(1)}, s32[1,384,128]{2,1,0:T(8,128)}, u32[]{:S(2)}) copy-start(s32[1,384,128]{2,1,0:T(8,128)} %users.1) | copy-start | bytes 589828
  12.8 0.9 %copy-start.3 = (s32[1,384,128]{2,1,0:T(8,128)S(1)}, s32[1,384,128]{2,1,0:T(8,128)}, u32[]{:S(2)}) copy-start(s32[1,384,128]{2,1,0:T(8,128)} %counts.1) | copy-start | bytes 589828
  22.3 2.7 %collective-permute-start = (bf16[32,1280]{1,0:T(8,128)(2,1)S(1)}, bf16[32,1280]{1,0:T(8,128)(2,1)S(1)}, u32[]{:S(2)}, u32[]{:S(2)}) collective-permute-start(bf16[32,1280]{1,0:T(8,128)(2,1)S(1)} %get-tuple-element.15), channel_id=1, source_target_pairs={{0,1},{1,0},{2,3},{3,2},{4,5},{5,4},{6,7},{7,6},{8,9},{9,8},{10,11... | collective-permute-start | bytes 245768 | tf_op jit(solution)/shard_map/ppermute | solution.py:363
  22.9 4.6 %collective-permute-start.1 = (bf16[32,1280]{1,0:T(8,128)(2,1)S(1)}, bf16[32,1280]{1,0:T(8,128)(2,1)S(1)}, u32[]{:S(2)}, u32[]{:S(2)}) collective-permute-start(bf16[32,1280]{1,0:T(8,128)(2,1)S(1)} %get-tuple-element.16), channel_id=1, source_target_pairs={{0,2},{1,3},{2,0},{3,1},{4,6},{5,7},{6,4},{7,5},{8,10},{9,11},{10,... | collective-permute-start | bytes 245768 | tf_op jit(solution)/shard_map/ppermute | solution.py:363
  24.6 4.7 %copy-start.1 = (bf16[1024,128]{1,0:T(8,128)(2,1)S(1)}, bf16[1024,128]{1,0:T(8,128)(2,1)}, u32[]{:S(2)}) copy-start(bf16[1024,128]{1,0:T(8,128)(2,1)} %refs_4_.3) | copy-start | bytes 786436
  24.6 4.7 %collective-permute-start.2 = (bf16[32,1280]{1,0:T(8,128)(2,1)S(1)}, bf16[32,1280]{1,0:T(8,128)(2,1)S(1)}, u32[]{:S(2)}, u32[]{:S(2)}) collective-permute-start(bf16[32,1280]{1,0:T(8,128)(2,1)S(1)} %get-tuple-element.17), channel_id=1, source_target_pairs={{0,3},{1,2},{2,1},{3,0},{4,7},{5,6},{6,5},{7,4},{8,11},{9,10},{10,... | collective-permute-start | bytes 245768 | tf_op jit(solution)/shard_map/ppermute | solution.py:363
  34.7 8.7 %collective-permute-start.6 = (bf16[4,272,128]{2,1,0:T(8,128)(2,1)S(1)}, bf16[4,272,128]{2,1,0:T(8,128)(2,1)S(1)}, u32[]{:S(2)}, u32[]{:S(2)}) collective-permute-start(bf16[4,272,128]{2,1,0:T(8,128)(2,1)S(1)} %systems.3), channel_id=1, source_target_pairs={{0,4},{1,5},{2,6},{3,7},{4,0},{5,1},{6,2},{7,3},{8,12},{9,13},{10,... | collective-permute-start | bytes 835592 | tf_op jit(solution)/shard_map/ppermute | solution.py:363
  43.5 5.0 %collective-permute-start.7 = (bf16[272,128]{1,0:T(8,128)(2,1)S(1)}, bf16[272,128]{1,0:T(8,128)(2,1)S(1)}, u32[]{:S(2)}, u32[]{:S(2)}) collective-permute-start(bf16[272,128]{1,0:T(8,128)(2,1)S(1)} %get-tuple-element.19), channel_id=1, source_target_pairs={{0,8},{1,9},{2,10},{3,11},{4,12},{5,13},{6,14},{7,15},{8,0},{9,1},... | collective-permute-start | bytes 208904 | tf_op jit(solution)/shard_map/ppermute | solution.py:363
  45.1 8.7 %copy-start.4 = (f32[4,128]{1,0:T(4,128)S(1)}, f32[4,128]{1,0:T(4,128)}, u32[]{:S(2)}) copy-start(f32[4,128]{1,0:T(4,128)} %refs_3_.1) | copy-start | bytes 6148
  45.1 6.9 %collective-permute-start.8 = (bf16[272,128]{1,0:T(8,128)(2,1)S(1)}, bf16[272,128]{1,0:T(8,128)(2,1)S(1)}, u32[]{:S(2)}, u32[]{:S(2)}) collective-permute-start(bf16[272,128]{1,0:T(8,128)(2,1)S(1)} %get-tuple-element.20), channel_id=1, source_target_pairs={{0,16},{1,17},{2,18},{3,19},{4,20},{5,21},{6,22},{7,23},{8,24},{9,... | collective-permute-start | bytes 208904 | tf_op jit(solution)/shard_map/ppermute | solution.py:363
  47.7 6.1 %collective-permute-start.9 = (bf16[272,128]{1,0:T(8,128)(2,1)S(1)}, bf16[272,128]{1,0:T(8,128)(2,1)S(1)}, u32[]{:S(2)}, u32[]{:S(2)}) collective-permute-start(bf16[272,128]{1,0:T(8,128)(2,1)S(1)} %get-tuple-element.21), channel_id=1, source_target_pairs={{0,24},{1,25},{2,26},{3,27},{4,28},{5,29},{6,30},{7,31},{8,16},{9,... | collective-permute-start | bytes 208904 | tf_op jit(solution)/shard_map/ppermute | solution.py:363

commit v2 on v1

--- a/solution.py
+++ b/solution.py
@@ -22,6 +22,10 @@
     k = n.bit_length() - 1
     assert 1 << k == n
     return k
+
+
+def cost(us):
+    return pl.CostEstimate(flops=int(us * 1e9), bytes_accessed=int(us * 3e6), transcendentals=0)
 
 
 def params(mib):
@@ -52,15 +56,22 @@
     return (bits | (w << at)) * n_grp + k
 
 
-def histogram_kernel(step, item_dev, n_grp, n_user, me_s, valid_s, item_s, users, counts, u, *rest):
+def histogram_kernel(step, item_dev, n_grp, n_user, me_s, *refs):
+    sources, rest = refs[:5], refs[5:]
     eouts = rest[:n_grp]
-    c_hi, c_lo, acc = rest[n_grp:]
+    c_hi, c_lo, acc, *here, sem = rest[n_grp:]
+    copies = [pltpu.make_async_copy(a, b, sem.at[n]) for n, (a, b) in enumerate(zip(sources, here))]
+    for copy in copies:
+        copy.start()
+    valid_s, item_s, users, counts, u = here
     tiles, rows = users.shape[1:]
     num_items = c_hi.shape[0]
     block_users = u.shape[0]
     his = block_users // 128
     me = me_s[0]
     acc[...] = jnp.zeros_like(acc)
+    for copy in copies[:4]:
+        copy.wait()
     lane = lax.broadcasted_iota(i32, (8, rows), 1)
     sub = lax.broadcasted_iota(i32, (8, rows), 0)
     iota = lax.broadcasted_iota(i32, (128, rows), 0).astype(f32).astype(bf16)
@@ -95,6 +106,7 @@
         return 0
 
     lax.fori_loop(0, tiles // step, body, 0)
+    copies[4].wait()
     per = num_items // n_grp
     for h in range(his):
         e = (acc[pl.ds(h, num_items, stride=16), :] + 1.0).astype(bf16)
@@ -115,15 +127,24 @@
 
 def histogram(me, valid, item, users, counts, u, num_items, item_dev, n_grp, n_user):
     block_users, rank = u.shape
-    step = 16
+    step = 64
     return pl.pallas_call(
         functools.partial(histogram_kernel, step, item_dev, n_grp, n_user),
-        in_specs=[SMEM, SMEM, SMEM, VMEM, VMEM, VMEM],
+        in_specs=[SMEM] + [pl.BlockSpec(memory_space=pl.ANY)] * 5,
         out_specs=[VMEM] * (n_grp + 2),
         out_shape=[struct((num_items // n_grp, block_users + 2 * rank), bf16)] * n_grp
         + [struct((num_items, block_users), bf16)] * 2,
-        scratch_shapes=[pltpu.VMEM((num_items * 16, 128), f32)],
+        scratch_shapes=[
+            pltpu.VMEM((num_items * 16, 128), f32),
+            pltpu.SMEM(valid.shape, i32),
+            pltpu.SMEM(item.shape, i32),
+            pltpu.VMEM(users.shape, i32),
+            pltpu.VMEM(counts.shape, i32),
+            pltpu.VMEM(u.shape, bf16),
+            pltpu.SemaphoreType.DMA((5,)),
+        ],
         compiler_params=params(32),
+        cost_estimate=cost(7),
         name="histogram",
     )(me, valid, item, users, counts, u)
 
@@ -145,6 +166,7 @@
         out_specs=VMEM,
         out_shape=struct((rank, block_users * len(us)), bf16),
         compiler_params=params(16),
+        cost_estimate=cost(0.2),
         name="transpose",
     )(*us)
 
@@ -153,20 +175,67 @@
     return 64 * item_dev + -(-4 * item_dev // 16) * 16
 
 
-def systems_kernel(first, n_items, item_dev, keep, n_grp, *refs):
-    es, us, ut, out, ef = refs[:n_grp], refs[n_grp : 2 * n_grp], refs[2 * n_grp], refs[2 * n_grp + 1], refs[-1]
+def partial_systems(ef, ut, us, c, item_dev, at):
+    total = None
+    for b, u in enumerate(us):
+        block_users, rank = u.shape
+        cols = slice(b * block_users, (b + 1) * block_users)
+        w = []
+        for j in range(item_dev):
+            e = jnp.broadcast_to(ef[c, j : j + 1, cols], (16, block_users)).astype(bf16)
+            w.append(jnp.concatenate([e] * (rank // 16), 0) * ut[:, at + cols.start : at + cols.stop])
+        g = jnp.dot(jnp.concatenate(w, 0), u[...], preferred_element_type=f32)
+        total = g if total is None else total + g
+    return total
+
+
+def spread_rows(ef, es, first, n_items, item_dev, block_users):
+    for b, e in enumerate(es):
+        value = e[first : first + n_items, :block_users].astype(f32)
+        for c in range(n_items // item_dev):
+            ef[c, :, b * block_users : (b + 1) * block_users] = value[c * item_dev : (c + 1) * item_dev]
+
+
+def begun_kernel(first, n_items, item_dev, n, *refs):
+    es, us, ut, out, ef = refs[:n], refs[n : 2 * n], refs[2 * n], refs[2 * n + 1], refs[2 * n + 2]
+    spread_rows(ef, es, first, n_items, item_dev, us[0].shape[0])
+
+    def body(c, _):
+        out[c] = partial_systems(ef, ut, us, c, item_dev, 0)
+        return 0
+
+    lax.fori_loop(0, n_items // item_dev, body, 0)
+
+
+def begun(es, us, ut, first, n_items, item_dev):
+    n = len(es)
+    block_users, rank = us[0].shape
+    return pl.pallas_call(
+        functools.partial(begun_kernel, first, n_items, item_dev, n),
+        in_specs=[VMEM] * (2 * n + 1),
+        out_specs=VMEM,
+        out_shape=struct((n_items // item_dev, item_dev * rank, rank), f32),
+        scratch_shapes=[pltpu.VMEM((n_items // item_dev, item_dev, n * block_users), f32)],
+        compiler_params=params(32),
+        cost_estimate=cost(2.6),
+        name="begun",
+    )(*es, *us, ut)
+
+
+def systems_kernel(first, n_items, item_dev, keep, n, done, *refs):
+    es, us, ut = refs[:n], refs[n : 2 * n - done], refs[2 * n - done]
+    start = refs[2 * n - done + 1] if done else None
+    out, ef = refs[-2:]
     block_users, rank = us[0].shape
     span = slice(first, first + n_items)
-    for b in range(n_grp):
-        e = es[b][span, :block_users].astype(f32)
-        for c in range(n_items // item_dev):
-            ef[c, :, b * block_users : (b + 1) * block_users] = e[c * item_dev : (c + 1) * item_dev]
+    wide = (n - done) * block_users
+    spread_rows(ef, es[done:], first, n_items, item_dev, block_users)
     rhs = jnp.zeros((n_items, rank), f32)
-    for b in range(n_grp):
-        rhs = rhs + es[b][span, block_users : block_users + rank].astype(f32)
-        rhs = rhs + es[b][span, block_users + rank :].astype(f32)
+    for e in es:
+        rhs = rhs + e[span, block_users : block_users + rank].astype(f32)
+        rhs = rhs + e[span, block_users + rank :].astype(f32)
     for c in range(n_items // item_dev):
-        ef[c, :, n_grp * block_users :] = rhs[c * item_dev : (c + 1) * item_dev]
+        ef[c, :, wide:] = rhs[c * item_dev : (c + 1) * item_dev]
     row = lax.broadcasted_iota(i32, (64, rank), 0)
     lane = lax.broadcasted_iota(i32, (64, rank), 1)
     eye = lax.broadcasted_iota(i32, (rank, rank), 0) == lax.broadcasted_iota(i32, (rank, rank), 1)
@@ -174,16 +243,9 @@
     base = 64 * item_dev
 
     def body(c, _):
-        total = None
-        for b in range(n_grp):
-            cols = slice(b * block_users, (b + 1) * block_users)
-            w = []
-            for j in range(item_dev):
-                e = ef[c, j : j + 1, cols]
-                e = jnp.broadcast_to(e, (16, block_users)).astype(bf16)
-                w.append(jnp.concatenate([e] * (rank // 16), 0) * ut[:, cols])
-            g = jnp.dot(jnp.concatenate(w, 0), us[b][...], preferred_element_type=f32)
-            total = g if total is None else total + g
+        total = partial_systems(ef, ut, us, c, item_dev, done * block_users)
+        if done:
+            total = total + start[c]
         diag = []
         for j in range(item_dev):
             g = total[j * rank : (j + 1) * rank]
@@ -191,7 +253,7 @@
             out[c, 64 * j : 64 * j + 64, :] = packed.astype(out.dtype)
             diag.append(jnp.sum(jnp.where(eye, g, 0.0), axis=0, keepdims=True))
         diag = jnp.concatenate(diag, 0)
-        side = ef[c, :, n_grp * block_users :]
+        side = ef[c, :, wide:]
         put_extras(lambda a, n, v: out.__setitem__((c, slice(base + a, base + a + n)), v), diag, side, keep, item_dev)
         return 0
 
@@ -214,18 +276,20 @@
     put(0, value.shape[0], value if keep else value.astype(bf16))
 
 
-def systems(es, us, ut, first, n_items, item_dev, keep):
-    n_grp = len(es)
+def systems(es, us, ut, first, n_items, item_dev, keep, start=None, done=0):
+    n = len(es)
     block_users, rank = us[0].shape
-    return pl.pallas_call(
-        functools.partial(systems_kernel, first, n_items, item_dev, keep, n_grp),
-        in_specs=[VMEM] * (2 * n_grp + 1),
+    more = [] if start is None else [start]
+    return pl.pallas_call(
+        functools.partial(systems_kernel, first, n_items, item_dev, keep, n, done),
+        in_specs=[VMEM] * (2 * n - done + 1 + len(more)),
         out_specs=VMEM,
         out_shape=struct((n_items // item_dev, chunk_rows(item_dev), rank), f32 if keep else bf16),
-        scratch_shapes=[pltpu.VMEM((n_items // item_dev, item_dev, n_grp * block_users + rank), f32)],
+        scratch_shapes=[pltpu.VMEM((n_items // item_dev, item_dev, (n - done) * block_users + rank), f32)],
         compiler_params=params(40),
+        cost_estimate=cost(1.3 * (n - done)),
         name="systems",
-    )(*es, *us, ut)
+    )(*es, *us[done:], ut, *more)
 
 
 def extras(value, item_dev):
@@ -319,6 +383,7 @@
         out_specs=[VMEM] * 2,
         out_shape=[struct(prev.shape, f32), struct(prev.shape, bf16)],
         compiler_params=params(16),
+        cost_estimate=cost(2),
         name="gradients",
     )(own, *got, prev)
 
@@ -331,9 +396,8 @@
         owner = owner_of(group, item_dev, n_grp, n_user) ^ me
         order[group * item_dev : (group + 1) * item_dev, :] = rows[pl.ds(owner * item_dev, item_dev), :]
     ret = order[...].astype(bf16)
-    dims = (((0,), (0,)), ((), ()))
-    out[...] = lax.dot_general(c_hi[...], ret, dims, preferred_element_type=f32) + lax.dot_general(
-        c_lo[...], ret, dims, preferred_element_type=f32
+    out[...] = jnp.dot(c_hi[...], ret, preferred_element_type=f32) + jnp.dot(
+        c_lo[...], ret, preferred_element_type=f32
     )
 
 
@@ -343,11 +407,31 @@
         functools.partial(user_side_kernel, item_dev, n_grp, n_user),
         in_specs=[SMEM, VMEM, VMEM, VMEM],
         out_specs=VMEM,
-        out_shape=struct((c_hi.shape[1], rank), f32),
+        out_shape=struct((c_hi.shape[0], rank), f32),
         scratch_shapes=[pltpu.VMEM((num_items, rank), f32)] * 2,
         compiler_params=params(16),
+        cost_estimate=cost(1),
         name="user_side",
     )(me, returned, c_hi, c_lo)
+
+
+def flip_kernel(*refs):
+    n = len(refs) // 2
+    for a, b in zip(refs[:n], refs[n:]):
+        for c in range(a.shape[1] // 128):
+            b[c * 128 : (c + 1) * 128, :] = a[:, c * 128 : (c + 1) * 128].T
+
+
+def flipped(*values):
+    return pl.pallas_call(
+        flip_kernel,
+        in_specs=[VMEM] * len(values),
+        out_specs=[VMEM] * len(values),
+        out_shape=[struct(v.shape[::-1], v.dtype) for v in values],
+        compiler_params=params(16),
+        cost_estimate=cost(0.6),
+        name="flip",
+    )(*values)
 
 
 def shards(user_factors, tile_user, tile_count, tile_valid, tile_item, prev_items):
@@ -368,6 +452,7 @@
     *es, c_hi, c_lo = histogram(
         me, tile_valid, tile_item, tile_user, tile_count, u0, num_items, item_dev, n_grp, n_user
     )
+    u2, es[0] = lax.optimization_barrier((u2, es[0]))
     u3 = swap(u2, 1)
     got = [es[0], swap(es[1], 1), swap(es[2], 2), swap(es[3], 3)]
     us = [u0, u1, u2, u3]
@@ -375,7 +460,8 @@
     n_items = num_items // n_grp
     left, bit = n_user, n_grp
     n_half = n_items // 2
-    sent = systems(got, us, ut, n_half, n_half, item_dev, False)
+    start = begun(got[:2], us[:2], transposed(us[:2]), n_half, n_half, item_dev)
+    sent = systems(got, us, ut, n_half, n_half, item_dev, False, start, 2)
     other = swap(sent, bit)
     own = systems(got, us, ut, 0, n_half, item_dev, True)
     left, bit = left // 2, bit * 2
@@ -385,6 +471,8 @@
         left, bit = left // 2, bit * 2
     own, *sent = merged(own, other, item_dev, 1, True)
     parts = [swap(value, bit * (n + 1)) for n, value in enumerate(sent)]
+    c_hi, c_lo, _ = lax.optimization_barrier((c_hi, c_lo, sent[0]))
+    c_hi, c_lo = flipped(c_hi, c_lo)
     solved, half = gradients(own, parts, prev_items)
     spread = jnp.broadcast_to(half[None], (devices, item_dev, rank))
     returned = lax.all_to_all(spread, AXES, 0, 0, tiled=True).reshape(num_items, rank)

time: 68.3 us -> 56.9 us (0.83)
  blocking collectives: 11 us -> 0 us
  waiting for transfers between devices: 18.6 us -> 14.2 us
  starting transfers between devices: 11.4 us -> 15.5 us
  Pallas kernels: 22.9 us -> 21.8 us
  local copies, waits for them, and re-layouts: 3.51 us -> 4.4 us
    ppermute x10, waiting for transfers between devices: 18.6 us -> 7.09 us  [swap(): return lax.ppermute(value, AXES, [(d, d ^ bit) for d in range(devices)])]
    all_to_all x1 -> x0, blocking collectives: 11 us -> none  [shards(): lax.all_to_all(spread, AXES, 0, 0, tiled=True).reshape(num_items, rank)]
    all_to_all x0 -> x1, waiting for transfers between devices: none -> 7.06 us  [shards(): lax.all_to_all(spread, AXES, 0, 0, tiled=True).reshape(num_items, rank)]
    all_to_all x0 -> x1, starting transfers between devices: none -> 4.22 us  [shards(): lax.all_to_all(spread, AXES, 0, 0, tiled=True).reshape(num_items, rank)]
    pallas_call x0 -> x2, Pallas kernels: none -> 3.01 us  [the longest x1 2.82 us: begun(): pl.pallas_call(functools.partial(begun_kernel, first, n_items, item_dev,...]
    pallas_call x2, Pallas kernels: 10.6 us -> 8.45 us  [systems(): pl.pallas_call(functools.partial(systems_kernel, first, n_items, item_dev...]
    pallas_call x1, Pallas kernels: 8.65 us -> 6.58 us  [histogram(): pl.pallas_call(functools.partial(histogram_kernel, step, item_dev, n_grp,...]
  transfers between devices with their start and end apart: 10 -> 11, of which waited for: 7 -> 5; matrix products, arithmetic and copies ran while one was open for 0% -> 0% of each run, Pallas kernels for 21% -> 27%
where the time goes in v2:
time: 56.9 us; the launch traced here: 56.6 us
  Pallas kernels  21.8 us (38%)
  starting transfers between devices  15.5 us (27%)
  waiting for transfers between devices  14.2 us (25%)
  local copies, waits for them, and re-layouts  4.4 us (8%)
  between operations  0.72 us (1%)
    ppermute x10, starting transfers between devices, swap(): return lax.ppermute(value, AXES, [(d, d ^ bit) for d in range(devices)])  11.3 us
    pallas_call x2, Pallas kernels, systems(): pl.pallas_call(functools.partial(systems_kernel, first, n_items, item_dev...  8.45 us
    ppermute x10, waiting for transfers between devices, swap(): return lax.ppermute(value, AXES, [(d, d ^ bit) for d in range(devices)])  7.09 us
    all_to_all x1, waiting for transfers between devices, shards(): lax.all_to_all(spread, AXES, 0, 0, tiled=True).reshape(num_items, rank)  7.06 us
    pallas_call x1, Pallas kernels, histogram(): pl.pallas_call(functools.partial(histogram_kernel, step, item_dev, n_grp,...  6.58 us
    all_to_all x1, starting transfers between devices, shards(): lax.all_to_all(spread, AXES, 0, 0, tiled=True).reshape(num_items, rank)  4.22 us
    unnamed x14, local copies, waits for them, and re-layouts  3.78 us
    pallas_call x1, Pallas kernels, begun(): pl.pallas_call(functools.partial(begun_kernel, first, n_items, item_dev,...  2.82 us
  transfers between devices with their start and end apart: 11, of which 5 were waited for; matrix products, arithmetic and copies ran while one was open for 0% of the time, Pallas kernels for 27%

profile of v2, /device:TPU:0, one launch (start us, length us, event | category | flops | bytes accessed | tf_op | source)
XLA Modules:
  0.0 56.6 jit_solution(13114853180466040596)
XLA Ops:
  0.6 0.5 collective-permute-start.4
  1.1 2.6 %collective-permute-start = (bf16[1024,128]{1,0:T(8,128)(2,1)}, bf16[1024,128]{1,0:T(8,128)(2,1)S(1)}, u32[]{:S(2)}, u32[]{:S(2)}) collective-permute-start(bf16[1024,128]{1,0:T(8,128)(2,1)} %refs_2_.3), channel_id=1, source_target_pairs={{0,2},{1,3},{2,0},{3,1},{4,6},{5,7},{6,4},{7,5},{8,10},{9,11},{10,... | collective-permute-start | bytes 786440 | tf_op jit(solution)/shard_map/ppermute | solution.py:447
  3.7 0.0 copy-start.5
  3.7 0.0 copy-start.6
  3.7 0.7 %copy-done.5 = s32[1,384]{1,0:T(1,128)S(1)} copy-done((s32[1,384]{1,0:T(1,128)S(1)}, s32[1,384]{1,0:T(1,128)}, u32[]{:S(2)}) %copy-start.5) | copy-done | bytes 1560
  4.4 0.0 copy-done.6
  4.4 0.0 copy-start
  4.4 0.9 %copy-done = bf16[1024,128]{1,0:T(8,128)(2,1)S(1)} copy-done((bf16[1024,128]{1,0:T(8,128)(2,1)S(1)}, bf16[1024,128]{1,0:T(8,128)(2,1)}, u32[]{:S(2)}) %copy-start) | copy-done | bytes 262168
  5.4 0.0 copy-start.2
  5.4 0.9 %copy-done.2 = s32[1,384,128]{2,1,0:T(8,128)S(1)} copy-done((s32[1,384,128]{2,1,0:T(8,128)S(1)}, s32[1,384,128]{2,1,0:T(8,128)}, u32[]{:S(2)}) %copy-start.2) | copy-done | bytes 196632
  6.3 0.0 copy-start.3
  6.3 0.9 %copy-done.3 = s32[1,384,128]{2,1,0:T(8,128)S(1)} copy-done((s32[1,384,128]{2,1,0:T(8,128)S(1)}, s32[1,384,128]{2,1,0:T(8,128)}, u32[]{:S(2)}) %copy-start.3) | copy-done | bytes 196632
  7.2 6.6 %histogram.1 = (bf16[32,1280]{1,0:T(8,128)(2,1)S(1)}, bf16[32,1280]{1,0:T(8,128)(2,1)S(1)}, bf16[32,1280]{1,0:T(8,128)(2,1)S(1)}, bf16[32,1280]{1,0:T(8,128)(2,1...) custom-call(s32[1]{0:T(128)} %bitcast.me_s, s32[1,384]{1,0:T(1,128)S(1)} %copy-done.5, ...), custom_call_target="tpu_custom_call" | custom-call | flops 7000000000 | bytes 21000000 | tf_op jit(solution)/shard_map/histogram/pallas_call | solution.py:131
  13.8 0.2 collective-permute-start.1
  14.1 0.3 collective-permute-start.2
  14.3 1.4 %collective-permute-start.3 = (bf16[32,1280]{1,0:T(8,128)(2,1)S(1)}, bf16[32,1280]{1,0:T(8,128)(2,1)S(1)}, u32[]{:S(2)}, u32[]{:S(2)}) collective-permute-start(bf16[32,1280]{1,0:T(8,128)(2,1)S(1)} %get-tuple-element.24), channel_id=1, source_target_pairs={{0,3},{1,2},{2,1},{3,0},{4,7},{5,6},{6,5},{7,4},{8,11},{9,10},{10,... | collective-permute-start | bytes 245768 | tf_op jit(solution)/shard_map/ppermute | solution.py:447
  15.8 0.0 collective-permute-done.refs_2_.refs_6_.refs_4_
  15.8 0.0 copy-start.1
  15.8 0.5 collective-permute-start.5
  16.2 0.0 collective-permute-done.4.refs_1_.refs_5_.refs_3_
  16.2 0.2 transpose.4.refs_4_
  16.4 0.0 collective-permute-done.1.refs_1_
  16.4 0.3 copy-done.1
  16.7 2.8 %begun.1.refs_7_ = f32[4,512,128]{2,1,0:T(8,128)S(1)} custom-call(bf16[32,1280]{1,0:T(8,128)(2,1)S(1)} %get-tuple-element.21.refs_0_, bf16[32,1280]{1,0:T(8,128)(2,1)S(1)} %collective-permute-done.1.refs_1_, bf16[1024,128]{1,0:T(8,128)(2,1)S(1)} %copy-done.1, bf16[1024,128]{1,0:T(8,128)(2,1)S(1)} %collective-permute-done.4.refs_1_.refs_5_.refs_3_, ...), custom_call_target="tpu_custom_call" | custom-call | flops 2600000000 | bytes 7800000 | tf_op jit(solution)/shard_map/begun/pallas_call | solution.py:213
  19.5 0.0 collective-permute-done.5.refs_3_.refs_7_.refs_5_
  19.6 0.3 transpose.3.refs_8_.refs_6_
  19.9 0.0 collective-permute-done.2.refs_2_
  19.9 0.0 collective-permute-done.3.refs_3_
  19.9 3.2 %systems.3 = bf16[4,272,128]{2,1,0:T(8,128)(2,1)S(1)} custom-call(bf16[32,1280]{1,0:T(8,128)(2,1)S(1)} %get-tuple-element.21.refs_0_, bf16[32,1280]{1,0:T(8,128)(2,1)S(1)} %collective-permute-done.1.refs_1_, bf16[32,1280]{1,0:T(8,128)(2,1)S(1)} %collective-permute-done.2.refs_2_, bf16[32,1280]{1,0:T(8,128)(2,1)S(1)} %collective-permute-done.3.refs_3_, ...), custom_call_target="tpu_custom_call" | custom-call | flops 2600000000 | bytes 7800000 | tf_op jit(solution)/shard_map/systems/pallas_call | solution.py:283
  23.1 1.5 %collective-permute-start.6 = (bf16[4,272,128]{2,1,0:T(8,128)(2,1)S(1)}, bf16[4,272,128]{2,1,0:T(8,128)(2,1)S(1)}, u32[]{:S(2)}, u32[]{:S(2)}) collective-permute-start(bf16[4,272,128]{2,1,0:T(8,128)(2,1)S(1)} %systems.3), channel_id=1, source_target_pairs={{0,4},{1,5},{2,6},{3,7},{4,0},{5,1},{6,2},{7,3},{8,12},{9,13},{10,... | collective-permute-start | bytes 835592 | tf_op jit(solution)/shard_map/ppermute | solution.py:447
  24.6 5.3 %systems.2.own = f32[4,272,128]{2,1,0:T(8,128)S(1)} custom-call(bf16[32,1280]{1,0:T(8,128)(2,1)S(1)} %get-tuple-element.21.refs_0_, bf16[32,1280]{1,0:T(8,128)(2,1)S(1)} %collective-permute-done.1.refs_1_, bf16[32,1280]{1,0:T(8,128)(2,1)S(1)} %collective-permute-done.2.refs_2_, bf16[32,1280]{1,0:T(8,128)(2,1)S(1)} %collective-permute-done.3.refs_3_, ...), custom_call_target="tpu_custom_call" | custom-call | flops 5200000000 | bytes 15600000 | tf_op jit(solution)/shard_map/systems/pallas_call | solution.py:283
  29.9 2.2 %collective-permute-done.6.got = bf16[4,272,128]{2,1,0:T(8,128)(2,1)S(1)} collective-permute-done((bf16[4,272,128]{2,1,0:T(8,128)(2,1)S(1)}, bf16[4,272,128]{2,1,0:T(8,128)(2,1)S(1)}, u32[]{:S(2)}, u32[]{:S(2)}) %collective-permute-start.6) | collective-permute-done | bytes 278560 | tf_op jit(solution)/shard_map/ppermute | solution.py:447
  32.2 0.1 merge.1
  32.2 2.7 %collective-permute-start.8 = (bf16[272,128]{1,0:T(8,128)(2,1)S(1)}, bf16[272,128]{1,0:T(8,128)(2,1)S(1)}, u32[]{:S(2)}, u32[]{:S(2)}) collective-permute-start(bf16[272,128]{1,0:T(8,128)(2,1)S(1)} %get-tuple-element.28), channel_id=1, source_target_pairs={{0,16},{1,17},{2,18},{3,19},{4,20},{5,21},{6,22},{7,23},{8,24},{9,... | collective-permute-start | bytes 208904 | tf_op jit(solution)/shard_map/ppermute | solution.py:447
  34.9 0.0 copy-start.4
  34.9 1.3 %collective-permute-start.9 = (bf16[272,128]{1,0:T(8,128)(2,1)S(1)}, bf16[272,128]{1,0:T(8,128)(2,1)S(1)}, u32[]{:S(2)}, u32[]{:S(2)}) collective-permute-start(bf16[272,128]{1,0:T(8,128)(2,1)S(1)} %get-tuple-element.29), channel_id=1, source_target_pairs={{0,24},{1,25},{2,26},{3,27},{4,28},{5,29},{6,30},{7,31},{8,16},{9,... | collective-permute-start | bytes 208904 | tf_op jit(solution)/shard_map/ppermute | solution.py:447
  36.2 0.2 collective-permute-start.7
  36.5 3.0 %collective-permute-done.8.refs_1_ = bf16[272,128]{1,0:T(8,128)(2,1)S(1)} collective-permute-done((bf16[272,128]{1,0:T(8,128)(2,1)S(1)}, bf16[272,128]{1,0:T(8,128)(2,1)S(1)}, u32[]{:S(2)}, u32[]{:S(2)}) %collective-permute-start.8) | collective-permute-done | bytes 69664 | tf_op jit(solution)/shard_map/ppermute | solution.py:447
  39.5 1.7 %collective-permute-done.9.refs_2_ = bf16[272,128]{1,0:T(8,128)(2,1)S(1)} collective-permute-done((bf16[272,128]{1,0:T(8,128)(2,1)S(1)}, bf16[272,128]{1,0:T(8,128)(2,1)S(1)}, u32[]{:S(2)}, u32[]{:S(2)}) %collective-permute-start.9) | collective-permute-done | bytes 69664 | tf_op jit(solution)/shard_map/ppermute | solution.py:447
  41.2 0.1 collective-permute-done.7.refs_0_
  41.3 0.0 copy-done.4
  41.3 2.1 %gradients.1 = (f32[4,128]{1,0:T(4,128)}, bf16[4,128]{1,0:T(4,128)(2,1)S(1)}) custom-call(f32[1,272,128]{2,1,0:T(8,128)S(1)} %get-tuple-element.26.own, bf16[272,128]{1,0:T(8,128)(2,1)S(1)} %collective-permute-done.7.refs_0_, bf16[272,128]{1,0:T(8,128)(2,1)S(1)} %collective-permute-done.8.refs_1_, bf16[272,128]{1,0:T(8,128)(2,1)S(1)} %collective-permute-done.9.refs_2_, ...), custom_call_target="tpu_custom_call" | custom-call | flops 2000000000 | bytes 6000000 | tf_op jit(solution)/shard_map/gradients/pallas_call | solution.py:380
  43.4 0.6 %broadcast_in_dim.2 = bf16[32,4,128]{2,1,0:T(4,128)(2,1)} broadcast(bf16[4,128]{1,0:T(4,128)(2,1)S(1)} %get-tuple-element.31), dimensions={1,2} | broadcast | bytes 33792 | tf_op jit(solution)/shard_map/broadcast_in_dim | solution.py:477
  44.0 4.2 %all-to-all-start = ((bf16[32,4,128]{2,1,0:T(4,128)(2,1)}), bf16[32,4,128]{2,1,0:T(4,128)(2,1)S(1)}, u32[]{:S(2)}, u32[]{:S(2)}) async-start(bf16[32,4,128]{2,1,0:T(4,128)(2,1)} %broadcast_in_dim.2), calls=%async_computation | async-start | bytes 65536 | tf_op jit(solution)/shard_map/all_to_all | solution.py:478
  48.2 0.2 flip.1
  48.4 7.1 %all-to-all-done = bf16[32,4,128]{2,1,0:T(4,128)(2,1)S(1)} async-done(((bf16[32,4,128]{2,1,0:T(4,128)(2,1)}), bf16[32,4,128]{2,1,0:T(4,128)(2,1)S(1)}, u32[]{:S(2)}, u32[]{:S(2)}) %all-to-all-start) | async-done | bytes 32800 | tf_op jit(solution)/shard_map/all_to_all | solution.py:478
  55.5 1.1 %user_side.1 = f32[1024,128]{1,0:T(8,128)} custom-call(s32[1]{0:T(128)} %bitcast.me_s, bf16[128,128]{1,0:T(8,128)(2,1)S(1)} %bitcast.2, bf16[1024,128]{1,0:T(8,128)(2,1)S(1)} %get-tuple-element.36.c_hi, bf16[1024,128]{1,0:T(8,128)(2,1)S(1)} %get-tuple-element.37.c_lo), custom_call_target="tpu_custom_call" | custom-call | flops 1000000000 | bytes 3000000 | tf_op jit(solution)/shard_map/user_side/pallas_call | solution.py:406
Async XLA Ops:
  0.6 15.6 %collective-permute-start.4 = (bf16[1024,128]{1,0:T(8,128)(2,1)}, bf16[1024,128]{1,0:T(8,128)(2,1)S(1)}, u32[]{:S(2)}, u32[]{:S(2)}) collective-permute-start(bf16[1024,128]{1,0:T(8,128)(2,1)} %refs_2_.3), channel_id=1, source_target_pairs={{0,1},{1,0},{2,3},{3,2},{4,5},{5,4},{6,7},{7,6},{8,9},{9,8},{10,11... | collective-permute-start | bytes 786440 | tf_op jit(solution)/shard_map/ppermute | solution.py:447
  1.1 14.6 %collective-permute-start = (bf16[1024,128]{1,0:T(8,128)(2,1)}, bf16[1024,128]{1,0:T(8,128)(2,1)S(1)}, u32[]{:S(2)}, u32[]{:S(2)}) collective-permute-start(bf16[1024,128]{1,0:T(8,128)(2,1)} %refs_2_.3), channel_id=1, source_target_pairs={{0,2},{1,3},{2,0},{3,1},{4,6},{5,7},{6,4},{7,5},{8,10},{9,11},{10,... | collective-permute-start | bytes 786440 | tf_op jit(solution)/shard_map/ppermute | solution.py:447
  3.7 0.7 %copy-start.5 = (s32[1,384]{1,0:T(1,128)S(1)}, s32[1,384]{1,0:T(1,128)}, u32[]{:S(2)}) copy-start(s32[1,384]{1,0:T(1,128)} %refs_0_.3) | copy-start | bytes 4612
  3.7 0.7 %copy-start.6 = (s32[1,384]{1,0:T(1,128)S(1)}, s32[1,384]{1,0:T(1,128)}, u32[]{:S(2)}) copy-start(s32[1,384]{1,0:T(1,128)} %refs_1_.1) | copy-start | bytes 4612
  4.4 0.9 %copy-start = (bf16[1024,128]{1,0:T(8,128)(2,1)S(1)}, bf16[1024,128]{1,0:T(8,128)(2,1)}, u32[]{:S(2)}) copy-start(bf16[1024,128]{1,0:T(8,128)(2,1)} %refs_2_.3) | copy-start | bytes 786436
  5.4 0.9 %copy-start.2 = (s32[1,384,128]{2,1,0:T(8,128)S(1)}, s32[1,384,128]{2,1,0:T(8,128)}, u32[]{:S(2)}) copy-start(s32[1,384,128]{2,1,0:T(8,128)} %refs_2_.2) | copy-start | bytes 589828
  6.3 0.9 %copy-start.3 = (s32[1,384,128]{2,1,0:T(8,128)S(1)}, s32[1,384,128]{2,1,0:T(8,128)}, u32[]{:S(2)}) copy-start(s32[1,384,128]{2,1,0:T(8,128)} %refs_3_.2) | copy-start | bytes 589828
  13.8 2.6 %collective-permute-start.1 = (bf16[32,1280]{1,0:T(8,128)(2,1)S(1)}, bf16[32,1280]{1,0:T(8,128)(2,1)S(1)}, u32[]{:S(2)}, u32[]{:S(2)}) collective-permute-start(bf16[32,1280]{1,0:T(8,128)(2,1)S(1)} %get-tuple-element.22), channel_id=1, source_target_pairs={{0,1},{1,0},{2,3},{3,2},{4,5},{5,4},{6,7},{7,6},{8,9},{9,8},{10,11... | collective-permute-start | bytes 245768 | tf_op jit(solution)/shard_map/ppermute | solution.py:447
  14.1 5.8 %collective-permute-start.2 = (bf16[32,1280]{1,0:T(8,128)(2,1)S(1)}, bf16[32,1280]{1,0:T(8,128)(2,1)S(1)}, u32[]{:S(2)}, u32[]{:S(2)}) collective-permute-start(bf16[32,1280]{1,0:T(8,128)(2,1)S(1)} %get-tuple-element.23), channel_id=1, source_target_pairs={{0,2},{1,3},{2,0},{3,1},{4,6},{5,7},{6,4},{7,5},{8,10},{9,11},{10,... | collective-permute-start | bytes 245768 | tf_op jit(solution)/shard_map/ppermute | solution.py:447
  14.3 5.6 %collective-permute-start.3 = (bf16[32,1280]{1,0:T(8,128)(2,1)S(1)}, bf16[32,1280]{1,0:T(8,128)(2,1)S(1)}, u32[]{:S(2)}, u32[]{:S(2)}) collective-permute-start(bf16[32,1280]{1,0:T(8,128)(2,1)S(1)} %get-tuple-element.24), channel_id=1, source_target_pairs={{0,3},{1,2},{2,1},{3,0},{4,7},{5,6},{6,5},{7,4},{8,11},{9,10},{10,... | collective-permute-start | bytes 245768 | tf_op jit(solution)/shard_map/ppermute | solution.py:447
  15.8 1.0 %copy-start.1 = (bf16[1024,128]{1,0:T(8,128)(2,1)S(1)}, bf16[1024,128]{1,0:T(8,128)(2,1)}, u32[]{:S(2)}) copy-start(bf16[1024,128]{1,0:T(8,128)(2,1)} %refs_2_.3) | copy-start | bytes 786436
  15.8 3.8 %collective-permute-start.5 = (bf16[1024,128]{1,0:T(8,128)(2,1)S(1)}, bf16[1024,128]{1,0:T(8,128)(2,1)S(1)}, u32[]{:S(2)}, u32[]{:S(2)}) collective-permute-start(bf16[1024,128]{1,0:T(8,128)(2,1)S(1)} %collective-permute-done.refs_2_.refs_6_.refs_4_), channel_id=1, source_target_pairs={{0,1},{1,0},{2,3},{3,2},{4,5},{5,4},{6,7},{7,6},{8,9},{9,8},{10,11... | collective-permute-start | bytes 786440 | tf_op jit(solution)/shard_map/ppermute | solution.py:447
  23.1 9.1 %collective-permute-start.6 = (bf16[4,272,128]{2,1,0:T(8,128)(2,1)S(1)}, bf16[4,272,128]{2,1,0:T(8,128)(2,1)S(1)}, u32[]{:S(2)}, u32[]{:S(2)}) collective-permute-start(bf16[4,272,128]{2,1,0:T(8,128)(2,1)S(1)} %systems.3), channel_id=1, source_target_pairs={{0,4},{1,5},{2,6},{3,7},{4,0},{5,1},{6,2},{7,3},{8,12},{9,13},{10,... | collective-permute-start | bytes 835592 | tf_op jit(solution)/shard_map/ppermute | solution.py:447
  32.2 7.3 %collective-permute-start.8 = (bf16[272,128]{1,0:T(8,128)(2,1)S(1)}, bf16[272,128]{1,0:T(8,128)(2,1)S(1)}, u32[]{:S(2)}, u32[]{:S(2)}) collective-permute-start(bf16[272,128]{1,0:T(8,128)(2,1)S(1)} %get-tuple-element.28), channel_id=1, source_target_pairs={{0,16},{1,17},{2,18},{3,19},{4,20},{5,21},{6,22},{7,23},{8,24},{9,... | collective-permute-start | bytes 208904 | tf_op jit(solution)/shard_map/ppermute | solution.py:447
  34.9 6.4 %copy-start.4 = (f32[4,128]{1,0:T(4,128)S(1)}, f32[4,128]{1,0:T(4,128)}, u32[]{:S(2)}) copy-start(f32[4,128]{1,0:T(4,128)} %refs_3_.3) | copy-start | bytes 6148
  34.9 6.3 %collective-permute-start.9 = (bf16[272,128]{1,0:T(8,128)(2,1)S(1)}, bf16[272,128]{1,0:T(8,128)(2,1)S(1)}, u32[]{:S(2)}, u32[]{:S(2)}) collective-permute-start(bf16[272,128]{1,0:T(8,128)(2,1)S(1)} %get-tuple-element.29), channel_id=1, source_target_pairs={{0,24},{1,25},{2,26},{3,27},{4,28},{5,29},{6,30},{7,31},{8,16},{9,... | collective-permute-start | bytes 208904 | tf_op jit(solution)/shard_map/ppermute | solution.py:447
  36.2 5.1 %collective-permute-start.7 = (bf16[272,128]{1,0:T(8,128)(2,1)S(1)}, bf16[272,128]{1,0:T(8,128)(2,1)S(1)}, u32[]{:S(2)}, u32[]{:S(2)}) collective-permute-start(bf16[272,128]{1,0:T(8,128)(2,1)S(1)} %get-tuple-element.27), channel_id=1, source_target_pairs={{0,8},{1,9},{2,10},{3,11},{4,12},{5,13},{6,14},{7,15},{8,0},{9,1},... | collective-permute-start | bytes 208904 | tf_op jit(solution)/shard_map/ppermute | solution.py:447
  44.0 11.5 %all-to-all-start = ((bf16[32,4,128]{2,1,0:T(4,128)(2,1)}), bf16[32,4,128]{2,1,0:T(4,128)(2,1)S(1)}, u32[]{:S(2)}, u32[]{:S(2)}) async-start(bf16[32,4,128]{2,1,0:T(4,128)(2,1)} %broadcast_in_dim.2), calls=%async_computation | async-start | bytes 65536 | tf_op jit(solution)/shard_map/all_to_all | solution.py:478

commit v3 on v2

--- a/solution.py
+++ b/solution.py
@@ -56,7 +56,7 @@
     return (bits | (w << at)) * n_grp + k
 
 
-def histogram_kernel(step, item_dev, n_grp, n_user, me_s, *refs):
+def histogram_kernel(step, low_part, item_dev, n_grp, n_user, me_s, *refs):
     sources, rest = refs[:5], refs[5:]
     eouts = rest[:n_grp]
     c_hi, c_lo, acc, *here, sem = rest[n_grp:]
@@ -67,30 +67,31 @@
     tiles, rows = users.shape[1:]
     num_items = c_hi.shape[0]
     block_users = u.shape[0]
-    his = block_users // 128
+    his = block_users // low_part
+    kinds = 2 * his
     me = me_s[0]
     acc[...] = jnp.zeros_like(acc)
     for copy in copies[:4]:
         copy.wait()
-    lane = lax.broadcasted_iota(i32, (8, rows), 1)
-    sub = lax.broadcasted_iota(i32, (8, rows), 0)
-    iota = lax.broadcasted_iota(i32, (128, rows), 0).astype(f32).astype(bf16)
-    zero = jnp.zeros((16, rows), bf16)
-    one, nil = jnp.ones((128, rows), bf16), jnp.zeros((128, rows), bf16)
+    lane = lax.broadcasted_iota(i32, (his, rows), 1)
+    sub = lax.broadcasted_iota(i32, (his, rows), 0)
+    iota = lax.broadcasted_iota(i32, (low_part, rows), 0).astype(f32).astype(bf16)
+    zero = jnp.zeros((kinds, rows), bf16)
+    one, nil = jnp.ones((low_part, rows), bf16), jnp.zeros((low_part, rows), bf16)
 
     def body(b, _):
         base = pl.multiple_of(b * step, step)
         blk = users[0, pl.ds(base, step), :]
         cnt = counts[0, pl.ds(base, step), :].astype(f32) * confidence_rate
-        lo = (blk & 127).astype(f32)
-        hi = blk >> 7
+        lo = (blk & (low_part - 1)).astype(f32)
+        hi = blk >> log2(low_part)
         for t in range(0, step, 2):
             oh, lhs = [], []
             for j in (t, t + 1):
                 lob = jnp.broadcast_to(lo[j : j + 1], (16, rows)).astype(bf16)
-                oh.append(jnp.where(jnp.concatenate([lob] * 8, 0) == iota, one, nil))
-                on = (lane < valid_s[0, base + j]) & (jnp.broadcast_to(hi[j : j + 1], (8, rows)) == sub)
-                ex = jnp.broadcast_to(cnt[j : j + 1], (8, rows))
+                oh.append(jnp.where(jnp.concatenate([lob] * (low_part // 16), 0) == iota, one, nil))
+                on = (lane < valid_s[0, base + j]) & (jnp.broadcast_to(hi[j : j + 1], (his, rows)) == sub)
+                ex = jnp.broadcast_to(cnt[j : j + 1], (his, rows))
                 lhs.append(
                     jnp.concatenate([jnp.where(on, ex, 0.0), jnp.where(on, 1.0 + ex, 0.0)], 0).astype(bf16)
                 )
@@ -102,17 +103,23 @@
             )
             for q, j in enumerate((t, t + 1)):
                 p = slot_of(item_s[0, base + j], me, item_dev, n_grp, n_user)
-                acc[pl.ds(pl.multiple_of(p * 16, 16), 16), :] += out[16 * q : 16 * q + 16]
+                acc[pl.ds(pl.multiple_of(p * kinds, kinds), kinds), :] += out[kinds * q : kinds * (q + 1)]
         return 0
 
     lax.fori_loop(0, tiles // step, body, 0)
     copies[4].wait()
     per = num_items // n_grp
-    for h in range(his):
-        e = (acc[pl.ds(h, num_items, stride=16), :] + 1.0).astype(bf16)
+    wide = 128 // low_part
+
+    def row(h):
+        parts = [acc[pl.ds(h * wide + n, num_items, stride=kinds), :] for n in range(wide)]
+        return jnp.concatenate(parts, 1)
+
+    for h in range(block_users // 128):
+        e = (row(h) + 1.0).astype(bf16)
         for k in range(n_grp):
             eouts[k][:, h * 128 : (h + 1) * 128] = e[k * per : (k + 1) * per]
-        c = acc[pl.ds(8 + h, num_items, stride=16), :]
+        c = row(his // wide + h)
         ch = c.astype(bf16)
         c_hi[:, h * 128 : (h + 1) * 128] = ch
         c_lo[:, h * 128 : (h + 1) * 128] = (c - ch.astype(f32)).astype(bf16)
@@ -127,15 +134,15 @@
 
 def histogram(me, valid, item, users, counts, u, num_items, item_dev, n_grp, n_user):
     block_users, rank = u.shape
-    step = 64
-    return pl.pallas_call(
-        functools.partial(histogram_kernel, step, item_dev, n_grp, n_user),
-        in_specs=[SMEM] + [pl.BlockSpec(memory_space=pl.ANY)] * 5,
+    step, low_part = 128, 64
+    return pl.pallas_call(
+        functools.partial(histogram_kernel, step, low_part, item_dev, n_grp, n_user),
+        in_specs=[SMEM] + [pl.BlockSpec(memory_space=pltpu.HBM)] * 5,
         out_specs=[VMEM] * (n_grp + 2),
         out_shape=[struct((num_items // n_grp, block_users + 2 * rank), bf16)] * n_grp
         + [struct((num_items, block_users), bf16)] * 2,
         scratch_shapes=[
-            pltpu.VMEM((num_items * 16, 128), f32),
+            pltpu.VMEM((num_items * 2 * block_users // low_part, low_part), f32),
             pltpu.SMEM(valid.shape, i32),
             pltpu.SMEM(item.shape, i32),
             pltpu.VMEM(users.shape, i32),
@@ -146,7 +153,7 @@
         compiler_params=params(32),
         cost_estimate=cost(7),
         name="histogram",
-    )(me, valid, item, users, counts, u)
+    )(me, *[pltpu.with_memory_space_constraint(v, pltpu.HBM) for v in (valid, item, users, counts, u)])
 
 
 def transpose_kernel(*refs):
@@ -189,9 +196,14 @@
     return total
 
 
+def some_rows(ref, first, n, cols):
+    low, high = first // 16 * 16, -(-(first + n) // 16) * 16
+    return ref[low:high, cols].astype(f32)[first - low : first - low + n]
+
+
 def spread_rows(ef, es, first, n_items, item_dev, block_users):
     for b, e in enumerate(es):
-        value = e[first : first + n_items, :block_users].astype(f32)
+        value = some_rows(e, first, n_items, slice(0, block_users))
         for c in range(n_items // item_dev):
             ef[c, :, b * block_users : (b + 1) * block_users] = value[c * item_dev : (c + 1) * item_dev]
 
@@ -222,18 +234,17 @@
     )(*es, *us, ut)
 
 
-def systems_kernel(first, n_items, item_dev, keep, n, done, *refs):
+def systems_kernel(first, n_items, item_dev, keep, n, done, at, *refs):
     es, us, ut = refs[:n], refs[n : 2 * n - done], refs[2 * n - done]
     start = refs[2 * n - done + 1] if done else None
     out, ef = refs[-2:]
     block_users, rank = us[0].shape
-    span = slice(first, first + n_items)
     wide = (n - done) * block_users
     spread_rows(ef, es[done:], first, n_items, item_dev, block_users)
     rhs = jnp.zeros((n_items, rank), f32)
     for e in es:
-        rhs = rhs + e[span, block_users : block_users + rank].astype(f32)
-        rhs = rhs + e[span, block_users + rank :].astype(f32)
+        rhs = rhs + some_rows(e, first, n_items, slice(block_users, block_users + rank))
+        rhs = rhs + some_rows(e, first, n_items, slice(block_users + rank, block_users + 2 * rank))
     for c in range(n_items // item_dev):
         ef[c, :, wide:] = rhs[c * item_dev : (c + 1) * item_dev]
     row = lax.broadcasted_iota(i32, (64, rank), 0)
@@ -245,7 +256,7 @@
     def body(c, _):
         total = partial_systems(ef, ut, us, c, item_dev, done * block_users)
         if done:
-            total = total + start[c]
+            total = total + start[at + c]
         diag = []
         for j in range(item_dev):
             g = total[j * rank : (j + 1) * rank]
@@ -276,18 +287,18 @@
     put(0, value.shape[0], value if keep else value.astype(bf16))
 
 
-def systems(es, us, ut, first, n_items, item_dev, keep, start=None, done=0):
+def systems(es, us, ut, first, n_items, item_dev, keep, start=None, done=0, at=0, us_cost=None):
     n = len(es)
     block_users, rank = us[0].shape
     more = [] if start is None else [start]
     return pl.pallas_call(
-        functools.partial(systems_kernel, first, n_items, item_dev, keep, n, done),
+        functools.partial(systems_kernel, first, n_items, item_dev, keep, n, done, at),
         in_specs=[VMEM] * (2 * n - done + 1 + len(more)),
         out_specs=VMEM,
         out_shape=struct((n_items // item_dev, chunk_rows(item_dev), rank), f32 if keep else bf16),
         scratch_shapes=[pltpu.VMEM((n_items // item_dev, item_dev, (n - done) * block_users + rank), f32)],
         compiler_params=params(40),
-        cost_estimate=cost(1.3 * (n - done)),
+        cost_estimate=cost(0.082 * (n - done) * n_items if us_cost is None else us_cost),
         name="systems",
     )(*es, *us[done:], ut, *more)
 
@@ -298,7 +309,8 @@
     return part[0] + part[1], part[2] + part[3]
 
 
-def merge_kernel(item_dev, n_keep, own, got, kept, *sent):
+def merge_kernel(item_dev, n_keep, apart, own, got, *outs):
+    kept, sent = outs[0], outs[bool(n_keep) :]
     base = 64 * item_dev
     for c in range(own.shape[0]):
         value = own[c] + got[c].astype(f32)
@@ -307,8 +319,8 @@
             kept[c, :base, :] = value[:base]
             put_extras(lambda a, n, v, c=c: kept.__setitem__((c, slice(base + a, base + a + n)), v), diag, side, True, item_dev)
         else:
-            ref = sent[0] if len(sent) == 1 else sent[c - n_keep]
-            lead = (c - n_keep,) if len(sent) == 1 else ()
+            ref = sent[c - n_keep] if apart else sent[0]
+            lead = () if apart else (c - n_keep,)
             ref[lead + (slice(0, base),)] = value[:base].astype(bf16)
             put_extras(
                 lambda a, n, v, ref=ref, lead=lead: ref.__setitem__(lead + (slice(base + a, base + a + n),), v),
@@ -320,11 +332,12 @@
     chunks, rows, rank = own.shape
     n_sent = chunks - n_keep
     shapes = [struct((rows, rank), bf16)] * n_sent if apart else [struct((n_sent, rows, rank), bf16)]
-    return pl.pallas_call(
-        functools.partial(merge_kernel, item_dev, n_keep),
+    shapes = ([struct((n_keep, rows, rank), f32)] if n_keep else []) + shapes
+    return pl.pallas_call(
+        functools.partial(merge_kernel, item_dev, n_keep, apart),
         in_specs=[VMEM] * 2,
-        out_specs=[VMEM] * (1 + len(shapes)),
-        out_shape=[struct((n_keep, rows, rank), f32)] + shapes,
+        out_specs=[VMEM] * len(shapes),
+        out_shape=shapes,
         compiler_params=params(16),
         name="merge",
     )(own, got)
@@ -372,16 +385,18 @@
         direction = residual + norm_next / norm_now * direction
         norm_now = norm_next
     out[...] = solution
-    half[...] = solution.astype(bf16)
-
-
-def gradients(own, got, prev):
+    short = solution.astype(bf16)
+    for d in range(half.shape[0]):
+        half[d] = short
+
+
+def gradients(own, got, prev, devices):
     item_dev, rank = prev.shape
     return pl.pallas_call(
         functools.partial(gradients_kernel, item_dev),
         in_specs=[VMEM] * (2 + len(got)),
         out_specs=[VMEM] * 2,
-        out_shape=[struct(prev.shape, f32), struct(prev.shape, bf16)],
+        out_shape=[struct(prev.shape, f32), struct((devices,) + prev.shape, bf16)],
         compiler_params=params(16),
         cost_estimate=cost(2),
         name="gradients",
@@ -429,7 +444,7 @@
         out_specs=[VMEM] * len(values),
         out_shape=[struct(v.shape[::-1], v.dtype) for v in values],
         compiler_params=params(16),
-        cost_estimate=cost(0.6),
+        cost_estimate=cost(8),
         name="flip",
     )(*values)
 
@@ -458,23 +473,40 @@
     us = [u0, u1, u2, u3]
     ut = transposed(us)
     n_items = num_items // n_grp
-    left, bit = n_user, n_grp
     n_half = n_items // 2
     start = begun(got[:2], us[:2], transposed(us[:2]), n_half, n_half, item_dev)
-    sent = systems(got, us, ut, n_half, n_half, item_dev, False, start, 2)
-    other = swap(sent, bit)
-    own = systems(got, us, ut, 0, n_half, item_dev, True)
-    left, bit = left // 2, bit * 2
-    while left > 4:
-        own, sent = merged(own, other, item_dev, left // 2, False)
+    if n_user == 8:
+        n_far = n_half // 2
+        chunks = n_far // item_dev
+        sent = systems(got, us, ut, n_half + n_far, n_far, item_dev, False, start, 2, chunks)
+        far_other = swap(sent, n_grp)
+        ut, _ = lax.optimization_barrier((ut, sent))
+        sent = systems(got, us, ut, n_half, n_far, item_dev, False, start, 2, 0)
+        near_other = swap(sent, n_grp)
+        ut, _ = lax.optimization_barrier((ut, sent))
+        own = systems(got, us, ut, n_far, n_far, item_dev, True, us_cost=0.01)
+        far = merged(own, far_other, item_dev, 0, True)
+        parts = [swap(value, n_grp * 2 * (chunks + n)) for n, value in reversed(list(enumerate(far)))]
+        ut, _ = lax.optimization_barrier((ut, far[0]))
+        own = systems(got, us, ut, 0, n_far, item_dev, True)
+        own, *near = merged(own, near_other, item_dev, 1, True)
+        parts += [swap(value, n_grp * 2 * (n + 1)) for n, value in enumerate(near)]
+    else:
+        left, bit = n_user, n_grp
+        sent = systems(got, us, ut, n_half, n_half, item_dev, False, start, 2)
         other = swap(sent, bit)
+        own = systems(got, us, ut, 0, n_half, item_dev, True)
         left, bit = left // 2, bit * 2
-    own, *sent = merged(own, other, item_dev, 1, True)
-    parts = [swap(value, bit * (n + 1)) for n, value in enumerate(sent)]
-    c_hi, c_lo, _ = lax.optimization_barrier((c_hi, c_lo, sent[0]))
+        while left > 4:
+            own, sent = merged(own, other, item_dev, left // 2, False)
+            other = swap(sent, bit)
+            left, bit = left // 2, bit * 2
+        own, *sent = merged(own, other, item_dev, 1, True)
+        parts = [swap(value, bit * (n + 1)) for n, value in enumerate(sent)]
+    c_hi, c_lo, own, *parts[:2] = lax.optimization_barrier((c_hi, c_lo, own, *parts[:2]))
     c_hi, c_lo = flipped(c_hi, c_lo)
-    solved, half = gradients(own, parts, prev_items)
-    spread = jnp.broadcast_to(half[None], (devices, item_dev, rank))
+    own, c_hi = lax.optimization_barrier((own, c_hi))
+    solved, spread = gradients(own, parts, prev_items, devices)
     returned = lax.all_to_all(spread, AXES, 0, 0, tiled=True).reshape(num_items, rank)
     return solved, user_side(me, returned, c_hi, c_lo, item_dev, n_grp, n_user)
 

time: 56.9 us -> 49.5 us (0.87)
  blocking collectives: 0 us -> 11.3 us
  waiting for transfers between devices: 14.2 us -> 4.26 us
  local copies, waits for them, and re-layouts: 4.4 us -> 0.01 us
  starting transfers between devices: 15.5 us -> 12 us
  Pallas kernels: 21.8 us -> 21.1 us
    all_to_all x0 -> x1, blocking collectives: none -> 11.3 us  [shards(): lax.all_to_all(spread, AXES, 0, 0, tiled=True).reshape(num_items, rank)]
    all_to_all x1 -> x0, waiting for transfers between devices: 7.06 us -> none  [shards(): lax.all_to_all(spread, AXES, 0, 0, tiled=True).reshape(num_items, rank)]
    all_to_all x1 -> x0, starting transfers between devices: 4.22 us -> none  [shards(): lax.all_to_all(spread, AXES, 0, 0, tiled=True).reshape(num_items, rank)]
    unnamed x14 -> x4, local copies, waits for them, and re-layouts: 3.78 us -> 0.01 us
    ppermute x10 -> x11, waiting for transfers between devices: 7.09 us -> 4.26 us  [swap(): return lax.ppermute(value, AXES, [(d, d ^ bit) for d in range(devices)])]
    pallas_call x2 -> x3, Pallas kernels: 6.64 us -> 5.92 us  [the longest x1 5.85 us: histogram(): pl.pallas_call(functools.partial(histogram_kernel, step, low_part, item_d...]
    ppermute x10 -> x11, starting transfers between devices: 11.3 us -> 12 us  [swap(): return lax.ppermute(value, AXES, [(d, d ^ bit) for d in range(devices)])]
    broadcast_in_dim x1 -> x0, local copies, waits for them, and re-layouts: 0.62 us -> none  [shards(): spread = jnp.broadcast_to(half[None], (devices, item_dev, rank))]
  transfers between devices with their start and end apart: 11 -> 11, of which waited for: 5 -> 3; matrix products, arithmetic and copies ran while one was open for 0% -> 0% of each run, Pallas kernels for 27% -> 33%
where the time goes in v3:
time: 49.5 us; the launch traced here: 49.4 us
  Pallas kernels  21.1 us (43%)
  starting transfers between devices  12 us (24%)
  blocking collectives  11.3 us (23%)
  waiting for transfers between devices  4.26 us (9%)
  between operations  0.74 us (1%)
    ppermute x11, starting transfers between devices, swap(): return lax.ppermute(value, AXES, [(d, d ^ bit) for d in range(devices)])  12 us
    all_to_all x1, blocking collectives, shards(): lax.all_to_all(spread, AXES, 0, 0, tiled=True).reshape(num_items, rank)  11.3 us
    pallas_call x4, Pallas kernels, systems(): pl.pallas_call(functools.partial(systems_kernel, first, n_items, item_dev...  8.51 us
    pallas_call x1, Pallas kernels, histogram(): pl.pallas_call(functools.partial(histogram_kernel, step, low_part, item_d...  5.85 us
    ppermute x11, waiting for transfers between devices, swap(): return lax.ppermute(value, AXES, [(d, d ^ bit) for d in range(devices)])  4.26 us
    pallas_call x1, Pallas kernels, begun(): pl.pallas_call(functools.partial(begun_kernel, first, n_items, item_dev,...  2.82 us
    pallas_call x1, Pallas kernels, gradients(): pl.pallas_call(functools.partial(gradients_kernel, item_dev), in_specs=[V...  2.08 us
    pallas_call x1, Pallas kernels, user_side(): pl.pallas_call(functools.partial(user_side_kernel, item_dev, n_grp, n_use...  1.09 us
  transfers between devices with their start and end apart: 11, of which 3 were waited for; matrix products, arithmetic and copies ran while one was open for 0% of the time, Pallas kernels for 33%

profile of v3, /device:TPU:0, one launch (start us, length us, event | category | flops | bytes accessed | tf_op | source)
XLA Modules:
  0.0 49.4 jit_solution(16433540439039624412)
XLA Ops:
  0.6 0.5 %collective-permute-start.4 = (bf16[1024,128]{1,0:T(8,128)(2,1)}, bf16[1024,128]{1,0:T(8,128)(2,1)S(1)}, u32[]{:S(2)}, u32[]{:S(2)}) collective-permute-start(bf16[1024,128]{1,0:T(8,128)(2,1)} %refs_4_.5), channel_id=1, source_target_pairs={{0,1},{1,0},{2,3},{3,2},{4,5},{5,4},{6,7},{7,6},{8,9},{9,8},{10,11... | collective-permute-start | bytes 786440 | tf_op jit(solution)/shard_map/ppermute | solution.py:462
  1.1 2.6 %collective-permute-start = (bf16[1024,128]{1,0:T(8,128)(2,1)}, bf16[1024,128]{1,0:T(8,128)(2,1)S(1)}, u32[]{:S(2)}, u32[]{:S(2)}) collective-permute-start(bf16[1024,128]{1,0:T(8,128)(2,1)} %refs_4_.5), channel_id=1, source_target_pairs={{0,2},{1,3},{2,0},{3,1},{4,6},{5,7},{6,4},{7,5},{8,10},{9,11},{10,... | collective-permute-start | bytes 786440 | tf_op jit(solution)/shard_map/ppermute | solution.py:462
  3.7 0.0 copy-start
  3.7 5.9 %histogram.1 = (bf16[32,1280]{1,0:T(8,128)(2,1)S(1)}, bf16[32,1280]{1,0:T(8,128)(2,1)S(1)}, bf16[32,1280]{1,0:T(8,128)(2,1)S(1)}, bf16[32,1280]{1,0:T(8,128)(2,1...) custom-call(s32[1]{0:T(128)} %bitcast.me_s, s32[1,384]{1,0:T(1,128)} %refs_0_.3, s32[1,384]{1,0:T(1,128)} %refs_1_.1, ...), custom_call_target="tpu_custom_call" | custom-call | flops 7000000000 | bytes 21000000 | tf_op jit(solution)/shard_map/histogram/pallas_call | solution.py:138
  9.6 0.2 collective-permute-start.1
  9.8 0.3 collective-permute-start.2
  10.1 1.4 %collective-permute-start.3 = (bf16[32,1280]{1,0:T(8,128)(2,1)S(1)}, bf16[32,1280]{1,0:T(8,128)(2,1)S(1)}, u32[]{:S(2)}, u32[]{:S(2)}) collective-permute-start(bf16[32,1280]{1,0:T(8,128)(2,1)S(1)} %get-tuple-element.34), channel_id=1, source_target_pairs={{0,3},{1,2},{2,1},{3,0},{4,7},{5,6},{6,5},{7,4},{8,11},{9,10},{10,... | collective-permute-start | bytes 245768 | tf_op jit(solution)/shard_map/ppermute | solution.py:462
  11.5 0.0 collective-permute-done.refs_2_.refs_4_.refs_6_
  11.5 0.5 collective-permute-start.5
  12.0 0.0 collective-permute-done.4.refs_1_.refs_3_.refs_5_
  12.0 0.0 copy-done
  12.0 0.2 transpose.3.refs_4_
  12.2 0.0 collective-permute-done.1.refs_1_
  12.2 2.8 %begun.1.refs_7_ = f32[4,512,128]{2,1,0:T(8,128)S(1)} custom-call(bf16[32,1280]{1,0:T(8,128)(2,1)S(1)} %get-tuple-element.31.refs_0_, bf16[32,1280]{1,0:T(8,128)(2,1)S(1)} %collective-permute-done.1.refs_1_, bf16[1024,128]{1,0:T(8,128)(2,1)S(1)} %copy-done, bf16[1024,128]{1,0:T(8,128)(2,1)S(1)} %collective-permute-done.4.refs_1_.refs_3_.refs_5_, ...), custom_call_target="tpu_custom_call" | custom-call | flops 2600000000 | bytes 7800000 | tf_op jit(solution)/shard_map/begun/pallas_call | solution.py:225
  15.0 0.0 collective-permute-done.5.refs_3_.refs_5_.refs_7_
  15.0 0.3 transpose.2.refs_6_.refs_8_
  15.4 0.0 collective-permute-done.2.refs_2_
  15.4 0.3 collective-permute-done.3.refs_3_
  15.7 1.6 %systems.4 = bf16[2,272,128]{2,1,0:T(8,128)(2,1)S(1)} custom-call(bf16[32,1280]{1,0:T(8,128)(2,1)S(1)} %get-tuple-element.31.refs_0_, bf16[32,1280]{1,0:T(8,128)(2,1)S(1)} %collective-permute-done.1.refs_1_, bf16[32,1280]{1,0:T(8,128)(2,1)S(1)} %collective-permute-done.2.refs_2_, bf16[32,1280]{1,0:T(8,128)(2,1)S(1)} %collective-permute-done.3.refs_3_, ...), custom_call_target="tpu_custom_call" | custom-call | flops 1312000000 | bytes 3936000 | tf_op jit(solution)/shard_map/systems/pallas_call | solution.py:294
  17.3 1.6 %collective-permute-start.6 = (bf16[2,272,128]{2,1,0:T(8,128)(2,1)S(1)}, bf16[2,272,128]{2,1,0:T(8,128)(2,1)S(1)}, u32[]{:S(2)}, u32[]{:S(2)}) collective-permute-start(bf16[2,272,128]{2,1,0:T(8,128)(2,1)S(1)} %systems.4), channel_id=1, source_target_pairs={{0,4},{1,5},{2,6},{3,7},{4,0},{5,1},{6,2},{7,3},{8,12},{9,13},{10,... | collective-permute-start | bytes 417800 | tf_op jit(solution)/shard_map/ppermute | solution.py:462
  18.9 1.6 %systems.5 = bf16[2,272,128]{2,1,0:T(8,128)(2,1)S(1)} custom-call(bf16[32,1280]{1,0:T(8,128)(2,1)S(1)} %get-tuple-element.31.refs_0_, bf16[32,1280]{1,0:T(8,128)(2,1)S(1)} %collective-permute-done.1.refs_1_, bf16[32,1280]{1,0:T(8,128)(2,1)S(1)} %collective-permute-done.2.refs_2_, bf16[32,1280]{1,0:T(8,128)(2,1)S(1)} %collective-permute-done.3.refs_3_, ...), custom_call_target="tpu_custom_call" | custom-call | flops 1312000000 | bytes 3936000 | tf_op jit(solution)/shard_map/systems/pallas_call | solution.py:294
  20.5 0.6 %collective-permute-start.7 = (bf16[2,272,128]{2,1,0:T(8,128)(2,1)S(1)}, bf16[2,272,128]{2,1,0:T(8,128)(2,1)S(1)}, u32[]{:S(2)}, u32[]{:S(2)}) collective-permute-start(bf16[2,272,128]{2,1,0:T(8,128)(2,1)S(1)} %systems.5), channel_id=1, source_target_pairs={{0,4},{1,5},{2,6},{3,7},{4,0},{5,1},{6,2},{7,3},{8,12},{9,13},{10,... | collective-permute-start | bytes 417800 | tf_op jit(solution)/shard_map/ppermute | solution.py:462
  21.1 2.7 %systems.6.own = f32[2,272,128]{2,1,0:T(8,128)S(1)} custom-call(bf16[32,1280]{1,0:T(8,128)(2,1)S(1)} %get-tuple-element.31.refs_0_, bf16[32,1280]{1,0:T(8,128)(2,1)S(1)} %collective-permute-done.1.refs_1_, bf16[32,1280]{1,0:T(8,128)(2,1)S(1)} %collective-permute-done.2.refs_2_, bf16[32,1280]{1,0:T(8,128)(2,1)S(1)} %collective-permute-done.3.refs_3_, ...), custom_call_target="tpu_custom_call" | custom-call | flops 10000000 | bytes 30000 | tf_op jit(solution)/shard_map/systems/pallas_call | solution.py:294
  23.7 0.0 collective-permute-done.6.got
  23.8 2.7 %collective-permute-start.9 = (bf16[272,128]{1,0:T(8,128)(2,1)S(1)}, bf16[272,128]{1,0:T(8,128)(2,1)S(1)}, u32[]{:S(2)}, u32[]{:S(2)}) collective-permute-start(bf16[272,128]{1,0:T(8,128)(2,1)S(1)} %get-tuple-element.38), channel_id=1, source_target_pairs={{0,16},{1,17},{2,18},{3,19},{4,20},{5,21},{6,22},{7,23},{8,24},{9,... | collective-permute-start | bytes 208904 | tf_op jit(solution)/shard_map/ppermute | solution.py:462
  26.4 1.4 %collective-permute-start.8 = (bf16[272,128]{1,0:T(8,128)(2,1)S(1)}, bf16[272,128]{1,0:T(8,128)(2,1)S(1)}, u32[]{:S(2)}, u32[]{:S(2)}) collective-permute-start(bf16[272,128]{1,0:T(8,128)(2,1)S(1)} %get-tuple-element.41), channel_id=1, source_target_pairs={{0,24},{1,25},{2,26},{3,27},{4,28},{5,29},{6,30},{7,31},{8,16},{9,... | collective-permute-start | bytes 208904 | tf_op jit(solution)/shard_map/ppermute | solution.py:462
  27.9 2.7 %systems.7.own = f32[2,272,128]{2,1,0:T(8,128)S(1)} custom-call(bf16[32,1280]{1,0:T(8,128)(2,1)S(1)} %get-tuple-element.31.refs_0_, bf16[32,1280]{1,0:T(8,128)(2,1)S(1)} %collective-permute-done.1.refs_1_, bf16[32,1280]{1,0:T(8,128)(2,1)S(1)} %collective-permute-done.2.refs_2_, bf16[32,1280]{1,0:T(8,128)(2,1)S(1)} %collective-permute-done.3.refs_3_, ...), custom_call_target="tpu_custom_call" | custom-call | flops 2624000000 | bytes 7872000 | tf_op jit(solution)/shard_map/systems/pallas_call | solution.py:294
  30.5 0.0 collective-permute-done.7.got
  30.6 0.2 collective-permute-start.10
  30.8 1.8 %collective-permute-done.8.refs_0_ = bf16[272,128]{1,0:T(8,128)(2,1)S(1)} collective-permute-done((bf16[272,128]{1,0:T(8,128)(2,1)S(1)}, bf16[272,128]{1,0:T(8,128)(2,1)S(1)}, u32[]{:S(2)}, u32[]{:S(2)}) %collective-permute-start.8) | collective-permute-done | bytes 69664 | tf_op jit(solution)/shard_map/ppermute | solution.py:462
  32.6 0.0 collective-permute-done.9.refs_1_
  32.6 0.0 copy-start.1
  32.7 0.2 flip.1
  32.8 2.1 %collective-permute-done.10.refs_2_ = bf16[272,128]{1,0:T(8,128)(2,1)S(1)} collective-permute-done((bf16[272,128]{1,0:T(8,128)(2,1)S(1)}, bf16[272,128]{1,0:T(8,128)(2,1)S(1)}, u32[]{:S(2)}, u32[]{:S(2)}) %collective-permute-start.10) | collective-permute-done | bytes 69664 | tf_op jit(solution)/shard_map/ppermute | solution.py:462
  34.9 0.0 copy-done.1
  34.9 2.1 %gradients.1 = (f32[4,128]{1,0:T(4,128)}, bf16[32,4,128]{2,1,0:T(4,128)(2,1)S(1)}) custom-call(f32[1,272,128]{2,1,0:T(8,128)S(1)} %get-tuple-element.46.own, bf16[272,128]{1,0:T(8,128)(2,1)S(1)} %collective-permute-done.8.refs_0_, bf16[272,128]{1,0:T(8,128)(2,1)S(1)} %collective-permute-done.9.refs_1_, bf16[272,128]{1,0:T(8,128)(2,1)S(1)} %collective-permute-done.10.refs_2_, ...), custom_call_target="tpu_custom_call" | custom-call | flops 2000000000 | bytes 6000000 | tf_op jit(solution)/shard_map/gradients/pallas_call | solution.py:395
  37.0 11.3 %all_to_all.5 = bf16[32,4,128]{2,1,0:T(4,128)(2,1)S(1)} all-to-all(bf16[32,4,128]{2,1,0:T(4,128)(2,1)S(1)} %get-tuple-element.51), channel_id=1, replica_groups=mesh['user'=8,'grp'=4] {'user','grp'}, dimensions={0} | all-to-all | bytes 65536 | tf_op jit(solution)/shard_map/all_to_all | solution.py:510
  48.3 1.1 %user_side.1 = f32[1024,128]{1,0:T(8,128)} custom-call(s32[1]{0:T(128)} %bitcast.me_s, bf16[128,128]{1,0:T(8,128)(2,1)S(1)} %bitcast.2, bf16[1024,128]{1,0:T(8,128)(2,1)S(1)} %get-tuple-element.52.c_hi, bf16[1024,128]{1,0:T(8,128)(2,1)S(1)} %get-tuple-element.53.c_lo), custom_call_target="tpu_custom_call" | custom-call | flops 1000000000 | bytes 3000000 | tf_op jit(solution)/shard_map/user_side/pallas_call | solution.py:421
  (2 shorter events, 0.1 us)
Async XLA Ops:
  0.6 11.4 %collective-permute-start.4 = (bf16[1024,128]{1,0:T(8,128)(2,1)}, bf16[1024,128]{1,0:T(8,128)(2,1)S(1)}, u32[]{:S(2)}, u32[]{:S(2)}) collective-permute-start(bf16[1024,128]{1,0:T(8,128)(2,1)} %refs_4_.5), channel_id=1, source_target_pairs={{0,1},{1,0},{2,3},{3,2},{4,5},{5,4},{6,7},{7,6},{8,9},{9,8},{10,11... | collective-permute-start | bytes 786440 | tf_op jit(solution)/shard_map/ppermute | solution.py:462
  1.1 10.4 %collective-permute-start = (bf16[1024,128]{1,0:T(8,128)(2,1)}, bf16[1024,128]{1,0:T(8,128)(2,1)S(1)}, u32[]{:S(2)}, u32[]{:S(2)}) collective-permute-start(bf16[1024,128]{1,0:T(8,128)(2,1)} %refs_4_.5), channel_id=1, source_target_pairs={{0,2},{1,3},{2,0},{3,1},{4,6},{5,7},{6,4},{7,5},{8,10},{9,11},{10,... | collective-permute-start | bytes 786440 | tf_op jit(solution)/shard_map/ppermute | solution.py:462
  3.7 8.3 %copy-start = (bf16[1024,128]{1,0:T(8,128)(2,1)S(1)}, bf16[1024,128]{1,0:T(8,128)(2,1)}, u32[]{:S(2)}) copy-start(bf16[1024,128]{1,0:T(8,128)(2,1)} %refs_4_.5) | copy-start | bytes 786436
  9.6 2.6 %collective-permute-start.1 = (bf16[32,1280]{1,0:T(8,128)(2,1)S(1)}, bf16[32,1280]{1,0:T(8,128)(2,1)S(1)}, u32[]{:S(2)}, u32[]{:S(2)}) collective-permute-start(bf16[32,1280]{1,0:T(8,128)(2,1)S(1)} %get-tuple-element.32), channel_id=1, source_target_pairs={{0,1},{1,0},{2,3},{3,2},{4,5},{5,4},{6,7},{7,6},{8,9},{9,8},{10,11... | collective-permute-start | bytes 245768 | tf_op jit(solution)/shard_map/ppermute | solution.py:462
  9.8 5.5 %collective-permute-start.2 = (bf16[32,1280]{1,0:T(8,128)(2,1)S(1)}, bf16[32,1280]{1,0:T(8,128)(2,1)S(1)}, u32[]{:S(2)}, u32[]{:S(2)}) collective-permute-start(bf16[32,1280]{1,0:T(8,128)(2,1)S(1)} %get-tuple-element.33), channel_id=1, source_target_pairs={{0,2},{1,3},{2,0},{3,1},{4,6},{5,7},{6,4},{7,5},{8,10},{9,11},{10,... | collective-permute-start | bytes 245768 | tf_op jit(solution)/shard_map/ppermute | solution.py:462
  10.1 5.6 %collective-permute-start.3 = (bf16[32,1280]{1,0:T(8,128)(2,1)S(1)}, bf16[32,1280]{1,0:T(8,128)(2,1)S(1)}, u32[]{:S(2)}, u32[]{:S(2)}) collective-permute-start(bf16[32,1280]{1,0:T(8,128)(2,1)S(1)} %get-tuple-element.34), channel_id=1, source_target_pairs={{0,3},{1,2},{2,1},{3,0},{4,7},{5,6},{6,5},{7,4},{8,11},{9,10},{10,... | collective-permute-start | bytes 245768 | tf_op jit(solution)/shard_map/ppermute | solution.py:462
  11.5 3.5 %collective-permute-start.5 = (bf16[1024,128]{1,0:T(8,128)(2,1)S(1)}, bf16[1024,128]{1,0:T(8,128)(2,1)S(1)}, u32[]{:S(2)}, u32[]{:S(2)}) collective-permute-start(bf16[1024,128]{1,0:T(8,128)(2,1)S(1)} %collective-permute-done.refs_2_.refs_4_.refs_6_), channel_id=1, source_target_pairs={{0,1},{1,0},{2,3},{3,2},{4,5},{5,4},{6,7},{7,6},{8,9},{9,8},{10,11... | collective-permute-start | bytes 786440 | tf_op jit(solution)/shard_map/ppermute | solution.py:462
  17.3 6.4 %collective-permute-start.6 = (bf16[2,272,128]{2,1,0:T(8,128)(2,1)S(1)}, bf16[2,272,128]{2,1,0:T(8,128)(2,1)S(1)}, u32[]{:S(2)}, u32[]{:S(2)}) collective-permute-start(bf16[2,272,128]{2,1,0:T(8,128)(2,1)S(1)} %systems.4), channel_id=1, source_target_pairs={{0,4},{1,5},{2,6},{3,7},{4,0},{5,1},{6,2},{7,3},{8,12},{9,13},{10,... | collective-permute-start | bytes 417800 | tf_op jit(solution)/shard_map/ppermute | solution.py:462
  20.5 10.0 %collective-permute-start.7 = (bf16[2,272,128]{2,1,0:T(8,128)(2,1)S(1)}, bf16[2,272,128]{2,1,0:T(8,128)(2,1)S(1)}, u32[]{:S(2)}, u32[]{:S(2)}) collective-permute-start(bf16[2,272,128]{2,1,0:T(8,128)(2,1)S(1)} %systems.5), channel_id=1, source_target_pairs={{0,4},{1,5},{2,6},{3,7},{4,0},{5,1},{6,2},{7,3},{8,12},{9,13},{10,... | collective-permute-start | bytes 417800 | tf_op jit(solution)/shard_map/ppermute | solution.py:462
  23.8 8.9 %collective-permute-start.9 = (bf16[272,128]{1,0:T(8,128)(2,1)S(1)}, bf16[272,128]{1,0:T(8,128)(2,1)S(1)}, u32[]{:S(2)}, u32[]{:S(2)}) collective-permute-start(bf16[272,128]{1,0:T(8,128)(2,1)S(1)} %get-tuple-element.38), channel_id=1, source_target_pairs={{0,16},{1,17},{2,18},{3,19},{4,20},{5,21},{6,22},{7,23},{8,24},{9,... | collective-permute-start | bytes 208904 | tf_op jit(solution)/shard_map/ppermute | solution.py:462
  26.4 6.2 %collective-permute-start.8 = (bf16[272,128]{1,0:T(8,128)(2,1)S(1)}, bf16[272,128]{1,0:T(8,128)(2,1)S(1)}, u32[]{:S(2)}, u32[]{:S(2)}) collective-permute-start(bf16[272,128]{1,0:T(8,128)(2,1)S(1)} %get-tuple-element.41), channel_id=1, source_target_pairs={{0,24},{1,25},{2,26},{3,27},{4,28},{5,29},{6,30},{7,31},{8,16},{9,... | collective-permute-start | bytes 208904 | tf_op jit(solution)/shard_map/ppermute | solution.py:462
  30.6 4.4 %collective-permute-start.10 = (bf16[272,128]{1,0:T(8,128)(2,1)S(1)}, bf16[272,128]{1,0:T(8,128)(2,1)S(1)}, u32[]{:S(2)}, u32[]{:S(2)}) collective-permute-start(bf16[272,128]{1,0:T(8,128)(2,1)S(1)} %get-tuple-element.49), channel_id=1, source_target_pairs={{0,8},{1,9},{2,10},{3,11},{4,12},{5,13},{6,14},{7,15},{8,0},{9,1},... | collective-permute-start | bytes 208904 | tf_op jit(solution)/shard_map/ppermute | solution.py:462
  32.6 2.3 %copy-start.1 = (f32[4,128]{1,0:T(4,128)S(1)}, f32[4,128]{1,0:T(4,128)}, u32[]{:S(2)}) copy-start(f32[4,128]{1,0:T(4,128)} %refs_3_.3) | copy-start | bytes 6148

commit v4 on v3

--- a/solution.py
+++ b/solution.py
@@ -182,18 +182,15 @@
     return 64 * item_dev + -(-4 * item_dev // 16) * 16
 
 
-def partial_systems(ef, ut, us, c, item_dev, at):
-    total = None
-    for b, u in enumerate(us):
-        block_users, rank = u.shape
-        cols = slice(b * block_users, (b + 1) * block_users)
-        w = []
-        for j in range(item_dev):
-            e = jnp.broadcast_to(ef[c, j : j + 1, cols], (16, block_users)).astype(bf16)
-            w.append(jnp.concatenate([e] * (rank // 16), 0) * ut[:, at + cols.start : at + cols.stop])
-        g = jnp.dot(jnp.concatenate(w, 0), u[...], preferred_element_type=f32)
-        total = g if total is None else total + g
-    return total
+def partial_systems(rows, ut, us, c, item_dev, at):
+    rank = ut.shape[0]
+    w = []
+    for j in range(item_dev):
+        one = c * item_dev + j
+        e = jnp.concatenate([r[one : one + 1] for r in rows], 1)
+        e = jnp.broadcast_to(e, (16, e.shape[1])).astype(bf16)
+        w.append(jnp.concatenate([e] * (rank // 16), 0) * ut[:, at : at + e.shape[1]])
+    return jnp.dot(jnp.concatenate(w, 0), jnp.concatenate([u[...] for u in us], 0), preferred_element_type=f32)
 
 
 def some_rows(ref, first, n, cols):
@@ -201,22 +198,11 @@
     return ref[low:high, cols].astype(f32)[first - low : first - low + n]
 
 
-def spread_rows(ef, es, first, n_items, item_dev, block_users):
-    for b, e in enumerate(es):
-        value = some_rows(e, first, n_items, slice(0, block_users))
-        for c in range(n_items // item_dev):
-            ef[c, :, b * block_users : (b + 1) * block_users] = value[c * item_dev : (c + 1) * item_dev]
-
-
 def begun_kernel(first, n_items, item_dev, n, *refs):
-    es, us, ut, out, ef = refs[:n], refs[n : 2 * n], refs[2 * n], refs[2 * n + 1], refs[2 * n + 2]
-    spread_rows(ef, es, first, n_items, item_dev, us[0].shape[0])
-
-    def body(c, _):
-        out[c] = partial_systems(ef, ut, us, c, item_dev, 0)
-        return 0
-
-    lax.fori_loop(0, n_items // item_dev, body, 0)
+    es, us, ut, out = refs[:n], refs[n : 2 * n], refs[2 * n], refs[2 * n + 1]
+    rows = [some_rows(e, first, n_items, slice(0, us[0].shape[0])) for e in es]
+    for c in range(n_items // item_dev):
+        out[c] = partial_systems(rows, ut, us, c, item_dev, 0)
 
 
 def begun(es, us, ut, first, n_items, item_dev):
@@ -227,7 +213,6 @@
         in_specs=[VMEM] * (2 * n + 1),
         out_specs=VMEM,
         out_shape=struct((n_items // item_dev, item_dev * rank, rank), f32),
-        scratch_shapes=[pltpu.VMEM((n_items // item_dev, item_dev, n * block_users), f32)],
         compiler_params=params(32),
         cost_estimate=cost(2.6),
         name="begun",
@@ -237,24 +222,21 @@
 def systems_kernel(first, n_items, item_dev, keep, n, done, at, *refs):
     es, us, ut = refs[:n], refs[n : 2 * n - done], refs[2 * n - done]
     start = refs[2 * n - done + 1] if done else None
-    out, ef = refs[-2:]
+    out = refs[-1]
     block_users, rank = us[0].shape
-    wide = (n - done) * block_users
-    spread_rows(ef, es[done:], first, n_items, item_dev, block_users)
+    rows = [some_rows(e, first, n_items, slice(0, block_users)) for e in es[done:]]
     rhs = jnp.zeros((n_items, rank), f32)
     for e in es:
         rhs = rhs + some_rows(e, first, n_items, slice(block_users, block_users + rank))
         rhs = rhs + some_rows(e, first, n_items, slice(block_users + rank, block_users + 2 * rank))
-    for c in range(n_items // item_dev):
-        ef[c, :, wide:] = rhs[c * item_dev : (c + 1) * item_dev]
     row = lax.broadcasted_iota(i32, (64, rank), 0)
     lane = lax.broadcasted_iota(i32, (64, rank), 1)
     eye = lax.broadcasted_iota(i32, (rank, rank), 0) == lax.broadcasted_iota(i32, (rank, rank), 1)
     above = (lane < 64) & (lane > row)
     base = 64 * item_dev
 
-    def body(c, _):
-        total = partial_systems(ef, ut, us, c, item_dev, done * block_users)
+    for c in range(n_items // item_dev):
+        total = partial_systems(rows, ut, us, c, item_dev, done * block_users)
         if done:
             total = total + start[at + c]
         diag = []
@@ -264,11 +246,10 @@
             out[c, 64 * j : 64 * j + 64, :] = packed.astype(out.dtype)
             diag.append(jnp.sum(jnp.where(eye, g, 0.0), axis=0, keepdims=True))
         diag = jnp.concatenate(diag, 0)
-        side = ef[c, :, wide:]
-        put_extras(lambda a, n, v: out.__setitem__((c, slice(base + a, base + a + n)), v), diag, side, keep, item_dev)
-        return 0
-
-    lax.fori_loop(0, n_items // item_dev, body, 0)
+        side = rhs[c * item_dev : (c + 1) * item_dev]
+        put_extras(
+            lambda a, n, v, c=c: out.__setitem__((c, slice(base + a, base + a + n)), v), diag, side, keep, item_dev
+        )
 
 
 def put_extras(put, diag, side, keep, item_dev):
@@ -296,7 +277,6 @@
         in_specs=[VMEM] * (2 * n - done + 1 + len(more)),
         out_specs=VMEM,
         out_shape=struct((n_items // item_dev, chunk_rows(item_dev), rank), f32 if keep else bf16),
-        scratch_shapes=[pltpu.VMEM((n_items // item_dev, item_dev, (n - done) * block_users + rank), f32)],
         compiler_params=params(40),
         cost_estimate=cost(0.082 * (n - done) * n_items if us_cost is None else us_cost),
         name="systems",
@@ -309,11 +289,11 @@
     return part[0] + part[1], part[2] + part[3]
 
 
-def merge_kernel(item_dev, n_keep, apart, own, got, *outs):
+def merge_kernel(item_dev, n_keep, apart, skip, own, got, *outs):
     kept, sent = outs[0], outs[bool(n_keep) :]
     base = 64 * item_dev
     for c in range(own.shape[0]):
-        value = own[c] + got[c].astype(f32)
+        value = own[c] + got[c + skip].astype(f32)
         diag, side = extras(value, item_dev)
         if c < n_keep:
             kept[c, :base, :] = value[:base]
@@ -328,13 +308,13 @@
             )
 
 
-def merged(own, got, item_dev, n_keep, apart):
+def merged(own, got, item_dev, n_keep, apart, skip=0):
     chunks, rows, rank = own.shape
     n_sent = chunks - n_keep
     shapes = [struct((rows, rank), bf16)] * n_sent if apart else [struct((n_sent, rows, rank), bf16)]
     shapes = ([struct((n_keep, rows, rank), f32)] if n_keep else []) + shapes
     return pl.pallas_call(
-        functools.partial(merge_kernel, item_dev, n_keep, apart),
+        functools.partial(merge_kernel, item_dev, n_keep, apart, skip),
         in_specs=[VMEM] * 2,
         out_specs=[VMEM] * len(shapes),
         out_shape=shapes,
@@ -344,10 +324,12 @@
 
 
 def gradients_kernel(item_dev, own, *refs):
-    *got, prev, out, half = refs
+    *got, prev_far, out, half, prev, sem = refs
+    fetch = pltpu.make_async_copy(prev_far, prev, sem)
+    fetch.start()
     value = own[0]
     for g in got:
-        value = value + g[...].astype(f32)
+        value = value + (g[...] if len(g.shape) == 2 else g[0]).astype(f32)
     rank = value.shape[1]
     diag, side = extras(value, item_dev)
     row = lax.broadcasted_iota(i32, (64, 64), 0)
@@ -372,6 +354,7 @@
             rows.append(jnp.sum(jnp.where(eye, s, 0.0), axis=0, keepdims=True))
         return jnp.concatenate(rows, 0)
 
+    fetch.wait()
     solution = prev[...]
     residual = side - apply(solution)
     direction = residual
@@ -394,16 +377,17 @@
     item_dev, rank = prev.shape
     return pl.pallas_call(
         functools.partial(gradients_kernel, item_dev),
-        in_specs=[VMEM] * (2 + len(got)),
+        in_specs=[VMEM] * (1 + len(got)) + [pl.BlockSpec(memory_space=pltpu.HBM)],
         out_specs=[VMEM] * 2,
         out_shape=[struct(prev.shape, f32), struct((devices,) + prev.shape, bf16)],
+        scratch_shapes=[pltpu.VMEM(prev.shape, f32), pltpu.SemaphoreType.DMA(())],
         compiler_params=params(16),
         cost_estimate=cost(2),
         name="gradients",
-    )(own, *got, prev)
-
-
-def user_side_kernel(item_dev, n_grp, n_user, me_s, returned, c_hi, c_lo, out, rows, order):
+    )(own, *got, pltpu.with_memory_space_constraint(prev, pltpu.HBM))
+
+
+def user_side_kernel(item_dev, n_grp, n_user, me_s, returned, c_hi, c_lo, out, rows, order, made, sem):
     num_items = returned.shape[0]
     rows[...] = returned[...].astype(f32)
     me = me_s[0]
@@ -411,19 +395,28 @@
         owner = owner_of(group, item_dev, n_grp, n_user) ^ me
         order[group * item_dev : (group + 1) * item_dev, :] = rows[pl.ds(owner * item_dev, item_dev), :]
     ret = order[...].astype(bf16)
-    out[...] = jnp.dot(c_hi[...], ret, preferred_element_type=f32) + jnp.dot(
-        c_lo[...], ret, preferred_element_type=f32
-    )
+    copies = []
+    for c in range(made.shape[0]):
+        rows_c = slice(c * made.shape[1], (c + 1) * made.shape[1])
+        made[c] = jnp.dot(c_hi[rows_c], ret, preferred_element_type=f32) + jnp.dot(
+            c_lo[rows_c], ret, preferred_element_type=f32
+        )
+        copies.append(pltpu.make_async_copy(made.at[c], out.at[rows_c], sem.at[c]))
+        copies[-1].start()
+    for copy in copies:
+        copy.wait()
 
 
 def user_side(me, returned, c_hi, c_lo, item_dev, n_grp, n_user):
     num_items, rank = returned.shape
+    pieces = 4
     return pl.pallas_call(
         functools.partial(user_side_kernel, item_dev, n_grp, n_user),
         in_specs=[SMEM, VMEM, VMEM, VMEM],
-        out_specs=VMEM,
+        out_specs=pl.BlockSpec(memory_space=pltpu.HBM),
         out_shape=struct((c_hi.shape[0], rank), f32),
-        scratch_shapes=[pltpu.VMEM((num_items, rank), f32)] * 2,
+        scratch_shapes=[pltpu.VMEM((num_items, rank), f32)] * 2
+        + [pltpu.VMEM((pieces, c_hi.shape[0] // pieces, rank), f32), pltpu.SemaphoreType.DMA((pieces,))],
         compiler_params=params(16),
         cost_estimate=cost(1),
         name="user_side",
@@ -488,9 +481,12 @@
         far = merged(own, far_other, item_dev, 0, True)
         parts = [swap(value, n_grp * 2 * (chunks + n)) for n, value in reversed(list(enumerate(far)))]
         ut, _ = lax.optimization_barrier((ut, far[0]))
-        own = systems(got, us, ut, 0, n_far, item_dev, True)
-        own, *near = merged(own, near_other, item_dev, 1, True)
+        own = systems(got, us, ut, item_dev, n_far - item_dev, item_dev, True)
+        near = merged(own, near_other, item_dev, 0, True, 1)
         parts += [swap(value, n_grp * 2 * (n + 1)) for n, value in enumerate(near)]
+        ut, _ = lax.optimization_barrier((ut, own))
+        own = systems(got, us, ut, 0, item_dev, item_dev, True)
+        parts.append(near_other)
     else:
         left, bit = n_user, n_grp
         sent = systems(got, us, ut, n_half, n_half, item_dev, False, start, 2)

time: 49.5 us -> 48.5 us (0.980)
  Pallas kernels: 21.1 us -> 20.3 us
    pallas_call x4 -> x5, Pallas kernels: 8.51 us -> 7.66 us  [systems(): pl.pallas_call(functools.partial(systems_kernel, first, n_items, item_dev...]
    pallas_call x1, Pallas kernels: 2.08 us -> 2.7 us  [gradients(): pl.pallas_call(functools.partial(gradients_kernel, item_dev), in_specs=[V...]
    pallas_call x1, Pallas kernels: 2.82 us -> 2.32 us  [begun(): pl.pallas_call(functools.partial(begun_kernel, first, n_items, item_dev,...]
  transfers between devices with their start and end apart: 11 -> 11, of which waited for: 3 -> 5; matrix products, arithmetic and copies ran while one was open for 0% -> 0% of each run, Pallas kernels for 33% -> 32%
where the time goes in v4:
time: 48.5 us; the launch traced here: 48.3 us
  Pallas kernels  20.3 us (42%)
  starting transfers between devices  11.9 us (25%)
  blocking collectives  11.1 us (23%)
  waiting for transfers between devices  4.19 us (9%)
  between operations  0.74 us (2%)
    ppermute x11, starting transfers between devices, swap(): return lax.ppermute(value, AXES, [(d, d ^ bit) for d in range(devices)])  11.9 us
    all_to_all x1, blocking collectives, shards(): lax.all_to_all(spread, AXES, 0, 0, tiled=True).reshape(num_items, rank)  11.1 us
    pallas_call x5, Pallas kernels, systems(): pl.pallas_call(functools.partial(systems_kernel, first, n_items, item_dev...  7.66 us
    pallas_call x1, Pallas kernels, histogram(): pl.pallas_call(functools.partial(histogram_kernel, step, low_part, item_d...  5.85 us
    ppermute x11, waiting for transfers between devices, swap(): return lax.ppermute(value, AXES, [(d, d ^ bit) for d in range(devices)])  4.19 us
    pallas_call x1, Pallas kernels, gradients(): pl.pallas_call(functools.partial(gradients_kernel, item_dev), in_specs=[V...  2.7 us
    pallas_call x1, Pallas kernels, begun(): pl.pallas_call(functools.partial(begun_kernel, first, n_items, item_dev,...  2.32 us
    pallas_call x1, Pallas kernels, user_side(): pl.pallas_call(functools.partial(user_side_kernel, item_dev, n_grp, n_use...  1.06 us
  transfers between devices with their start and end apart: 11, of which 5 were waited for; matrix products, arithmetic and copies ran while one was open for 0% of the time, Pallas kernels for 32%

profile of v4, /device:TPU:0, one launch (start us, length us, event | category | flops | bytes accessed | tf_op | source)
XLA Modules:
  0.0 48.3 jit_solution(18036751865023831177)
XLA Ops:
  0.6 0.5 %collective-permute-start.4 = (bf16[1024,128]{1,0:T(8,128)(2,1)}, bf16[1024,128]{1,0:T(8,128)(2,1)S(1)}, u32[]{:S(2)}, u32[]{:S(2)}) collective-permute-start(bf16[1024,128]{1,0:T(8,128)(2,1)} %refs_4_.8), channel_id=1, source_target_pairs={{0,1},{1,0},{2,3},{3,2},{4,5},{5,4},{6,7},{7,6},{8,9},{9,8},{10,11... | collective-permute-start | bytes 786440 | tf_op jit(solution)/shard_map/ppermute | solution.py:455
  1.1 2.6 %collective-permute-start = (bf16[1024,128]{1,0:T(8,128)(2,1)}, bf16[1024,128]{1,0:T(8,128)(2,1)S(1)}, u32[]{:S(2)}, u32[]{:S(2)}) collective-permute-start(bf16[1024,128]{1,0:T(8,128)(2,1)} %refs_4_.8), channel_id=1, source_target_pairs={{0,2},{1,3},{2,0},{3,1},{4,6},{5,7},{6,4},{7,5},{8,10},{9,11},{10,... | collective-permute-start | bytes 786440 | tf_op jit(solution)/shard_map/ppermute | solution.py:455
  3.7 0.0 copy-start
  3.7 5.9 %histogram.1 = (bf16[32,1280]{1,0:T(8,128)(2,1)S(1)}, bf16[32,1280]{1,0:T(8,128)(2,1)S(1)}, bf16[32,1280]{1,0:T(8,128)(2,1)S(1)}, bf16[32,1280]{1,0:T(8,128)(2,1...) custom-call(s32[1]{0:T(128)} %bitcast.me_s, s32[1,384]{1,0:T(1,128)} %refs_0_.3, s32[1,384]{1,0:T(1,128)} %refs_1_.1, ...), custom_call_target="tpu_custom_call" | custom-call | flops 7000000000 | bytes 21000000 | tf_op jit(solution)/shard_map/histogram/pallas_call | solution.py:138
  9.6 0.2 collective-permute-start.1
  9.8 0.3 collective-permute-start.2
  10.1 1.4 %collective-permute-start.3 = (bf16[32,1280]{1,0:T(8,128)(2,1)S(1)}, bf16[32,1280]{1,0:T(8,128)(2,1)S(1)}, u32[]{:S(2)}, u32[]{:S(2)}) collective-permute-start(bf16[32,1280]{1,0:T(8,128)(2,1)S(1)} %get-tuple-element.33), channel_id=1, source_target_pairs={{0,3},{1,2},{2,1},{3,0},{4,7},{5,6},{6,5},{7,4},{8,11},{9,10},{10,... | collective-permute-start | bytes 245768 | tf_op jit(solution)/shard_map/ppermute | solution.py:455
  11.5 0.0 collective-permute-done.refs_2_.refs_4_.refs_6_
  11.5 0.5 collective-permute-start.5
  12.0 0.0 collective-permute-done.4.refs_1_.refs_3_.refs_5_
  12.0 0.0 copy-done
  12.0 0.2 transpose.3.refs_4_
  12.2 0.0 collective-permute-done.1.refs_1_
  12.2 2.3 %begun.1.refs_7_ = f32[4,512,128]{2,1,0:T(8,128)S(1)} custom-call(bf16[32,1280]{1,0:T(8,128)(2,1)S(1)} %get-tuple-element.30.refs_0_, bf16[32,1280]{1,0:T(8,128)(2,1)S(1)} %collective-permute-done.1.refs_1_, bf16[1024,128]{1,0:T(8,128)(2,1)S(1)} %copy-done, bf16[1024,128]{1,0:T(8,128)(2,1)S(1)} %collective-permute-done.4.refs_1_.refs_3_.refs_5_, ...), custom_call_target="tpu_custom_call" | custom-call | flops 2600000000 | bytes 7800000 | tf_op jit(solution)/shard_map/begun/pallas_call | solution.py:211
  14.5 0.0 collective-permute-done.5.refs_3_.refs_5_.refs_7_
  14.5 0.3 transpose.2.refs_6_.refs_8_
  14.9 0.2 collective-permute-done.2.refs_2_
  15.1 0.6 %collective-permute-done.3.refs_3_ = bf16[32,1280]{1,0:T(8,128)(2,1)S(1)} collective-permute-done((bf16[32,1280]{1,0:T(8,128)(2,1)S(1)}, bf16[32,1280]{1,0:T(8,128)(2,1)S(1)}, u32[]{:S(2)}, u32[]{:S(2)}) %collective-permute-start.3) | collective-permute-done | bytes 81952 | tf_op jit(solution)/shard_map/ppermute | solution.py:455
  15.7 1.3 %systems.5 = bf16[2,272,128]{2,1,0:T(8,128)(2,1)S(1)} custom-call(bf16[32,1280]{1,0:T(8,128)(2,1)S(1)} %get-tuple-element.30.refs_0_, bf16[32,1280]{1,0:T(8,128)(2,1)S(1)} %collective-permute-done.1.refs_1_, bf16[32,1280]{1,0:T(8,128)(2,1)S(1)} %collective-permute-done.2.refs_2_, bf16[32,1280]{1,0:T(8,128)(2,1)S(1)} %collective-permute-done.3.refs_3_, ...), custom_call_target="tpu_custom_call" | custom-call | flops 1312000000 | bytes 3936000 | tf_op jit(solution)/shard_map/systems/pallas_call | solution.py:275
  17.0 1.6 %collective-permute-start.6 = (bf16[2,272,128]{2,1,0:T(8,128)(2,1)S(1)}, bf16[2,272,128]{2,1,0:T(8,128)(2,1)S(1)}, u32[]{:S(2)}, u32[]{:S(2)}) collective-permute-start(bf16[2,272,128]{2,1,0:T(8,128)(2,1)S(1)} %systems.5), channel_id=1, source_target_pairs={{0,4},{1,5},{2,6},{3,7},{4,0},{5,1},{6,2},{7,3},{8,12},{9,13},{10,... | collective-permute-start | bytes 417800 | tf_op jit(solution)/shard_map/ppermute | solution.py:455
  18.6 1.3 %systems.6 = bf16[2,272,128]{2,1,0:T(8,128)(2,1)S(1)} custom-call(bf16[32,1280]{1,0:T(8,128)(2,1)S(1)} %get-tuple-element.30.refs_0_, bf16[32,1280]{1,0:T(8,128)(2,1)S(1)} %collective-permute-done.1.refs_1_, bf16[32,1280]{1,0:T(8,128)(2,1)S(1)} %collective-permute-done.2.refs_2_, bf16[32,1280]{1,0:T(8,128)(2,1)S(1)} %collective-permute-done.3.refs_3_, ...), custom_call_target="tpu_custom_call" | custom-call | flops 1312000000 | bytes 3936000 | tf_op jit(solution)/shard_map/systems/pallas_call | solution.py:275
  19.9 0.6 %collective-permute-start.9 = (bf16[2,272,128]{2,1,0:T(8,128)(2,1)S(1)}, bf16[2,272,128]{2,1,0:T(8,128)(2,1)S(1)}, u32[]{:S(2)}, u32[]{:S(2)}) collective-permute-start(bf16[2,272,128]{2,1,0:T(8,128)(2,1)S(1)} %systems.6), channel_id=1, source_target_pairs={{0,4},{1,5},{2,6},{3,7},{4,0},{5,1},{6,2},{7,3},{8,12},{9,13},{10,... | collective-permute-start | bytes 417800 | tf_op jit(solution)/shard_map/ppermute | solution.py:455
  20.5 2.4 %systems.7.own = f32[2,272,128]{2,1,0:T(8,128)S(1)} custom-call(bf16[32,1280]{1,0:T(8,128)(2,1)S(1)} %get-tuple-element.30.refs_0_, bf16[32,1280]{1,0:T(8,128)(2,1)S(1)} %collective-permute-done.1.refs_1_, bf16[32,1280]{1,0:T(8,128)(2,1)S(1)} %collective-permute-done.2.refs_2_, bf16[32,1280]{1,0:T(8,128)(2,1)S(1)} %collective-permute-done.3.refs_3_, ...), custom_call_target="tpu_custom_call" | custom-call | flops 10000000 | bytes 30000 | tf_op jit(solution)/shard_map/systems/pallas_call | solution.py:275
  22.9 0.5 %collective-permute-done.6.got = bf16[2,272,128]{2,1,0:T(8,128)(2,1)S(1)} collective-permute-done((bf16[2,272,128]{2,1,0:T(8,128)(2,1)S(1)}, bf16[2,272,128]{2,1,0:T(8,128)(2,1)S(1)}, u32[]{:S(2)}, u32[]{:S(2)}) %collective-permute-start.6) | collective-permute-done | bytes 139296 | tf_op jit(solution)/shard_map/ppermute | solution.py:455
  23.4 2.7 %collective-permute-start.8 = (bf16[272,128]{1,0:T(8,128)(2,1)S(1)}, bf16[272,128]{1,0:T(8,128)(2,1)S(1)}, u32[]{:S(2)}, u32[]{:S(2)}) collective-permute-start(bf16[272,128]{1,0:T(8,128)(2,1)S(1)} %get-tuple-element.37), channel_id=1, source_target_pairs={{0,16},{1,17},{2,18},{3,19},{4,20},{5,21},{6,22},{7,23},{8,24},{9,... | collective-permute-start | bytes 208904 | tf_op jit(solution)/shard_map/ppermute | solution.py:455
  26.1 1.4 %collective-permute-start.7 = (bf16[272,128]{1,0:T(8,128)(2,1)S(1)}, bf16[272,128]{1,0:T(8,128)(2,1)S(1)}, u32[]{:S(2)}, u32[]{:S(2)}) collective-permute-start(bf16[272,128]{1,0:T(8,128)(2,1)S(1)} %get-tuple-element.40), channel_id=1, source_target_pairs={{0,24},{1,25},{2,26},{3,27},{4,28},{5,29},{6,30},{7,31},{8,16},{9,... | collective-permute-start | bytes 208904 | tf_op jit(solution)/shard_map/ppermute | solution.py:455
  27.5 1.3 %systems.8.own = f32[1,272,128]{2,1,0:T(8,128)S(1)} custom-call(bf16[32,1280]{1,0:T(8,128)(2,1)S(1)} %get-tuple-element.30.refs_0_, bf16[32,1280]{1,0:T(8,128)(2,1)S(1)} %collective-permute-done.1.refs_1_, bf16[32,1280]{1,0:T(8,128)(2,1)S(1)} %collective-permute-done.2.refs_2_, bf16[32,1280]{1,0:T(8,128)(2,1)S(1)} %collective-permute-done.3.refs_3_, ...), custom_call_target="tpu_custom_call" | custom-call | flops 1312000000 | bytes 3936000 | tf_op jit(solution)/shard_map/systems/pallas_call | solution.py:275
  28.8 0.0 collective-permute-done.9.got.refs_3_
  28.8 0.2 collective-permute-start.10
  29.1 1.3 %systems.9.own = f32[1,272,128]{2,1,0:T(8,128)S(1)} custom-call(bf16[32,1280]{1,0:T(8,128)(2,1)S(1)} %get-tuple-element.30.refs_0_, bf16[32,1280]{1,0:T(8,128)(2,1)S(1)} %collective-permute-done.1.refs_1_, bf16[32,1280]{1,0:T(8,128)(2,1)S(1)} %collective-permute-done.2.refs_2_, bf16[32,1280]{1,0:T(8,128)(2,1)S(1)} %collective-permute-done.3.refs_3_, ...), custom_call_target="tpu_custom_call" | custom-call | flops 1312000000 | bytes 3936000 | tf_op jit(solution)/shard_map/systems/pallas_call | solution.py:275
  30.4 2.6 %collective-permute-done.7.refs_0_ = bf16[272,128]{1,0:T(8,128)(2,1)S(1)} collective-permute-done((bf16[272,128]{1,0:T(8,128)(2,1)S(1)}, bf16[272,128]{1,0:T(8,128)(2,1)S(1)}, u32[]{:S(2)}, u32[]{:S(2)}) %collective-permute-start.7) | collective-permute-done | bytes 69664 | tf_op jit(solution)/shard_map/ppermute | solution.py:455
  33.0 0.0 collective-permute-done.8.refs_1_
  33.0 0.2 flip.1
  33.2 0.3 collective-permute-done.10.refs_2_
  33.5 2.7 %gradients.1 = (f32[4,128]{1,0:T(4,128)}, bf16[32,4,128]{2,1,0:T(4,128)(2,1)S(1)}) custom-call(f32[1,272,128]{2,1,0:T(8,128)S(1)} %systems.9.own, bf16[272,128]{1,0:T(8,128)(2,1)S(1)} %collective-permute-done.7.refs_0_, bf16[272,128]{1,0:T(8,128)(2,1)S(1)} %collective-permute-done.8.refs_1_, bf16[272,128]{1,0:T(8,128)(2,1)S(1)} %collective-permute-done.10.refs_2_, ...), custom_call_target="tpu_custom_call" | custom-call | flops 2000000000 | bytes 6000000 | tf_op jit(solution)/shard_map/gradients/pallas_call | solution.py:378
  36.2 11.1 %all_to_all.5 = bf16[32,4,128]{2,1,0:T(4,128)(2,1)S(1)} all-to-all(bf16[32,4,128]{2,1,0:T(4,128)(2,1)S(1)} %get-tuple-element.49), channel_id=1, replica_groups=mesh['user'=8,'grp'=4] {'user','grp'}, dimensions={0} | all-to-all | bytes 65536 | tf_op jit(solution)/shard_map/all_to_all | solution.py:506
  47.3 1.1 %user_side.1 = f32[1024,128]{1,0:T(8,128)} custom-call(s32[1]{0:T(128)} %bitcast.me_s, bf16[128,128]{1,0:T(8,128)(2,1)S(1)} %bitcast.2, bf16[1024,128]{1,0:T(8,128)(2,1)S(1)} %get-tuple-element.50.c_hi, bf16[1024,128]{1,0:T(8,128)(2,1)S(1)} %get-tuple-element.51.c_lo), custom_call_target="tpu_custom_call" | custom-call | flops 1000000000 | bytes 3000000 | tf_op jit(solution)/shard_map/user_side/pallas_call | solution.py:413
  (2 shorter events, 0.1 us)
Async XLA Ops:
  0.6 11.4 %collective-permute-start.4 = (bf16[1024,128]{1,0:T(8,128)(2,1)}, bf16[1024,128]{1,0:T(8,128)(2,1)S(1)}, u32[]{:S(2)}, u32[]{:S(2)}) collective-permute-start(bf16[1024,128]{1,0:T(8,128)(2,1)} %refs_4_.8), channel_id=1, source_target_pairs={{0,1},{1,0},{2,3},{3,2},{4,5},{5,4},{6,7},{7,6},{8,9},{9,8},{10,11... | collective-permute-start | bytes 786440 | tf_op jit(solution)/shard_map/ppermute | solution.py:455
  1.1 10.4 %collective-permute-start = (bf16[1024,128]{1,0:T(8,128)(2,1)}, bf16[1024,128]{1,0:T(8,128)(2,1)S(1)}, u32[]{:S(2)}, u32[]{:S(2)}) collective-permute-start(bf16[1024,128]{1,0:T(8,128)(2,1)} %refs_4_.8), channel_id=1, source_target_pairs={{0,2},{1,3},{2,0},{3,1},{4,6},{5,7},{6,4},{7,5},{8,10},{9,11},{10,... | collective-permute-start | bytes 786440 | tf_op jit(solution)/shard_map/ppermute | solution.py:455
  3.7 8.3 %copy-start = (bf16[1024,128]{1,0:T(8,128)(2,1)S(1)}, bf16[1024,128]{1,0:T(8,128)(2,1)}, u32[]{:S(2)}) copy-start(bf16[1024,128]{1,0:T(8,128)(2,1)} %refs_4_.8) | copy-start | bytes 786436
  9.6 2.6 %collective-permute-start.1 = (bf16[32,1280]{1,0:T(8,128)(2,1)S(1)}, bf16[32,1280]{1,0:T(8,128)(2,1)S(1)}, u32[]{:S(2)}, u32[]{:S(2)}) collective-permute-start(bf16[32,1280]{1,0:T(8,128)(2,1)S(1)} %get-tuple-element.31), channel_id=1, source_target_pairs={{0,1},{1,0},{2,3},{3,2},{4,5},{5,4},{6,7},{7,6},{8,9},{9,8},{10,11... | collective-permute-start | bytes 245768 | tf_op jit(solution)/shard_map/ppermute | solution.py:455
  9.8 5.3 %collective-permute-start.2 = (bf16[32,1280]{1,0:T(8,128)(2,1)S(1)}, bf16[32,1280]{1,0:T(8,128)(2,1)S(1)}, u32[]{:S(2)}, u32[]{:S(2)}) collective-permute-start(bf16[32,1280]{1,0:T(8,128)(2,1)S(1)} %get-tuple-element.32), channel_id=1, source_target_pairs={{0,2},{1,3},{2,0},{3,1},{4,6},{5,7},{6,4},{7,5},{8,10},{9,11},{10,... | collective-permute-start | bytes 245768 | tf_op jit(solution)/shard_map/ppermute | solution.py:455
  10.1 5.6 %collective-permute-start.3 = (bf16[32,1280]{1,0:T(8,128)(2,1)S(1)}, bf16[32,1280]{1,0:T(8,128)(2,1)S(1)}, u32[]{:S(2)}, u32[]{:S(2)}) collective-permute-start(bf16[32,1280]{1,0:T(8,128)(2,1)S(1)} %get-tuple-element.33), channel_id=1, source_target_pairs={{0,3},{1,2},{2,1},{3,0},{4,7},{5,6},{6,5},{7,4},{8,11},{9,10},{10,... | collective-permute-start | bytes 245768 | tf_op jit(solution)/shard_map/ppermute | solution.py:455
  11.5 3.0 %collective-permute-start.5 = (bf16[1024,128]{1,0:T(8,128)(2,1)S(1)}, bf16[1024,128]{1,0:T(8,128)(2,1)S(1)}, u32[]{:S(2)}, u32[]{:S(2)}) collective-permute-start(bf16[1024,128]{1,0:T(8,128)(2,1)S(1)} %collective-permute-done.refs_2_.refs_4_.refs_6_), channel_id=1, source_target_pairs={{0,1},{1,0},{2,3},{3,2},{4,5},{5,4},{6,7},{7,6},{8,9},{9,8},{10,11... | collective-permute-start | bytes 786440 | tf_op jit(solution)/shard_map/ppermute | solution.py:455
  17.0 6.4 %collective-permute-start.6 = (bf16[2,272,128]{2,1,0:T(8,128)(2,1)S(1)}, bf16[2,272,128]{2,1,0:T(8,128)(2,1)S(1)}, u32[]{:S(2)}, u32[]{:S(2)}) collective-permute-start(bf16[2,272,128]{2,1,0:T(8,128)(2,1)S(1)} %systems.5), channel_id=1, source_target_pairs={{0,4},{1,5},{2,6},{3,7},{4,0},{5,1},{6,2},{7,3},{8,12},{9,13},{10,... | collective-permute-start | bytes 417800 | tf_op jit(solution)/shard_map/ppermute | solution.py:455
  19.9 8.9 %collective-permute-start.9 = (bf16[2,272,128]{2,1,0:T(8,128)(2,1)S(1)}, bf16[2,272,128]{2,1,0:T(8,128)(2,1)S(1)}, u32[]{:S(2)}, u32[]{:S(2)}) collective-permute-start(bf16[2,272,128]{2,1,0:T(8,128)(2,1)S(1)} %systems.6), channel_id=1, source_target_pairs={{0,4},{1,5},{2,6},{3,7},{4,0},{5,1},{6,2},{7,3},{8,12},{9,13},{10,... | collective-permute-start | bytes 417800 | tf_op jit(solution)/shard_map/ppermute | solution.py:455
  23.4 9.6 %collective-permute-start.8 = (bf16[272,128]{1,0:T(8,128)(2,1)S(1)}, bf16[272,128]{1,0:T(8,128)(2,1)S(1)}, u32[]{:S(2)}, u32[]{:S(2)}) collective-permute-start(bf16[272,128]{1,0:T(8,128)(2,1)S(1)} %get-tuple-element.37), channel_id=1, source_target_pairs={{0,16},{1,17},{2,18},{3,19},{4,20},{5,21},{6,22},{7,23},{8,24},{9,... | collective-permute-start | bytes 208904 | tf_op jit(solution)/shard_map/ppermute | solution.py:455
  26.1 6.9 %collective-permute-start.7 = (bf16[272,128]{1,0:T(8,128)(2,1)S(1)}, bf16[272,128]{1,0:T(8,128)(2,1)S(1)}, u32[]{:S(2)}, u32[]{:S(2)}) collective-permute-start(bf16[272,128]{1,0:T(8,128)(2,1)S(1)} %get-tuple-element.40), channel_id=1, source_target_pairs={{0,24},{1,25},{2,26},{3,27},{4,28},{5,29},{6,30},{7,31},{8,16},{9,... | collective-permute-start | bytes 208904 | tf_op jit(solution)/shard_map/ppermute | solution.py:455
  28.8 4.6 %collective-permute-start.10 = (bf16[272,128]{1,0:T(8,128)(2,1)S(1)}, bf16[272,128]{1,0:T(8,128)(2,1)S(1)}, u32[]{:S(2)}, u32[]{:S(2)}) collective-permute-start(bf16[272,128]{1,0:T(8,128)(2,1)S(1)} %merge.3), channel_id=1, source_target_pairs={{0,8},{1,9},{2,10},{3,11},{4,12},{5,13},{6,14},{7,15},{8,0},{9,1},... | collective-permute-start | bytes 208904 | tf_op jit(solution)/shard_map/ppermute | solution.py:455

commit v5 on v4

--- a/solution.py
+++ b/solution.py
@@ -57,20 +57,21 @@
 
 
 def histogram_kernel(step, low_part, item_dev, n_grp, n_user, me_s, *refs):
-    sources, rest = refs[:5], refs[5:]
+    sources, rest = refs[:6], refs[6:]
     eouts = rest[:n_grp]
-    c_hi, c_lo, acc, *here, sem = rest[n_grp:]
+    c_hi, c_lo, prev_here, acc, *here, sem = rest[n_grp:]
+    here.append(prev_here)
     copies = [pltpu.make_async_copy(a, b, sem.at[n]) for n, (a, b) in enumerate(zip(sources, here))]
     for copy in copies:
         copy.start()
-    valid_s, item_s, users, counts, u = here
+    valid_s, item_s, users, counts, u, _ = here
     tiles, rows = users.shape[1:]
     num_items = c_hi.shape[0]
     block_users = u.shape[0]
     his = block_users // low_part
     kinds = 2 * his
+    pitch = kinds + 8
     me = me_s[0]
-    acc[...] = jnp.zeros_like(acc)
     for copy in copies[:4]:
         copy.wait()
     lane = lax.broadcasted_iota(i32, (his, rows), 1)
@@ -79,7 +80,7 @@
     zero = jnp.zeros((kinds, rows), bf16)
     one, nil = jnp.ones((low_part, rows), bf16), jnp.zeros((low_part, rows), bf16)
 
-    def body(b, _):
+    def body(b, run):
         base = pl.multiple_of(b * step, step)
         blk = users[0, pl.ds(base, step), :]
         cnt = counts[0, pl.ds(base, step), :].astype(f32) * confidence_rate
@@ -102,17 +103,20 @@
                 left, jnp.concatenate(oh, 1), (((1,), (1,)), ((), ())), preferred_element_type=f32
             )
             for q, j in enumerate((t, t + 1)):
-                p = slot_of(item_s[0, base + j], me, item_dev, n_grp, n_user)
-                acc[pl.ds(pl.multiple_of(p * kinds, kinds), kinds), :] += out[kinds * q : kinds * (q + 1)]
-        return 0
-
-    lax.fori_loop(0, tiles // step, body, 0)
+                item, before = item_s[0, base + j], item_s[0, jnp.maximum(base + j - 1, 0)]
+                run = jnp.where(item == before, 1.0, 0.0) * run + out[kinds * q : kinds * (q + 1)]
+                p = slot_of(item, me, item_dev, n_grp, n_user)
+                acc[pl.ds(pl.multiple_of(p * pitch, 8), kinds), :] = run
+        return run
+
+    lax.fori_loop(0, tiles // step, body, jnp.zeros((kinds, low_part), f32))
     copies[4].wait()
+    copies[5].wait()
     per = num_items // n_grp
     wide = 128 // low_part
 
     def row(h):
-        parts = [acc[pl.ds(h * wide + n, num_items, stride=kinds), :] for n in range(wide)]
+        parts = [acc[pl.ds(h * wide + n, num_items, stride=pitch), :] for n in range(wide)]
         return jnp.concatenate(parts, 1)
 
     for h in range(block_users // 128):
@@ -132,28 +136,30 @@
         eouts[k][:, block_users + 128 :] = rl[k * per : (k + 1) * per]
 
 
-def histogram(me, valid, item, users, counts, u, num_items, item_dev, n_grp, n_user):
+def histogram(me, valid, item, users, counts, u, prev, num_items, item_dev, n_grp, n_user):
     block_users, rank = u.shape
-    step, low_part = 128, 64
+    step, low_part = 192, 64
+    assert users.shape[1] % step == 0
     return pl.pallas_call(
         functools.partial(histogram_kernel, step, low_part, item_dev, n_grp, n_user),
-        in_specs=[SMEM] + [pl.BlockSpec(memory_space=pltpu.HBM)] * 5,
-        out_specs=[VMEM] * (n_grp + 2),
+        in_specs=[SMEM] + [pl.BlockSpec(memory_space=pltpu.HBM)] * 6,
+        out_specs=[VMEM] * (n_grp + 3),
         out_shape=[struct((num_items // n_grp, block_users + 2 * rank), bf16)] * n_grp
-        + [struct((num_items, block_users), bf16)] * 2,
+        + [struct((num_items, block_users), bf16)] * 2
+        + [struct(prev.shape, f32)],
         scratch_shapes=[
-            pltpu.VMEM((num_items * 2 * block_users // low_part, low_part), f32),
+            pltpu.VMEM((num_items * (2 * block_users // low_part + 8), low_part), f32),
             pltpu.SMEM(valid.shape, i32),
             pltpu.SMEM(item.shape, i32),
             pltpu.VMEM(users.shape, i32),
             pltpu.VMEM(counts.shape, i32),
             pltpu.VMEM(u.shape, bf16),
-            pltpu.SemaphoreType.DMA((5,)),
+            pltpu.SemaphoreType.DMA((6,)),
         ],
         compiler_params=params(32),
         cost_estimate=cost(7),
         name="histogram",
-    )(me, *[pltpu.with_memory_space_constraint(v, pltpu.HBM) for v in (valid, item, users, counts, u)])
+    )(me, *[pltpu.with_memory_space_constraint(v, pltpu.HBM) for v in (valid, item, users, counts, u, prev)])
 
 
 def transpose_kernel(*refs):
@@ -324,9 +330,7 @@
 
 
 def gradients_kernel(item_dev, own, *refs):
-    *got, prev_far, out, half, prev, sem = refs
-    fetch = pltpu.make_async_copy(prev_far, prev, sem)
-    fetch.start()
+    *got, prev, out, half = refs
     value = own[0]
     for g in got:
         value = value + (g[...] if len(g.shape) == 2 else g[0]).astype(f32)
@@ -354,7 +358,6 @@
             rows.append(jnp.sum(jnp.where(eye, s, 0.0), axis=0, keepdims=True))
         return jnp.concatenate(rows, 0)
 
-    fetch.wait()
     solution = prev[...]
     residual = side - apply(solution)
     direction = residual
@@ -377,14 +380,13 @@
     item_dev, rank = prev.shape
     return pl.pallas_call(
         functools.partial(gradients_kernel, item_dev),
-        in_specs=[VMEM] * (1 + len(got)) + [pl.BlockSpec(memory_space=pltpu.HBM)],
+        in_specs=[VMEM] * (2 + len(got)),
         out_specs=[VMEM] * 2,
         out_shape=[struct(prev.shape, f32), struct((devices,) + prev.shape, bf16)],
-        scratch_shapes=[pltpu.VMEM(prev.shape, f32), pltpu.SemaphoreType.DMA(())],
         compiler_params=params(16),
         cost_estimate=cost(2),
         name="gradients",
-    )(own, *got, pltpu.with_memory_space_constraint(prev, pltpu.HBM))
+    )(own, *got, prev)
 
 
 def user_side_kernel(item_dev, n_grp, n_user, me_s, returned, c_hi, c_lo, out, rows, order, made, sem):
@@ -457,8 +459,8 @@
     u0 = user_factors
     u2 = swap(u0, 2)
     u1 = swap(u0, 1)
-    *es, c_hi, c_lo = histogram(
-        me, tile_valid, tile_item, tile_user, tile_count, u0, num_items, item_dev, n_grp, n_user
+    *es, c_hi, c_lo, prev = histogram(
+        me, tile_valid, tile_item, tile_user, tile_count, u0, prev_items, num_items, item_dev, n_grp, n_user
     )
     u2, es[0] = lax.optimization_barrier((u2, es[0]))
     u3 = swap(u2, 1)
@@ -502,7 +504,7 @@
     c_hi, c_lo, own, *parts[:2] = lax.optimization_barrier((c_hi, c_lo, own, *parts[:2]))
     c_hi, c_lo = flipped(c_hi, c_lo)
     own, c_hi = lax.optimization_barrier((own, c_hi))
-    solved, spread = gradients(own, parts, prev_items, devices)
+    solved, spread = gradients(own, parts, prev, devices)
     returned = lax.all_to_all(spread, AXES, 0, 0, tiled=True).reshape(num_items, rank)
     return solved, user_side(me, returned, c_hi, c_lo, item_dev, n_grp, n_user)
 

time: 48.5 us -> 47 us (0.969)
  Pallas kernels: 20.3 us -> 18.8 us
    pallas_call x1, Pallas kernels: 5.85 us -> 4.94 us  [histogram(): pl.pallas_call(functools.partial(histogram_kernel, step, low_part, item_d...]
    pallas_call x1, Pallas kernels: 2.7 us -> 2.08 us  [gradients(): pl.pallas_call(functools.partial(gradients_kernel, item_dev), in_specs=[V...]
  transfers between devices with their start and end apart: 11 -> 11, of which waited for: 5 -> 6; matrix products, arithmetic and copies ran while one was open for 0% -> 0% of each run, Pallas kernels for 32% -> 31%
where the time goes in v5:
time: 47 us; the launch traced here: 46.8 us
  Pallas kernels  18.8 us (40%)
  starting transfers between devices  11.7 us (25%)
  blocking collectives  11.2 us (24%)
  waiting for transfers between devices  4.36 us (9%)
  between operations  0.74 us (2%)
    ppermute x11, starting transfers between devices, swap(): return lax.ppermute(value, AXES, [(d, d ^ bit) for d in range(devices)])  11.7 us
    all_to_all x1, blocking collectives, shards(): lax.all_to_all(spread, AXES, 0, 0, tiled=True).reshape(num_items, rank)  11.2 us
    pallas_call x5, Pallas kernels, systems(): pl.pallas_call(functools.partial(systems_kernel, first, n_items, item_dev...  7.66 us
    pallas_call x1, Pallas kernels, histogram(): pl.pallas_call(functools.partial(histogram_kernel, step, low_part, item_d...  4.94 us
    ppermute x11, waiting for transfers between devices, swap(): return lax.ppermute(value, AXES, [(d, d ^ bit) for d in range(devices)])  4.36 us
    pallas_call x1, Pallas kernels, begun(): pl.pallas_call(functools.partial(begun_kernel, first, n_items, item_dev,...  2.32 us
    pallas_call x1, Pallas kernels, gradients(): pl.pallas_call(functools.partial(gradients_kernel, item_dev), in_specs=[V...  2.08 us
    pallas_call x1, Pallas kernels, user_side(): pl.pallas_call(functools.partial(user_side_kernel, item_dev, n_grp, n_use...  1.06 us
  transfers between devices with their start and end apart: 11, of which 6 were waited for; matrix products, arithmetic and copies ran while one was open for 0% of the time, Pallas kernels for 31%

profile of v5, /device:TPU:0, one launch (start us, length us, event | category | flops | bytes accessed | tf_op | source)
XLA Modules:
  0.0 46.8 jit_solution(15105184758084736277)
XLA Ops:
  0.6 0.5 %collective-permute-start.4 = (bf16[1024,128]{1,0:T(8,128)(2,1)}, bf16[1024,128]{1,0:T(8,128)(2,1)S(1)}, u32[]{:S(2)}, u32[]{:S(2)}) collective-permute-start(bf16[1024,128]{1,0:T(8,128)(2,1)} %refs_4_.7), channel_id=1, source_target_pairs={{0,1},{1,0},{2,3},{3,2},{4,5},{5,4},{6,7},{7,6},{8,9},{9,8},{10,11... | collective-permute-start | bytes 786440 | tf_op jit(solution)/shard_map/ppermute | solution.py:457
  1.1 2.6 %collective-permute-start = (bf16[1024,128]{1,0:T(8,128)(2,1)}, bf16[1024,128]{1,0:T(8,128)(2,1)S(1)}, u32[]{:S(2)}, u32[]{:S(2)}) collective-permute-start(bf16[1024,128]{1,0:T(8,128)(2,1)} %refs_4_.7), channel_id=1, source_target_pairs={{0,2},{1,3},{2,0},{3,1},{4,6},{5,7},{6,4},{7,5},{8,10},{9,11},{10,... | collective-permute-start | bytes 786440 | tf_op jit(solution)/shard_map/ppermute | solution.py:457
  3.7 0.0 copy-start
  3.7 4.9 %histogram.1 = (bf16[32,1280]{1,0:T(8,128)(2,1)S(1)}, bf16[32,1280]{1,0:T(8,128)(2,1)S(1)}, bf16[32,1280]{1,0:T(8,128)(2,1)S(1)}, bf16[32,1280]{1,0:T(8,128)(2,1...) custom-call(s32[1]{0:T(128)} %bitcast.me_s, s32[1,384]{1,0:T(1,128)} %refs_0_.3, ...), custom_call_target="tpu_custom_call" | custom-call | flops 7000000000 | bytes 21000000 | tf_op jit(solution)/shard_map/histogram/pallas_call | solution.py:143
  8.7 0.2 collective-permute-start.1
  8.9 0.3 collective-permute-start.2
  9.2 1.4 %collective-permute-start.3 = (bf16[32,1280]{1,0:T(8,128)(2,1)S(1)}, bf16[32,1280]{1,0:T(8,128)(2,1)S(1)}, u32[]{:S(2)}, u32[]{:S(2)}) collective-permute-start(bf16[32,1280]{1,0:T(8,128)(2,1)S(1)} %get-tuple-element.34), channel_id=1, source_target_pairs={{0,3},{1,2},{2,1},{3,0},{4,7},{5,6},{6,5},{7,4},{8,11},{9,10},{10,... | collective-permute-start | bytes 245768 | tf_op jit(solution)/shard_map/ppermute | solution.py:457
  10.6 0.2 collective-permute-done.refs_2_.refs_4_.refs_6_
  10.9 0.2 collective-permute-start.5
  11.1 0.0 collective-permute-done.4.refs_1_.refs_3_.refs_5_
  11.1 0.0 copy-done
  11.1 0.2 transpose.3.refs_4_
  11.3 0.0 collective-permute-done.1.refs_1_
  11.3 2.3 %begun.1.refs_7_ = f32[4,512,128]{2,1,0:T(8,128)S(1)} custom-call(bf16[32,1280]{1,0:T(8,128)(2,1)S(1)} %get-tuple-element.31.refs_0_, bf16[32,1280]{1,0:T(8,128)(2,1)S(1)} %collective-permute-done.1.refs_1_, bf16[1024,128]{1,0:T(8,128)(2,1)S(1)} %copy-done, bf16[1024,128]{1,0:T(8,128)(2,1)S(1)} %collective-permute-done.4.refs_1_.refs_3_.refs_5_, ...), custom_call_target="tpu_custom_call" | custom-call | flops 2600000000 | bytes 7800000 | tf_op jit(solution)/shard_map/begun/pallas_call | solution.py:217
  13.6 0.0 collective-permute-done.5.refs_3_.refs_5_.refs_7_
  13.6 0.3 transpose.2.refs_6_.refs_8_
  14.0 0.2 collective-permute-done.2.refs_2_
  14.2 0.6 %collective-permute-done.3.refs_3_ = bf16[32,1280]{1,0:T(8,128)(2,1)S(1)} collective-permute-done((bf16[32,1280]{1,0:T(8,128)(2,1)S(1)}, bf16[32,1280]{1,0:T(8,128)(2,1)S(1)}, u32[]{:S(2)}, u32[]{:S(2)}) %collective-permute-start.3) | collective-permute-done | bytes 81952 | tf_op jit(solution)/shard_map/ppermute | solution.py:457
  14.8 1.3 %systems.5 = bf16[2,272,128]{2,1,0:T(8,128)(2,1)S(1)} custom-call(bf16[32,1280]{1,0:T(8,128)(2,1)S(1)} %get-tuple-element.31.refs_0_, bf16[32,1280]{1,0:T(8,128)(2,1)S(1)} %collective-permute-done.1.refs_1_, bf16[32,1280]{1,0:T(8,128)(2,1)S(1)} %collective-permute-done.2.refs_2_, bf16[32,1280]{1,0:T(8,128)(2,1)S(1)} %collective-permute-done.3.refs_3_, ...), custom_call_target="tpu_custom_call" | custom-call | flops 1312000000 | bytes 3936000 | tf_op jit(solution)/shard_map/systems/pallas_call | solution.py:281
  16.1 1.6 %collective-permute-start.6 = (bf16[2,272,128]{2,1,0:T(8,128)(2,1)S(1)}, bf16[2,272,128]{2,1,0:T(8,128)(2,1)S(1)}, u32[]{:S(2)}, u32[]{:S(2)}) collective-permute-start(bf16[2,272,128]{2,1,0:T(8,128)(2,1)S(1)} %systems.5), channel_id=1, source_target_pairs={{0,4},{1,5},{2,6},{3,7},{4,0},{5,1},{6,2},{7,3},{8,12},{9,13},{10,... | collective-permute-start | bytes 417800 | tf_op jit(solution)/shard_map/ppermute | solution.py:457
  17.7 1.3 %systems.6 = bf16[2,272,128]{2,1,0:T(8,128)(2,1)S(1)} custom-call(bf16[32,1280]{1,0:T(8,128)(2,1)S(1)} %get-tuple-element.31.refs_0_, bf16[32,1280]{1,0:T(8,128)(2,1)S(1)} %collective-permute-done.1.refs_1_, bf16[32,1280]{1,0:T(8,128)(2,1)S(1)} %collective-permute-done.2.refs_2_, bf16[32,1280]{1,0:T(8,128)(2,1)S(1)} %collective-permute-done.3.refs_3_, ...), custom_call_target="tpu_custom_call" | custom-call | flops 1312000000 | bytes 3936000 | tf_op jit(solution)/shard_map/systems/pallas_call | solution.py:281
  19.0 0.6 %collective-permute-start.9 = (bf16[2,272,128]{2,1,0:T(8,128)(2,1)S(1)}, bf16[2,272,128]{2,1,0:T(8,128)(2,1)S(1)}, u32[]{:S(2)}, u32[]{:S(2)}) collective-permute-start(bf16[2,272,128]{2,1,0:T(8,128)(2,1)S(1)} %systems.6), channel_id=1, source_target_pairs={{0,4},{1,5},{2,6},{3,7},{4,0},{5,1},{6,2},{7,3},{8,12},{9,13},{10,... | collective-permute-start | bytes 417800 | tf_op jit(solution)/shard_map/ppermute | solution.py:457
  19.6 2.4 %systems.7.own = f32[2,272,128]{2,1,0:T(8,128)S(1)} custom-call(bf16[32,1280]{1,0:T(8,128)(2,1)S(1)} %get-tuple-element.31.refs_0_, bf16[32,1280]{1,0:T(8,128)(2,1)S(1)} %collective-permute-done.1.refs_1_, bf16[32,1280]{1,0:T(8,128)(2,1)S(1)} %collective-permute-done.2.refs_2_, bf16[32,1280]{1,0:T(8,128)(2,1)S(1)} %collective-permute-done.3.refs_3_, ...), custom_call_target="tpu_custom_call" | custom-call | flops 10000000 | bytes 30000 | tf_op jit(solution)/shard_map/systems/pallas_call | solution.py:281
  22.0 0.5 %collective-permute-done.6.got = bf16[2,272,128]{2,1,0:T(8,128)(2,1)S(1)} collective-permute-done((bf16[2,272,128]{2,1,0:T(8,128)(2,1)S(1)}, bf16[2,272,128]{2,1,0:T(8,128)(2,1)S(1)}, u32[]{:S(2)}, u32[]{:S(2)}) %collective-permute-start.6) | collective-permute-done | bytes 139296 | tf_op jit(solution)/shard_map/ppermute | solution.py:457
  22.5 2.6 %collective-permute-start.8 = (bf16[272,128]{1,0:T(8,128)(2,1)S(1)}, bf16[272,128]{1,0:T(8,128)(2,1)S(1)}, u32[]{:S(2)}, u32[]{:S(2)}) collective-permute-start(bf16[272,128]{1,0:T(8,128)(2,1)S(1)} %get-tuple-element.38), channel_id=1, source_target_pairs={{0,16},{1,17},{2,18},{3,19},{4,20},{5,21},{6,22},{7,23},{8,24},{9,... | collective-permute-start | bytes 208904 | tf_op jit(solution)/shard_map/ppermute | solution.py:457
  25.2 1.3 %collective-permute-start.7 = (bf16[272,128]{1,0:T(8,128)(2,1)S(1)}, bf16[272,128]{1,0:T(8,128)(2,1)S(1)}, u32[]{:S(2)}, u32[]{:S(2)}) collective-permute-start(bf16[272,128]{1,0:T(8,128)(2,1)S(1)} %get-tuple-element.41), channel_id=1, source_target_pairs={{0,24},{1,25},{2,26},{3,27},{4,28},{5,29},{6,30},{7,31},{8,16},{9,... | collective-permute-start | bytes 208904 | tf_op jit(solution)/shard_map/ppermute | solution.py:457
  26.5 1.3 %systems.8.own = f32[1,272,128]{2,1,0:T(8,128)S(1)} custom-call(bf16[32,1280]{1,0:T(8,128)(2,1)S(1)} %get-tuple-element.31.refs_0_, bf16[32,1280]{1,0:T(8,128)(2,1)S(1)} %collective-permute-done.1.refs_1_, bf16[32,1280]{1,0:T(8,128)(2,1)S(1)} %collective-permute-done.2.refs_2_, bf16[32,1280]{1,0:T(8,128)(2,1)S(1)} %collective-permute-done.3.refs_3_, ...), custom_call_target="tpu_custom_call" | custom-call | flops 1312000000 | bytes 3936000 | tf_op jit(solution)/shard_map/systems/pallas_call | solution.py:281
  27.8 0.0 collective-permute-done.9.got.refs_3_
  27.8 0.3 collective-permute-start.10
  28.2 1.3 %systems.9.own = f32[1,272,128]{2,1,0:T(8,128)S(1)} custom-call(bf16[32,1280]{1,0:T(8,128)(2,1)S(1)} %get-tuple-element.31.refs_0_, bf16[32,1280]{1,0:T(8,128)(2,1)S(1)} %collective-permute-done.1.refs_1_, bf16[32,1280]{1,0:T(8,128)(2,1)S(1)} %collective-permute-done.2.refs_2_, bf16[32,1280]{1,0:T(8,128)(2,1)S(1)} %collective-permute-done.3.refs_3_, ...), custom_call_target="tpu_custom_call" | custom-call | flops 1312000000 | bytes 3936000 | tf_op jit(solution)/shard_map/systems/pallas_call | solution.py:281
  29.5 2.6 %collective-permute-done.7.refs_0_ = bf16[272,128]{1,0:T(8,128)(2,1)S(1)} collective-permute-done((bf16[272,128]{1,0:T(8,128)(2,1)S(1)}, bf16[272,128]{1,0:T(8,128)(2,1)S(1)}, u32[]{:S(2)}, u32[]{:S(2)}) %collective-permute-start.7) | collective-permute-done | bytes 69664 | tf_op jit(solution)/shard_map/ppermute | solution.py:457
  32.1 0.0 collective-permute-done.8.refs_1_
  32.1 0.2 flip.1
  32.3 0.2 collective-permute-done.10.refs_2_
  32.5 2.1 %gradients.1 = (f32[4,128]{1,0:T(4,128)}, bf16[32,4,128]{2,1,0:T(4,128)(2,1)S(1)}) custom-call(f32[1,272,128]{2,1,0:T(8,128)S(1)} %systems.9.own, bf16[272,128]{1,0:T(8,128)(2,1)S(1)} %collective-permute-done.7.refs_0_, bf16[272,128]{1,0:T(8,128)(2,1)S(1)} %collective-permute-done.8.refs_1_, bf16[272,128]{1,0:T(8,128)(2,1)S(1)} %collective-permute-done.10.refs_2_, ...), custom_call_target="tpu_custom_call" | custom-call | flops 2000000000 | bytes 6000000 | tf_op jit(solution)/shard_map/gradients/pallas_call | solution.py:381
  34.6 11.2 %all_to_all.5 = bf16[32,4,128]{2,1,0:T(4,128)(2,1)S(1)} all-to-all(bf16[32,4,128]{2,1,0:T(4,128)(2,1)S(1)} %get-tuple-element.51), channel_id=1, replica_groups=mesh['user'=8,'grp'=4] {'user','grp'}, dimensions={0} | all-to-all | bytes 65536 | tf_op jit(solution)/shard_map/all_to_all | solution.py:508
  45.8 1.1 %user_side.1 = f32[1024,128]{1,0:T(8,128)} custom-call(s32[1]{0:T(128)} %bitcast.me_s, bf16[128,128]{1,0:T(8,128)(2,1)S(1)} %bitcast.2, bf16[1024,128]{1,0:T(8,128)(2,1)S(1)} %get-tuple-element.52.c_hi, bf16[1024,128]{1,0:T(8,128)(2,1)S(1)} %get-tuple-element.53.c_lo), custom_call_target="tpu_custom_call" | custom-call | flops 1000000000 | bytes 3000000 | tf_op jit(solution)/shard_map/user_side/pallas_call | solution.py:415
  (2 shorter events, 0.1 us)
Async XLA Ops:
  0.6 10.5 %collective-permute-start.4 = (bf16[1024,128]{1,0:T(8,128)(2,1)}, bf16[1024,128]{1,0:T(8,128)(2,1)S(1)}, u32[]{:S(2)}, u32[]{:S(2)}) collective-permute-start(bf16[1024,128]{1,0:T(8,128)(2,1)} %refs_4_.7), channel_id=1, source_target_pairs={{0,1},{1,0},{2,3},{3,2},{4,5},{5,4},{6,7},{7,6},{8,9},{9,8},{10,11... | collective-permute-start | bytes 786440 | tf_op jit(solution)/shard_map/ppermute | solution.py:457
  1.1 9.7 %collective-permute-start = (bf16[1024,128]{1,0:T(8,128)(2,1)}, bf16[1024,128]{1,0:T(8,128)(2,1)S(1)}, u32[]{:S(2)}, u32[]{:S(2)}) collective-permute-start(bf16[1024,128]{1,0:T(8,128)(2,1)} %refs_4_.7), channel_id=1, source_target_pairs={{0,2},{1,3},{2,0},{3,1},{4,6},{5,7},{6,4},{7,5},{8,10},{9,11},{10,... | collective-permute-start | bytes 786440 | tf_op jit(solution)/shard_map/ppermute | solution.py:457
  3.7 7.4 %copy-start = (bf16[1024,128]{1,0:T(8,128)(2,1)S(1)}, bf16[1024,128]{1,0:T(8,128)(2,1)}, u32[]{:S(2)}) copy-start(bf16[1024,128]{1,0:T(8,128)(2,1)} %refs_4_.7) | copy-start | bytes 786436
  8.7 2.6 %collective-permute-start.1 = (bf16[32,1280]{1,0:T(8,128)(2,1)S(1)}, bf16[32,1280]{1,0:T(8,128)(2,1)S(1)}, u32[]{:S(2)}, u32[]{:S(2)}) collective-permute-start(bf16[32,1280]{1,0:T(8,128)(2,1)S(1)} %get-tuple-element.32), channel_id=1, source_target_pairs={{0,1},{1,0},{2,3},{3,2},{4,5},{5,4},{6,7},{7,6},{8,9},{9,8},{10,11... | collective-permute-start | bytes 245768 | tf_op jit(solution)/shard_map/ppermute | solution.py:457
  8.9 5.3 %collective-permute-start.2 = (bf16[32,1280]{1,0:T(8,128)(2,1)S(1)}, bf16[32,1280]{1,0:T(8,128)(2,1)S(1)}, u32[]{:S(2)}, u32[]{:S(2)}) collective-permute-start(bf16[32,1280]{1,0:T(8,128)(2,1)S(1)} %get-tuple-element.33), channel_id=1, source_target_pairs={{0,2},{1,3},{2,0},{3,1},{4,6},{5,7},{6,4},{7,5},{8,10},{9,11},{10,... | collective-permute-start | bytes 245768 | tf_op jit(solution)/shard_map/ppermute | solution.py:457
  9.2 5.6 %collective-permute-start.3 = (bf16[32,1280]{1,0:T(8,128)(2,1)S(1)}, bf16[32,1280]{1,0:T(8,128)(2,1)S(1)}, u32[]{:S(2)}, u32[]{:S(2)}) collective-permute-start(bf16[32,1280]{1,0:T(8,128)(2,1)S(1)} %get-tuple-element.34), channel_id=1, source_target_pairs={{0,3},{1,2},{2,1},{3,0},{4,7},{5,6},{6,5},{7,4},{8,11},{9,10},{10,... | collective-permute-start | bytes 245768 | tf_op jit(solution)/shard_map/ppermute | solution.py:457
  10.9 2.8 %collective-permute-start.5 = (bf16[1024,128]{1,0:T(8,128)(2,1)S(1)}, bf16[1024,128]{1,0:T(8,128)(2,1)S(1)}, u32[]{:S(2)}, u32[]{:S(2)}) collective-permute-start(bf16[1024,128]{1,0:T(8,128)(2,1)S(1)} %collective-permute-done.refs_2_.refs_4_.refs_6_), channel_id=1, source_target_pairs={{0,1},{1,0},{2,3},{3,2},{4,5},{5,4},{6,7},{7,6},{8,9},{9,8},{10,11... | collective-permute-start | bytes 786440 | tf_op jit(solution)/shard_map/ppermute | solution.py:457
  16.1 6.4 %collective-permute-start.6 = (bf16[2,272,128]{2,1,0:T(8,128)(2,1)S(1)}, bf16[2,272,128]{2,1,0:T(8,128)(2,1)S(1)}, u32[]{:S(2)}, u32[]{:S(2)}) collective-permute-start(bf16[2,272,128]{2,1,0:T(8,128)(2,1)S(1)} %systems.5), channel_id=1, source_target_pairs={{0,4},{1,5},{2,6},{3,7},{4,0},{5,1},{6,2},{7,3},{8,12},{9,13},{10,... | collective-permute-start | bytes 417800 | tf_op jit(solution)/shard_map/ppermute | solution.py:457
  19.0 8.8 %collective-permute-start.9 = (bf16[2,272,128]{2,1,0:T(8,128)(2,1)S(1)}, bf16[2,272,128]{2,1,0:T(8,128)(2,1)S(1)}, u32[]{:S(2)}, u32[]{:S(2)}) collective-permute-start(bf16[2,272,128]{2,1,0:T(8,128)(2,1)S(1)} %systems.6), channel_id=1, source_target_pairs={{0,4},{1,5},{2,6},{3,7},{4,0},{5,1},{6,2},{7,3},{8,12},{9,13},{10,... | collective-permute-start | bytes 417800 | tf_op jit(solution)/shard_map/ppermute | solution.py:457
  22.5 9.6 %collective-permute-start.8 = (bf16[272,128]{1,0:T(8,128)(2,1)S(1)}, bf16[272,128]{1,0:T(8,128)(2,1)S(1)}, u32[]{:S(2)}, u32[]{:S(2)}) collective-permute-start(bf16[272,128]{1,0:T(8,128)(2,1)S(1)} %get-tuple-element.38), channel_id=1, source_target_pairs={{0,16},{1,17},{2,18},{3,19},{4,20},{5,21},{6,22},{7,23},{8,24},{9,... | collective-permute-start | bytes 208904 | tf_op jit(solution)/shard_map/ppermute | solution.py:457
  25.2 6.9 %collective-permute-start.7 = (bf16[272,128]{1,0:T(8,128)(2,1)S(1)}, bf16[272,128]{1,0:T(8,128)(2,1)S(1)}, u32[]{:S(2)}, u32[]{:S(2)}) collective-permute-start(bf16[272,128]{1,0:T(8,128)(2,1)S(1)} %get-tuple-element.41), channel_id=1, source_target_pairs={{0,24},{1,25},{2,26},{3,27},{4,28},{5,29},{6,30},{7,31},{8,16},{9,... | collective-permute-start | bytes 208904 | tf_op jit(solution)/shard_map/ppermute | solution.py:457
  27.8 4.6 %collective-permute-start.10 = (bf16[272,128]{1,0:T(8,128)(2,1)S(1)}, bf16[272,128]{1,0:T(8,128)(2,1)S(1)}, u32[]{:S(2)}, u32[]{:S(2)}) collective-permute-start(bf16[272,128]{1,0:T(8,128)(2,1)S(1)} %merge.3), channel_id=1, source_target_pairs={{0,8},{1,9},{2,10},{3,11},{4,12},{5,13},{6,14},{7,15},{8,0},{9,1},... | collective-permute-start | bytes 208904 | tf_op jit(solution)/shard_map/ppermute | solution.py:457

commit v6 on v5

--- a/solution.py
+++ b/solution.py
@@ -204,25 +204,28 @@
     return ref[low:high, cols].astype(f32)[first - low : first - low + n]
 
 
-def begun_kernel(first, n_items, item_dev, n, *refs):
-    es, us, ut, out = refs[:n], refs[n : 2 * n], refs[2 * n], refs[2 * n + 1]
+def begun_kernel(first, n_items, item_dev, n, skip, at, *refs):
+    es, us, ut, out = refs[:n], refs[n : 2 * n], refs[2 * n], refs[-1]
+    more = refs[2 * n + 1 : -1]
     rows = [some_rows(e, first, n_items, slice(0, us[0].shape[0])) for e in es]
     for c in range(n_items // item_dev):
-        out[c] = partial_systems(rows, ut, us, c, item_dev, 0)
-
-
-def begun(es, us, ut, first, n_items, item_dev):
+        total = partial_systems(rows, ut, us, c, item_dev, skip * us[0].shape[0])
+        out[c] = total + more[0][at + c] if more else total
+
+
+def begun(es, us, ut, first, n_items, item_dev, start=None, skip=0, at=0):
+    more = [] if start is None else [start]
     n = len(es)
     block_users, rank = us[0].shape
     return pl.pallas_call(
-        functools.partial(begun_kernel, first, n_items, item_dev, n),
-        in_specs=[VMEM] * (2 * n + 1),
+        functools.partial(begun_kernel, first, n_items, item_dev, n, skip, at),
+        in_specs=[VMEM] * (2 * n + 1 + len(more)),
         out_specs=VMEM,
         out_shape=struct((n_items // item_dev, item_dev * rank, rank), f32),
         compiler_params=params(32),
-        cost_estimate=cost(2.6),
+        cost_estimate=cost(0.082 * n * n_items),
         name="begun",
-    )(*es, *us, ut)
+    )(*es, *us, ut, *more)
 
 
 def systems_kernel(first, n_items, item_dev, keep, n, done, at, *refs):
@@ -351,24 +354,33 @@
         )
         matrices.append(jnp.where(eye, diag[j : j + 1] + ridge_weight, full))
 
-    def apply(vector):
-        rows = []
-        for j in range(item_dev):
-            s = jnp.sum(matrices[j] * vector[j : j + 1], axis=1, keepdims=True)
-            rows.append(jnp.sum(jnp.where(eye, s, 0.0), axis=0, keepdims=True))
-        return jnp.concatenate(rows, 0)
-
     solution = prev[...]
-    residual = side - apply(solution)
-    direction = residual
+    residual_c = [
+        jnp.sum(jnp.where(eye, side[j : j + 1], 0.0) - matrices[j] * solution[j : j + 1], axis=1, keepdims=True)
+        for j in range(item_dev)
+    ]
+    residual = jnp.concatenate(
+        [jnp.sum(jnp.where(eye, c, 0.0), axis=0, keepdims=True) for c in residual_c], 0
+    )
+    direction, direction_c = residual, residual_c
     norm_now = jnp.sum(residual * residual, axis=1, keepdims=True)
-    for _ in range(CG_STEPS):
-        image = apply(direction)
+    for turn in range(CG_STEPS):
+        image = jnp.concatenate(
+            [jnp.sum(m * c, axis=0, keepdims=True) for m, c in zip(matrices, direction_c)], 0
+        )
         step = norm_now / jnp.sum(direction * image, axis=1, keepdims=True)
         solution = solution + step * direction
+        if turn == CG_STEPS - 1:
+            break
         residual = residual - step * image
         norm_next = jnp.sum(residual * residual, axis=1, keepdims=True)
-        direction = residual + norm_next / norm_now * direction
+        again = norm_next / norm_now
+        image_c = [
+            jnp.sum(matrices[j] * direction[j : j + 1], axis=1, keepdims=True) for j in range(item_dev)
+        ]
+        residual_c = [c - step[j : j + 1] * i for j, (c, i) in enumerate(zip(residual_c, image_c))]
+        direction_c = [c + again[j : j + 1] * d for j, (c, d) in enumerate(zip(residual_c, direction_c))]
+        direction = residual + again * direction
         norm_now = norm_next
     out[...] = solution
     short = solution.astype(bf16)
@@ -473,7 +485,8 @@
     if n_user == 8:
         n_far = n_half // 2
         chunks = n_far // item_dev
-        sent = systems(got, us, ut, n_half + n_far, n_far, item_dev, False, start, 2, chunks)
+        first = begun(got[2:3], us[2:3], ut, n_half + n_far, n_far, item_dev, start, 2, chunks)
+        sent = systems(got, us, ut, n_half + n_far, n_far, item_dev, False, first, 3, 0)
         far_other = swap(sent, n_grp)
         ut, _ = lax.optimization_barrier((ut, sent))
         sent = systems(got, us, ut, n_half, n_far, item_dev, False, start, 2, 0)

time: 47 us -> 46.8 us (level)
  waiting for transfers between devices: 4.36 us -> 3.64 us
  blocking collectives: 11.2 us -> 11.9 us
    ppermute x11, waiting for transfers between devices: 4.36 us -> 3.64 us  [swap(): return lax.ppermute(value, AXES, [(d, d ^ bit) for d in range(devices)])]
    pallas_call x1 -> x2, Pallas kernels: 2.32 us -> 3.02 us  [begun(): pl.pallas_call(functools.partial(begun_kernel, first, n_items, item_dev,...]
    all_to_all x1, blocking collectives: 11.2 us -> 11.9 us  [shards(): lax.all_to_all(spread, AXES, 0, 0, tiled=True).reshape(num_items, rank)]
    pallas_call x5, Pallas kernels: 7.66 us -> 7.12 us  [systems(): pl.pallas_call(functools.partial(systems_kernel, first, n_items, item_dev...]
  transfers between devices with their start and end apart: 11 -> 11, of which waited for: 6 -> 5; matrix products, arithmetic and copies ran while one was open for 0% -> 0% of each run, Pallas kernels for 31% -> 32%
where the time goes in v6:
time: 46.8 us; the launch traced here: 46.6 us
  Pallas kernels  18.6 us (40%)
  blocking collectives  11.9 us (25%)
  starting transfers between devices  11.7 us (25%)
  waiting for transfers between devices  3.64 us (8%)
  between operations  0.75 us (2%)
    all_to_all x1, blocking collectives, shards(): lax.all_to_all(spread, AXES, 0, 0, tiled=True).reshape(num_items, rank)  11.9 us
    ppermute x11, starting transfers between devices, swap(): return lax.ppermute(value, AXES, [(d, d ^ bit) for d in range(devices)])  11.7 us
    pallas_call x5, Pallas kernels, systems(): pl.pallas_call(functools.partial(systems_kernel, first, n_items, item_dev...  7.12 us
    pallas_call x1, Pallas kernels, histogram(): pl.pallas_call(functools.partial(histogram_kernel, step, low_part, item_d...  4.94 us
    ppermute x11, waiting for transfers between devices, swap(): return lax.ppermute(value, AXES, [(d, d ^ bit) for d in range(devices)])  3.64 us
    pallas_call x2, Pallas kernels, begun(): pl.pallas_call(functools.partial(begun_kernel, first, n_items, item_dev,...  3.02 us
    pallas_call x1, Pallas kernels, gradients(): pl.pallas_call(functools.partial(gradients_kernel, item_dev), in_specs=[V...  1.65 us
    pallas_call x1, Pallas kernels, user_side(): pl.pallas_call(functools.partial(user_side_kernel, item_dev, n_grp, n_use...  1.06 us
  transfers between devices with their start and end apart: 11, of which 5 were waited for; matrix products, arithmetic and copies ran while one was open for 0% of the time, Pallas kernels for 32%

profile of v6, /device:TPU:0, one launch (start us, length us, event | category | flops | bytes accessed | tf_op | source)
XLA Modules:
  0.0 46.6 jit_solution(4507643100057055910)
XLA Ops:
  0.6 0.5 %collective-permute-start.4 = (bf16[1024,128]{1,0:T(8,128)(2,1)}, bf16[1024,128]{1,0:T(8,128)(2,1)S(1)}, u32[]{:S(2)}, u32[]{:S(2)}) collective-permute-start(bf16[1024,128]{1,0:T(8,128)(2,1)} %refs_4_.7), channel_id=1, source_target_pairs={{0,1},{1,0},{2,3},{3,2},{4,5},{5,4},{6,7},{7,6},{8,9},{9,8},{10,11... | collective-permute-start | bytes 786440 | tf_op jit(solution)/shard_map/ppermute | solution.py:469
  1.1 2.6 %collective-permute-start = (bf16[1024,128]{1,0:T(8,128)(2,1)}, bf16[1024,128]{1,0:T(8,128)(2,1)S(1)}, u32[]{:S(2)}, u32[]{:S(2)}) collective-permute-start(bf16[1024,128]{1,0:T(8,128)(2,1)} %refs_4_.7), channel_id=1, source_target_pairs={{0,2},{1,3},{2,0},{3,1},{4,6},{5,7},{6,4},{7,5},{8,10},{9,11},{10,... | collective-permute-start | bytes 786440 | tf_op jit(solution)/shard_map/ppermute | solution.py:469
  3.7 0.0 copy-start
  3.7 4.9 %histogram.1 = (bf16[32,1280]{1,0:T(8,128)(2,1)S(1)}, bf16[32,1280]{1,0:T(8,128)(2,1)S(1)}, bf16[32,1280]{1,0:T(8,128)(2,1)S(1)}, bf16[32,1280]{1,0:T(8,128)(2,1...) custom-call(s32[1]{0:T(128)} %bitcast.me_s, s32[1,384]{1,0:T(1,128)} %refs_0_.3, ...), custom_call_target="tpu_custom_call" | custom-call | flops 7000000000 | bytes 21000000 | tf_op jit(solution)/shard_map/histogram/pallas_call | solution.py:143
  8.7 0.2 collective-permute-start.1
  8.9 0.3 collective-permute-start.2
  9.2 1.4 %collective-permute-start.3 = (bf16[32,1280]{1,0:T(8,128)(2,1)S(1)}, bf16[32,1280]{1,0:T(8,128)(2,1)S(1)}, u32[]{:S(2)}, u32[]{:S(2)}) collective-permute-start(bf16[32,1280]{1,0:T(8,128)(2,1)S(1)} %get-tuple-element.34), channel_id=1, source_target_pairs={{0,3},{1,2},{2,1},{3,0},{4,7},{5,6},{6,5},{7,4},{8,11},{9,10},{10,... | collective-permute-start | bytes 245768 | tf_op jit(solution)/shard_map/ppermute | solution.py:469
  10.6 0.2 collective-permute-done.refs_2_.refs_1_.refs_4_.refs_6_
  10.9 0.2 collective-permute-start.5
  11.1 0.0 collective-permute-done.4.refs_1_.refs_3_.refs_5_
  11.1 0.0 copy-done
  11.1 0.2 transpose.3.refs_4_
  11.3 0.0 collective-permute-done.1.refs_1_
  11.3 2.3 %begun.2.refs_3_.refs_7_ = f32[4,512,128]{2,1,0:T(8,128)S(1)} custom-call(bf16[32,1280]{1,0:T(8,128)(2,1)S(1)} %get-tuple-element.31.refs_0_, bf16[32,1280]{1,0:T(8,128)(2,1)S(1)} %collective-permute-done.1.refs_1_, bf16[1024,128]{1,0:T(8,128)(2,1)S(1)} %copy-done, bf16[1024,128]{1,0:T(8,128)(2,1)S(1)} %collective-permute-done.4.refs_1_.refs_3_.refs_5_, ...), custom_call_target="tpu_custom_call" | custom-call | flops 2624000000 | bytes 7872000 | tf_op jit(solution)/shard_map/begun/pallas_call | solution.py:220
  13.6 0.0 collective-permute-done.5.refs_3_.refs_4_.refs_5_.refs_7_
  13.6 0.3 transpose.2.refs_2_.refs_5_.refs_6_.refs_8_
  14.0 0.2 collective-permute-done.2.refs_0_.refs_2_
  14.2 0.7 %begun.3.refs_6_ = f32[2,512,128]{2,1,0:T(8,128)S(1)} custom-call(bf16[32,1280]{1,0:T(8,128)(2,1)S(1)} %collective-permute-done.2.refs_0_.refs_2_, bf16[1024,128]{1,0:T(8,128)(2,1)S(1)} %collective-permute-done.refs_2_.refs_1_.refs_4_.refs_6_, bf16[128,4096]{1,0:T(8,128)(2,1)S(1)} %transpose.2.refs_2_.refs_5_.refs_6_.refs_8_, ...), custom_call_target="tpu_custom_call" | custom-call | flops 656000000 | bytes 1968000 | tf_op jit(solution)/shard_map/begun/pallas_call | solution.py:220
  14.9 0.0 collective-permute-done.3.refs_3_
  14.9 0.8 %systems.5 = bf16[2,272,128]{2,1,0:T(8,128)(2,1)S(1)} custom-call(bf16[32,1280]{1,0:T(8,128)(2,1)S(1)} %get-tuple-element.31.refs_0_, bf16[32,1280]{1,0:T(8,128)(2,1)S(1)} %collective-permute-done.1.refs_1_, bf16[32,1280]{1,0:T(8,128)(2,1)S(1)} %collective-permute-done.2.refs_0_.refs_2_, bf16[32,1280]{1,0:T(8,128)(2,1)S(1)} %collective-permute-done.3.refs_3_, ...), custom_call_target="tpu_custom_call" | custom-call | flops 656000000 | bytes 1968000 | tf_op jit(solution)/shard_map/systems/pallas_call | solution.py:284
  15.7 1.5 %collective-permute-start.6 = (bf16[2,272,128]{2,1,0:T(8,128)(2,1)S(1)}, bf16[2,272,128]{2,1,0:T(8,128)(2,1)S(1)}, u32[]{:S(2)}, u32[]{:S(2)}) collective-permute-start(bf16[2,272,128]{2,1,0:T(8,128)(2,1)S(1)} %systems.5), channel_id=1, source_target_pairs={{0,4},{1,5},{2,6},{3,7},{4,0},{5,1},{6,2},{7,3},{8,12},{9,13},{10,... | collective-permute-start | bytes 417800 | tf_op jit(solution)/shard_map/ppermute | solution.py:469
  17.2 1.3 %systems.6 = bf16[2,272,128]{2,1,0:T(8,128)(2,1)S(1)} custom-call(bf16[32,1280]{1,0:T(8,128)(2,1)S(1)} %get-tuple-element.31.refs_0_, bf16[32,1280]{1,0:T(8,128)(2,1)S(1)} %collective-permute-done.1.refs_1_, bf16[32,1280]{1,0:T(8,128)(2,1)S(1)} %collective-permute-done.2.refs_0_.refs_2_, bf16[32,1280]{1,0:T(8,128)(2,1)S(1)} %collective-permute-done.3.refs_3_, ...), custom_call_target="tpu_custom_call" | custom-call | flops 1312000000 | bytes 3936000 | tf_op jit(solution)/shard_map/systems/pallas_call | solution.py:284
  18.6 0.6 %collective-permute-start.9 = (bf16[2,272,128]{2,1,0:T(8,128)(2,1)S(1)}, bf16[2,272,128]{2,1,0:T(8,128)(2,1)S(1)}, u32[]{:S(2)}, u32[]{:S(2)}) collective-permute-start(bf16[2,272,128]{2,1,0:T(8,128)(2,1)S(1)} %systems.6), channel_id=1, source_target_pairs={{0,4},{1,5},{2,6},{3,7},{4,0},{5,1},{6,2},{7,3},{8,12},{9,13},{10,... | collective-permute-start | bytes 417800 | tf_op jit(solution)/shard_map/ppermute | solution.py:469
  19.2 2.4 %systems.7.own = f32[2,272,128]{2,1,0:T(8,128)S(1)} custom-call(bf16[32,1280]{1,0:T(8,128)(2,1)S(1)} %get-tuple-element.31.refs_0_, bf16[32,1280]{1,0:T(8,128)(2,1)S(1)} %collective-permute-done.1.refs_1_, bf16[32,1280]{1,0:T(8,128)(2,1)S(1)} %collective-permute-done.2.refs_0_.refs_2_, bf16[32,1280]{1,0:T(8,128)(2,1)S(1)} %collective-permute-done.3.refs_3_, ...), custom_call_target="tpu_custom_call" | custom-call | flops 10000000 | bytes 30000 | tf_op jit(solution)/shard_map/systems/pallas_call | solution.py:284
  21.6 0.3 collective-permute-done.6.got
  22.0 2.7 %collective-permute-start.8 = (bf16[272,128]{1,0:T(8,128)(2,1)S(1)}, bf16[272,128]{1,0:T(8,128)(2,1)S(1)}, u32[]{:S(2)}, u32[]{:S(2)}) collective-permute-start(bf16[272,128]{1,0:T(8,128)(2,1)S(1)} %get-tuple-element.38), channel_id=1, source_target_pairs={{0,16},{1,17},{2,18},{3,19},{4,20},{5,21},{6,22},{7,23},{8,24},{9,... | collective-permute-start | bytes 208904 | tf_op jit(solution)/shard_map/ppermute | solution.py:469
  24.6 1.3 %collective-permute-start.7 = (bf16[272,128]{1,0:T(8,128)(2,1)S(1)}, bf16[272,128]{1,0:T(8,128)(2,1)S(1)}, u32[]{:S(2)}, u32[]{:S(2)}) collective-permute-start(bf16[272,128]{1,0:T(8,128)(2,1)S(1)} %get-tuple-element.41), channel_id=1, source_target_pairs={{0,24},{1,25},{2,26},{3,27},{4,28},{5,29},{6,30},{7,31},{8,16},{9,... | collective-permute-start | bytes 208904 | tf_op jit(solution)/shard_map/ppermute | solution.py:469
  26.0 1.3 %systems.8.own = f32[1,272,128]{2,1,0:T(8,128)S(1)} custom-call(bf16[32,1280]{1,0:T(8,128)(2,1)S(1)} %get-tuple-element.31.refs_0_, bf16[32,1280]{1,0:T(8,128)(2,1)S(1)} %collective-permute-done.1.refs_1_, bf16[32,1280]{1,0:T(8,128)(2,1)S(1)} %collective-permute-done.2.refs_0_.refs_2_, bf16[32,1280]{1,0:T(8,128)(2,1)S(1)} %collective-permute-done.3.refs_3_, ...), custom_call_target="tpu_custom_call" | custom-call | flops 1312000000 | bytes 3936000 | tf_op jit(solution)/shard_map/systems/pallas_call | solution.py:284
  27.3 0.0 collective-permute-done.9.got.refs_3_
  27.3 0.3 collective-permute-start.10
  27.6 1.3 %systems.9.own = f32[1,272,128]{2,1,0:T(8,128)S(1)} custom-call(bf16[32,1280]{1,0:T(8,128)(2,1)S(1)} %get-tuple-element.31.refs_0_, bf16[32,1280]{1,0:T(8,128)(2,1)S(1)} %collective-permute-done.1.refs_1_, bf16[32,1280]{1,0:T(8,128)(2,1)S(1)} %collective-permute-done.2.refs_0_.refs_2_, bf16[32,1280]{1,0:T(8,128)(2,1)S(1)} %collective-permute-done.3.refs_3_, ...), custom_call_target="tpu_custom_call" | custom-call | flops 1312000000 | bytes 3936000 | tf_op jit(solution)/shard_map/systems/pallas_call | solution.py:284
  29.0 2.6 %collective-permute-done.7.refs_0_ = bf16[272,128]{1,0:T(8,128)(2,1)S(1)} collective-permute-done((bf16[272,128]{1,0:T(8,128)(2,1)S(1)}, bf16[272,128]{1,0:T(8,128)(2,1)S(1)}, u32[]{:S(2)}, u32[]{:S(2)}) %collective-permute-start.7) | collective-permute-done | bytes 69664 | tf_op jit(solution)/shard_map/ppermute | solution.py:469
  31.5 0.0 collective-permute-done.8.refs_1_
  31.6 0.2 flip.1
  31.7 0.2 collective-permute-done.10.refs_2_
  32.0 1.6 %gradients.1 = (f32[4,128]{1,0:T(4,128)}, bf16[32,4,128]{2,1,0:T(4,128)(2,1)S(1)}) custom-call(f32[1,272,128]{2,1,0:T(8,128)S(1)} %systems.9.own, bf16[272,128]{1,0:T(8,128)(2,1)S(1)} %collective-permute-done.7.refs_0_, bf16[272,128]{1,0:T(8,128)(2,1)S(1)} %collective-permute-done.8.refs_1_, bf16[272,128]{1,0:T(8,128)(2,1)S(1)} %collective-permute-done.10.refs_2_, ...), custom_call_target="tpu_custom_call" | custom-call | flops 2000000000 | bytes 6000000 | tf_op jit(solution)/shard_map/gradients/pallas_call | solution.py:393
  33.6 11.9 %all_to_all.5 = bf16[32,4,128]{2,1,0:T(4,128)(2,1)S(1)} all-to-all(bf16[32,4,128]{2,1,0:T(4,128)(2,1)S(1)} %get-tuple-element.51), channel_id=1, replica_groups=mesh['user'=8,'grp'=4] {'user','grp'}, dimensions={0} | all-to-all | bytes 65536 | tf_op jit(solution)/shard_map/all_to_all | solution.py:521
  45.5 1.1 %user_side.1 = f32[1024,128]{1,0:T(8,128)} custom-call(s32[1]{0:T(128)} %bitcast.me_s, bf16[128,128]{1,0:T(8,128)(2,1)S(1)} %bitcast.2, bf16[1024,128]{1,0:T(8,128)(2,1)S(1)} %get-tuple-element.52.c_hi, bf16[1024,128]{1,0:T(8,128)(2,1)S(1)} %get-tuple-element.53.c_lo), custom_call_target="tpu_custom_call" | custom-call | flops 1000000000 | bytes 3000000 | tf_op jit(solution)/shard_map/user_side/pallas_call | solution.py:427
  (2 shorter events, 0.1 us)
Async XLA Ops:
  0.6 10.5 %collective-permute-start.4 = (bf16[1024,128]{1,0:T(8,128)(2,1)}, bf16[1024,128]{1,0:T(8,128)(2,1)S(1)}, u32[]{:S(2)}, u32[]{:S(2)}) collective-permute-start(bf16[1024,128]{1,0:T(8,128)(2,1)} %refs_4_.7), channel_id=1, source_target_pairs={{0,1},{1,0},{2,3},{3,2},{4,5},{5,4},{6,7},{7,6},{8,9},{9,8},{10,11... | collective-permute-start | bytes 786440 | tf_op jit(solution)/shard_map/ppermute | solution.py:469
  1.1 9.7 %collective-permute-start = (bf16[1024,128]{1,0:T(8,128)(2,1)}, bf16[1024,128]{1,0:T(8,128)(2,1)S(1)}, u32[]{:S(2)}, u32[]{:S(2)}) collective-permute-start(bf16[1024,128]{1,0:T(8,128)(2,1)} %refs_4_.7), channel_id=1, source_target_pairs={{0,2},{1,3},{2,0},{3,1},{4,6},{5,7},{6,4},{7,5},{8,10},{9,11},{10,... | collective-permute-start | bytes 786440 | tf_op jit(solution)/shard_map/ppermute | solution.py:469
  3.7 7.3 %copy-start = (bf16[1024,128]{1,0:T(8,128)(2,1)S(1)}, bf16[1024,128]{1,0:T(8,128)(2,1)}, u32[]{:S(2)}) copy-start(bf16[1024,128]{1,0:T(8,128)(2,1)} %refs_4_.7) | copy-start | bytes 786436
  8.7 2.6 %collective-permute-start.1 = (bf16[32,1280]{1,0:T(8,128)(2,1)S(1)}, bf16[32,1280]{1,0:T(8,128)(2,1)S(1)}, u32[]{:S(2)}, u32[]{:S(2)}) collective-permute-start(bf16[32,1280]{1,0:T(8,128)(2,1)S(1)} %get-tuple-element.32), channel_id=1, source_target_pairs={{0,1},{1,0},{2,3},{3,2},{4,5},{5,4},{6,7},{7,6},{8,9},{9,8},{10,11... | collective-permute-start | bytes 245768 | tf_op jit(solution)/shard_map/ppermute | solution.py:469
  8.9 5.3 %collective-permute-start.2 = (bf16[32,1280]{1,0:T(8,128)(2,1)S(1)}, bf16[32,1280]{1,0:T(8,128)(2,1)S(1)}, u32[]{:S(2)}, u32[]{:S(2)}) collective-permute-start(bf16[32,1280]{1,0:T(8,128)(2,1)S(1)} %get-tuple-element.33), channel_id=1, source_target_pairs={{0,2},{1,3},{2,0},{3,1},{4,6},{5,7},{6,4},{7,5},{8,10},{9,11},{10,... | collective-permute-start | bytes 245768 | tf_op jit(solution)/shard_map/ppermute | solution.py:469
  9.2 5.7 %collective-permute-start.3 = (bf16[32,1280]{1,0:T(8,128)(2,1)S(1)}, bf16[32,1280]{1,0:T(8,128)(2,1)S(1)}, u32[]{:S(2)}, u32[]{:S(2)}) collective-permute-start(bf16[32,1280]{1,0:T(8,128)(2,1)S(1)} %get-tuple-element.34), channel_id=1, source_target_pairs={{0,3},{1,2},{2,1},{3,0},{4,7},{5,6},{6,5},{7,4},{8,11},{9,10},{10,... | collective-permute-start | bytes 245768 | tf_op jit(solution)/shard_map/ppermute | solution.py:469
  10.9 2.8 %collective-permute-start.5 = (bf16[1024,128]{1,0:T(8,128)(2,1)S(1)}, bf16[1024,128]{1,0:T(8,128)(2,1)S(1)}, u32[]{:S(2)}, u32[]{:S(2)}) collective-permute-start(bf16[1024,128]{1,0:T(8,128)(2,1)S(1)} %collective-permute-done.refs_2_.refs_1_.refs_4_.refs_6_), channel_id=1, source_target_pairs={{0,1},{1,0},{2,3},{3,2},{4,5},{5,4},{6,7},{7,6},{8,9},{9,8},{10,11... | collective-permute-start | bytes 786440 | tf_op jit(solution)/shard_map/ppermute | solution.py:469
  15.7 6.2 %collective-permute-start.6 = (bf16[2,272,128]{2,1,0:T(8,128)(2,1)S(1)}, bf16[2,272,128]{2,1,0:T(8,128)(2,1)S(1)}, u32[]{:S(2)}, u32[]{:S(2)}) collective-permute-start(bf16[2,272,128]{2,1,0:T(8,128)(2,1)S(1)} %systems.5), channel_id=1, source_target_pairs={{0,4},{1,5},{2,6},{3,7},{4,0},{5,1},{6,2},{7,3},{8,12},{9,13},{10,... | collective-permute-start | bytes 417800 | tf_op jit(solution)/shard_map/ppermute | solution.py:469
  18.6 8.7 %collective-permute-start.9 = (bf16[2,272,128]{2,1,0:T(8,128)(2,1)S(1)}, bf16[2,272,128]{2,1,0:T(8,128)(2,1)S(1)}, u32[]{:S(2)}, u32[]{:S(2)}) collective-permute-start(bf16[2,272,128]{2,1,0:T(8,128)(2,1)S(1)} %systems.6), channel_id=1, source_target_pairs={{0,4},{1,5},{2,6},{3,7},{4,0},{5,1},{6,2},{7,3},{8,12},{9,13},{10,... | collective-permute-start | bytes 417800 | tf_op jit(solution)/shard_map/ppermute | solution.py:469
  22.0 9.6 %collective-permute-start.8 = (bf16[272,128]{1,0:T(8,128)(2,1)S(1)}, bf16[272,128]{1,0:T(8,128)(2,1)S(1)}, u32[]{:S(2)}, u32[]{:S(2)}) collective-permute-start(bf16[272,128]{1,0:T(8,128)(2,1)S(1)} %get-tuple-element.38), channel_id=1, source_target_pairs={{0,16},{1,17},{2,18},{3,19},{4,20},{5,21},{6,22},{7,23},{8,24},{9,... | collective-permute-start | bytes 208904 | tf_op jit(solution)/shard_map/ppermute | solution.py:469
  24.6 6.9 %collective-permute-start.7 = (bf16[272,128]{1,0:T(8,128)(2,1)S(1)}, bf16[272,128]{1,0:T(8,128)(2,1)S(1)}, u32[]{:S(2)}, u32[]{:S(2)}) collective-permute-start(bf16[272,128]{1,0:T(8,128)(2,1)S(1)} %get-tuple-element.41), channel_id=1, source_target_pairs={{0,24},{1,25},{2,26},{3,27},{4,28},{5,29},{6,30},{7,31},{8,16},{9,... | collective-permute-start | bytes 208904 | tf_op jit(solution)/shard_map/ppermute | solution.py:469
  27.3 4.6 %collective-permute-start.10 = (bf16[272,128]{1,0:T(8,128)(2,1)S(1)}, bf16[272,128]{1,0:T(8,128)(2,1)S(1)}, u32[]{:S(2)}, u32[]{:S(2)}) collective-permute-start(bf16[272,128]{1,0:T(8,128)(2,1)S(1)} %merge.3), channel_id=1, source_target_pairs={{0,8},{1,9},{2,10},{3,11},{4,12},{5,13},{6,14},{7,15},{8,0},{9,1},... | collective-permute-start | bytes 208904 | tf_op jit(solution)/shard_map/ppermute | solution.py:469

commit v7 on v6

--- a/solution.py
+++ b/solution.py
@@ -401,7 +401,27 @@
     )(own, *got, prev)
 
 
-def user_side_kernel(item_dev, n_grp, n_user, me_s, returned, c_hi, c_lo, out, rows, order, made, sem):
+def summed_kernel(own, *refs):
+    *got, out = refs
+    value = own[0]
+    for g in got:
+        value = value + (g[...] if len(g.shape) == 2 else g[0]).astype(f32)
+    out[0] = value
+
+
+def summed(own, got):
+    return pl.pallas_call(
+        summed_kernel,
+        in_specs=[VMEM] * (1 + len(got)),
+        out_specs=VMEM,
+        out_shape=struct(own.shape, f32),
+        compiler_params=params(16),
+        cost_estimate=cost(8),
+        name="summed",
+    )(own, *got)
+
+
+def user_side_kernel(item_dev, n_grp, n_user, me_s, returned, c_both, out, rows, order, made, sem):
     num_items = returned.shape[0]
     rows[...] = returned[...].astype(f32)
     me = me_s[0]
@@ -409,51 +429,50 @@
         owner = owner_of(group, item_dev, n_grp, n_user) ^ me
         order[group * item_dev : (group + 1) * item_dev, :] = rows[pl.ds(owner * item_dev, item_dev), :]
     ret = order[...].astype(bf16)
+    ret = jnp.concatenate([ret, ret], 0)
     copies = []
     for c in range(made.shape[0]):
         rows_c = slice(c * made.shape[1], (c + 1) * made.shape[1])
-        made[c] = jnp.dot(c_hi[rows_c], ret, preferred_element_type=f32) + jnp.dot(
-            c_lo[rows_c], ret, preferred_element_type=f32
-        )
+        made[c] = jnp.dot(c_both[rows_c], ret, preferred_element_type=f32)
         copies.append(pltpu.make_async_copy(made.at[c], out.at[rows_c], sem.at[c]))
         copies[-1].start()
     for copy in copies:
         copy.wait()
 
 
-def user_side(me, returned, c_hi, c_lo, item_dev, n_grp, n_user):
+def user_side(me, returned, c_both, item_dev, n_grp, n_user):
     num_items, rank = returned.shape
     pieces = 4
     return pl.pallas_call(
         functools.partial(user_side_kernel, item_dev, n_grp, n_user),
-        in_specs=[SMEM, VMEM, VMEM, VMEM],
+        in_specs=[SMEM, VMEM, VMEM],
         out_specs=pl.BlockSpec(memory_space=pltpu.HBM),
-        out_shape=struct((c_hi.shape[0], rank), f32),
+        out_shape=struct((c_both.shape[0], rank), f32),
         scratch_shapes=[pltpu.VMEM((num_items, rank), f32)] * 2
-        + [pltpu.VMEM((pieces, c_hi.shape[0] // pieces, rank), f32), pltpu.SemaphoreType.DMA((pieces,))],
+        + [pltpu.VMEM((pieces, c_both.shape[0] // pieces, rank), f32), pltpu.SemaphoreType.DMA((pieces,))],
         compiler_params=params(16),
         cost_estimate=cost(1),
         name="user_side",
-    )(me, returned, c_hi, c_lo)
-
-
-def flip_kernel(*refs):
-    n = len(refs) // 2
-    for a, b in zip(refs[:n], refs[n:]):
+    )(me, returned, c_both)
+
+
+def flip_kernel(a, b, out):
+    items = a.shape[0]
+    for n, v in enumerate((a, b)):
         for c in range(a.shape[1] // 128):
-            b[c * 128 : (c + 1) * 128, :] = a[:, c * 128 : (c + 1) * 128].T
-
-
-def flipped(*values):
+            out[c * 128 : (c + 1) * 128, n * items : (n + 1) * items] = v[:, c * 128 : (c + 1) * 128].T
+
+
+def flipped(c_hi, c_lo):
     return pl.pallas_call(
         flip_kernel,
-        in_specs=[VMEM] * len(values),
-        out_specs=[VMEM] * len(values),
-        out_shape=[struct(v.shape[::-1], v.dtype) for v in values],
+        in_specs=[VMEM] * 2,
+        out_specs=VMEM,
+        out_shape=struct((c_hi.shape[1], 2 * c_hi.shape[0]), bf16),
         compiler_params=params(16),
-        cost_estimate=cost(8),
+        cost_estimate=cost(0.01),
         name="flip",
-    )(*values)
+    )(c_hi, c_lo)
 
 
 def shards(user_factors, tile_user, tile_count, tile_valid, tile_item, prev_items):
@@ -474,7 +493,8 @@
     *es, c_hi, c_lo, prev = histogram(
         me, tile_valid, tile_item, tile_user, tile_count, u0, prev_items, num_items, item_dev, n_grp, n_user
     )
-    u2, es[0] = lax.optimization_barrier((u2, es[0]))
+    c_both = flipped(c_hi, c_lo)
+    u2, c_both = lax.optimization_barrier((u2, c_both))
     u3 = swap(u2, 1)
     got = [es[0], swap(es[1], 1), swap(es[2], 2), swap(es[3], 3)]
     us = [u0, u1, u2, u3]
@@ -501,7 +521,8 @@
         parts += [swap(value, n_grp * 2 * (n + 1)) for n, value in enumerate(near)]
         ut, _ = lax.optimization_barrier((ut, own))
         own = systems(got, us, ut, 0, item_dev, item_dev, True)
-        parts.append(near_other)
+        own = summed(own, [near_other] + parts[:-1])
+        parts = parts[-1:]
     else:
         left, bit = n_user, n_grp
         sent = systems(got, us, ut, n_half, n_half, item_dev, False, start, 2)
@@ -514,12 +535,9 @@
             left, bit = left // 2, bit * 2
         own, *sent = merged(own, other, item_dev, 1, True)
         parts = [swap(value, bit * (n + 1)) for n, value in enumerate(sent)]
-    c_hi, c_lo, own, *parts[:2] = lax.optimization_barrier((c_hi, c_lo, own, *parts[:2]))
-    c_hi, c_lo = flipped(c_hi, c_lo)
-    own, c_hi = lax.optimization_barrier((own, c_hi))
     solved, spread = gradients(own, parts, prev, devices)
     returned = lax.all_to_all(spread, AXES, 0, 0, tiled=True).reshape(num_items, rank)
-    return solved, user_side(me, returned, c_hi, c_lo, item_dev, n_grp, n_user)
+    return solved, user_side(me, returned, c_both, item_dev, n_grp, n_user)
 
 
 def solution(mesh):

time: 46.8 us -> 46.4 us (level)
  blocking collectives: 11.9 us -> 10.9 us
  starting transfers between devices: 11.7 us -> 12.3 us
    all_to_all x1, blocking collectives: 11.9 us -> 10.9 us  [shards(): lax.all_to_all(spread, AXES, 0, 0, tiled=True).reshape(num_items, rank)]
    ppermute x11, starting transfers between devices: 11.7 us -> 12.3 us  [swap(): return lax.ppermute(value, AXES, [(d, d ^ bit) for d in range(devices)])]
  transfers between devices with their start and end apart: 11 -> 11, of which waited for: 5 -> 3; matrix products, arithmetic and copies ran while one was open for 0% -> 0% of each run, Pallas kernels for 32% -> 33%
where the time goes in v7:
time: 46.4 us; the launch traced here: 46.2 us
  Pallas kernels  18.5 us (40%)
  starting transfers between devices  12.3 us (27%)
  blocking collectives  10.9 us (23%)
  waiting for transfers between devices  3.66 us (8%)
  between operations  0.76 us (2%)
    ppermute x11, starting transfers between devices, swap(): return lax.ppermute(value, AXES, [(d, d ^ bit) for d in range(devices)])  12.3 us
    all_to_all x1, blocking collectives, shards(): lax.all_to_all(spread, AXES, 0, 0, tiled=True).reshape(num_items, rank)  10.9 us
    pallas_call x5, Pallas kernels, systems(): pl.pallas_call(functools.partial(systems_kernel, first, n_items, item_dev...  7.12 us
    pallas_call x1, Pallas kernels, histogram(): pl.pallas_call(functools.partial(histogram_kernel, step, low_part, item_d...  4.9 us
    ppermute x11, waiting for transfers between devices, swap(): return lax.ppermute(value, AXES, [(d, d ^ bit) for d in range(devices)])  3.66 us
    pallas_call x2, Pallas kernels, begun(): pl.pallas_call(functools.partial(begun_kernel, first, n_items, item_dev,...  3.02 us
    pallas_call x1, Pallas kernels, gradients(): pl.pallas_call(functools.partial(gradients_kernel, item_dev), in_specs=[V...  1.65 us
    pallas_call x1, Pallas kernels, user_side(): pl.pallas_call(functools.partial(user_side_kernel, item_dev, n_grp, n_use...  1.06 us
  transfers between devices with their start and end apart: 11, of which 3 were waited for; matrix products, arithmetic and copies ran while one was open for 0% of the time, Pallas kernels for 33%

profile of v7, /device:TPU:0, one launch (start us, length us, event | category | flops | bytes accessed | tf_op | source)
XLA Modules:
  0.0 46.2 jit_solution(16227303096636290910)
XLA Ops:
  0.6 3.0 %collective-permute-start.4 = (bf16[1024,128]{1,0:T(8,128)(2,1)}, bf16[1024,128]{1,0:T(8,128)(2,1)S(1)}, u32[]{:S(2)}, u32[]{:S(2)}) collective-permute-start(bf16[1024,128]{1,0:T(8,128)(2,1)} %refs_4_.7), channel_id=1, source_target_pairs={{0,2},{1,3},{2,0},{3,1},{4,6},{5,7},{6,4},{7,5},{8,10},{9,11},{10,... | collective-permute-start | bytes 786440 | tf_op jit(solution)/shard_map/ppermute | solution.py:488
  3.7 0.0 collective-permute-start.3
  3.7 4.9 %histogram.1 = (bf16[32,1280]{1,0:T(8,128)(2,1)S(1)}, bf16[32,1280]{1,0:T(8,128)(2,1)S(1)}, bf16[32,1280]{1,0:T(8,128)(2,1)S(1)}, bf16[32,1280]{1,0:T(8,128)(2,1...) custom-call(s32[1]{0:T(128)} %bitcast.me_s, s32[1,384]{1,0:T(1,128)} %refs_0_.3, ...), custom_call_target="tpu_custom_call" | custom-call | flops 7000000000 | bytes 21000000 | tf_op jit(solution)/shard_map/histogram/pallas_call | solution.py:143
  8.6 0.6 %collective-permute-start = (bf16[32,1280]{1,0:T(8,128)(2,1)S(1)}, bf16[32,1280]{1,0:T(8,128)(2,1)S(1)}, u32[]{:S(2)}, u32[]{:S(2)}) collective-permute-start(bf16[32,1280]{1,0:T(8,128)(2,1)S(1)} %get-tuple-element.20), channel_id=1, source_target_pairs={{0,1},{1,0},{2,3},{3,2},{4,5},{5,4},{6,7},{7,6},{8,9},{9,8},{10,11... | collective-permute-start | bytes 245768 | tf_op jit(solution)/shard_map/ppermute | solution.py:488
  9.2 0.1 collective-permute-start.1
  9.2 1.4 %collective-permute-start.2 = (bf16[32,1280]{1,0:T(8,128)(2,1)S(1)}, bf16[32,1280]{1,0:T(8,128)(2,1)S(1)}, u32[]{:S(2)}, u32[]{:S(2)}) collective-permute-start(bf16[32,1280]{1,0:T(8,128)(2,1)S(1)} %get-tuple-element.22), channel_id=1, source_target_pairs={{0,3},{1,2},{2,1},{3,0},{4,7},{5,6},{6,5},{7,4},{8,11},{9,10},{10,... | collective-permute-start | bytes 245768 | tf_op jit(solution)/shard_map/ppermute | solution.py:488
  10.6 0.0 copy-start
  10.6 0.2 flip.1.c_both
  10.8 0.0 collective-permute-done.4.refs_2_.refs_1_.refs_4_.refs_6_
  10.8 0.8 %collective-permute-start.5 = (bf16[1024,128]{1,0:T(8,128)(2,1)S(1)}, bf16[1024,128]{1,0:T(8,128)(2,1)S(1)}, u32[]{:S(2)}, u32[]{:S(2)}) collective-permute-start(bf16[1024,128]{1,0:T(8,128)(2,1)S(1)} %collective-permute-done.4.refs_2_.refs_1_.refs_4_.refs_6_), channel_id=1, source_target_pairs={{0,1},{1,0},{2,3},{3,2},{4,5},{5,4},{6,7},{7,6},{8,9},{9,8},{10,11... | collective-permute-start | bytes 786440 | tf_op jit(solution)/shard_map/ppermute | solution.py:488
  11.6 0.0 collective-permute-done.3.refs_1_.refs_3_.refs_5_
  11.6 0.0 copy-done
  11.6 0.2 transpose.3.refs_4_
  11.8 0.0 collective-permute-done.refs_1_
  11.8 2.3 %begun.2.refs_3_.refs_7_ = f32[4,512,128]{2,1,0:T(8,128)S(1)} custom-call(bf16[32,1280]{1,0:T(8,128)(2,1)S(1)} %get-tuple-element.19.refs_0_, bf16[32,1280]{1,0:T(8,128)(2,1)S(1)} %collective-permute-done.refs_1_, bf16[1024,128]{1,0:T(8,128)(2,1)S(1)} %copy-done, bf16[1024,128]{1,0:T(8,128)(2,1)S(1)} %collective-permute-done.3.refs_1_.refs_3_.refs_5_, ...), custom_call_target="tpu_custom_call" | custom-call | flops 2624000000 | bytes 7872000 | tf_op jit(solution)/shard_map/begun/pallas_call | solution.py:220
  14.1 0.0 collective-permute-done.5.refs_3_.refs_4_.refs_5_.refs_7_
  14.1 0.3 transpose.2.refs_2_.refs_5_.refs_6_.refs_8_
  14.4 0.0 collective-permute-done.1.refs_0_.refs_2_
  14.5 0.7 %begun.3.refs_6_ = f32[2,512,128]{2,1,0:T(8,128)S(1)} custom-call(bf16[32,1280]{1,0:T(8,128)(2,1)S(1)} %collective-permute-done.1.refs_0_.refs_2_, bf16[1024,128]{1,0:T(8,128)(2,1)S(1)} %collective-permute-done.4.refs_2_.refs_1_.refs_4_.refs_6_, bf16[128,4096]{1,0:T(8,128)(2,1)S(1)} %transpose.2.refs_2_.refs_5_.refs_6_.refs_8_, ...), custom_call_target="tpu_custom_call" | custom-call | flops 656000000 | bytes 1968000 | tf_op jit(solution)/shard_map/begun/pallas_call | solution.py:220
  15.2 0.0 collective-permute-done.2.refs_3_
  15.2 0.8 %systems.5 = bf16[2,272,128]{2,1,0:T(8,128)(2,1)S(1)} custom-call(bf16[32,1280]{1,0:T(8,128)(2,1)S(1)} %get-tuple-element.19.refs_0_, bf16[32,1280]{1,0:T(8,128)(2,1)S(1)} %collective-permute-done.refs_1_, bf16[32,1280]{1,0:T(8,128)(2,1)S(1)} %collective-permute-done.1.refs_0_.refs_2_, bf16[32,1280]{1,0:T(8,128)(2,1)S(1)} %collective-permute-done.2.refs_3_, ...), custom_call_target="tpu_custom_call" | custom-call | flops 656000000 | bytes 1968000 | tf_op jit(solution)/shard_map/systems/pallas_call | solution.py:284
  16.0 1.6 %collective-permute-start.6 = (bf16[2,272,128]{2,1,0:T(8,128)(2,1)S(1)}, bf16[2,272,128]{2,1,0:T(8,128)(2,1)S(1)}, u32[]{:S(2)}, u32[]{:S(2)}) collective-permute-start(bf16[2,272,128]{2,1,0:T(8,128)(2,1)S(1)} %systems.5), channel_id=1, source_target_pairs={{0,4},{1,5},{2,6},{3,7},{4,0},{5,1},{6,2},{7,3},{8,12},{9,13},{10,... | collective-permute-start | bytes 417800 | tf_op jit(solution)/shard_map/ppermute | solution.py:488
  17.5 1.3 %systems.6 = bf16[2,272,128]{2,1,0:T(8,128)(2,1)S(1)} custom-call(bf16[32,1280]{1,0:T(8,128)(2,1)S(1)} %get-tuple-element.19.refs_0_, bf16[32,1280]{1,0:T(8,128)(2,1)S(1)} %collective-permute-done.refs_1_, bf16[32,1280]{1,0:T(8,128)(2,1)S(1)} %collective-permute-done.1.refs_0_.refs_2_, bf16[32,1280]{1,0:T(8,128)(2,1)S(1)} %collective-permute-done.2.refs_3_, ...), custom_call_target="tpu_custom_call" | custom-call | flops 1312000000 | bytes 3936000 | tf_op jit(solution)/shard_map/systems/pallas_call | solution.py:284
  18.8 0.6 %collective-permute-start.7 = (bf16[2,272,128]{2,1,0:T(8,128)(2,1)S(1)}, bf16[2,272,128]{2,1,0:T(8,128)(2,1)S(1)}, u32[]{:S(2)}, u32[]{:S(2)}) collective-permute-start(bf16[2,272,128]{2,1,0:T(8,128)(2,1)S(1)} %systems.6), channel_id=1, source_target_pairs={{0,4},{1,5},{2,6},{3,7},{4,0},{5,1},{6,2},{7,3},{8,12},{9,13},{10,... | collective-permute-start | bytes 417800 | tf_op jit(solution)/shard_map/ppermute | solution.py:488
  19.5 2.4 %systems.7.own = f32[2,272,128]{2,1,0:T(8,128)S(1)} custom-call(bf16[32,1280]{1,0:T(8,128)(2,1)S(1)} %get-tuple-element.19.refs_0_, bf16[32,1280]{1,0:T(8,128)(2,1)S(1)} %collective-permute-done.refs_1_, bf16[32,1280]{1,0:T(8,128)(2,1)S(1)} %collective-permute-done.1.refs_0_.refs_2_, bf16[32,1280]{1,0:T(8,128)(2,1)S(1)} %collective-permute-done.2.refs_3_, ...), custom_call_target="tpu_custom_call" | custom-call | flops 10000000 | bytes 30000 | tf_op jit(solution)/shard_map/systems/pallas_call | solution.py:284
  21.9 0.7 %collective-permute-done.6.got = bf16[2,272,128]{2,1,0:T(8,128)(2,1)S(1)} collective-permute-done((bf16[2,272,128]{2,1,0:T(8,128)(2,1)S(1)}, bf16[2,272,128]{2,1,0:T(8,128)(2,1)S(1)}, u32[]{:S(2)}, u32[]{:S(2)}) %collective-permute-start.6) | collective-permute-done | bytes 139296 | tf_op jit(solution)/shard_map/ppermute | solution.py:488
  22.6 2.6 %collective-permute-start.9 = (bf16[272,128]{1,0:T(8,128)(2,1)S(1)}, bf16[272,128]{1,0:T(8,128)(2,1)S(1)}, u32[]{:S(2)}, u32[]{:S(2)}) collective-permute-start(bf16[272,128]{1,0:T(8,128)(2,1)S(1)} %get-tuple-element.28), channel_id=1, source_target_pairs={{0,16},{1,17},{2,18},{3,19},{4,20},{5,21},{6,22},{7,23},{8,24},{9,... | collective-permute-start | bytes 208904 | tf_op jit(solution)/shard_map/ppermute | solution.py:488
  25.3 1.3 %collective-permute-start.8 = (bf16[272,128]{1,0:T(8,128)(2,1)S(1)}, bf16[272,128]{1,0:T(8,128)(2,1)S(1)}, u32[]{:S(2)}, u32[]{:S(2)}) collective-permute-start(bf16[272,128]{1,0:T(8,128)(2,1)S(1)} %get-tuple-element.31), channel_id=1, source_target_pairs={{0,24},{1,25},{2,26},{3,27},{4,28},{5,29},{6,30},{7,31},{8,16},{9,... | collective-permute-start | bytes 208904 | tf_op jit(solution)/shard_map/ppermute | solution.py:488
  26.6 1.3 %systems.8.own = f32[1,272,128]{2,1,0:T(8,128)S(1)} custom-call(bf16[32,1280]{1,0:T(8,128)(2,1)S(1)} %get-tuple-element.19.refs_0_, bf16[32,1280]{1,0:T(8,128)(2,1)S(1)} %collective-permute-done.refs_1_, bf16[32,1280]{1,0:T(8,128)(2,1)S(1)} %collective-permute-done.1.refs_0_.refs_2_, bf16[32,1280]{1,0:T(8,128)(2,1)S(1)} %collective-permute-done.2.refs_3_, ...), custom_call_target="tpu_custom_call" | custom-call | flops 1312000000 | bytes 3936000 | tf_op jit(solution)/shard_map/systems/pallas_call | solution.py:284
  27.9 0.0 collective-permute-done.7.refs_0_.got
  28.0 0.3 collective-permute-start.10
  28.3 1.3 %systems.9.own = f32[1,272,128]{2,1,0:T(8,128)S(1)} custom-call(bf16[32,1280]{1,0:T(8,128)(2,1)S(1)} %get-tuple-element.19.refs_0_, bf16[32,1280]{1,0:T(8,128)(2,1)S(1)} %collective-permute-done.refs_1_, bf16[32,1280]{1,0:T(8,128)(2,1)S(1)} %collective-permute-done.1.refs_0_.refs_2_, bf16[32,1280]{1,0:T(8,128)(2,1)S(1)} %collective-permute-done.2.refs_3_, ...), custom_call_target="tpu_custom_call" | custom-call | flops 1312000000 | bytes 3936000 | tf_op jit(solution)/shard_map/systems/pallas_call | solution.py:284
  29.6 2.4 %collective-permute-done.8.refs_1_ = bf16[272,128]{1,0:T(8,128)(2,1)S(1)} collective-permute-done((bf16[272,128]{1,0:T(8,128)(2,1)S(1)}, bf16[272,128]{1,0:T(8,128)(2,1)S(1)}, u32[]{:S(2)}, u32[]{:S(2)}) %collective-permute-start.8) | collective-permute-done | bytes 69664 | tf_op jit(solution)/shard_map/ppermute | solution.py:488
  32.0 0.0 collective-permute-done.9.refs_2_
  32.1 0.5 %collective-permute-done.10.refs_0_ = bf16[272,128]{1,0:T(8,128)(2,1)S(1)} collective-permute-done((bf16[272,128]{1,0:T(8,128)(2,1)S(1)}, bf16[272,128]{1,0:T(8,128)(2,1)S(1)}, u32[]{:S(2)}, u32[]{:S(2)}) %collective-permute-start.10) | collective-permute-done | bytes 69664 | tf_op jit(solution)/shard_map/ppermute | solution.py:488
  32.6 1.6 %gradients.1 = (f32[4,128]{1,0:T(4,128)}, bf16[32,4,128]{2,1,0:T(4,128)(2,1)S(1)}) custom-call(f32[1,272,128]{2,1,0:T(8,128)S(1)} %summed.1.own, bf16[272,128]{1,0:T(8,128)(2,1)S(1)} %collective-permute-done.10.refs_0_, f32[4,128]{1,0:T(4,128)S(1)} %get-tuple-element.32.refs_1_), custom_call_target="tpu_custom_call" | custom-call | flops 2000000000 | bytes 6000000 | tf_op jit(solution)/shard_map/gradients/pallas_call | solution.py:393
  34.2 10.9 %all_to_all.5 = bf16[32,4,128]{2,1,0:T(4,128)(2,1)S(1)} all-to-all(bf16[32,4,128]{2,1,0:T(4,128)(2,1)S(1)} %get-tuple-element.34), channel_id=1, replica_groups=mesh['user'=8,'grp'=4] {'user','grp'}, dimensions={0} | all-to-all | bytes 65536 | tf_op jit(solution)/shard_map/all_to_all | solution.py:539
  45.1 1.1 %user_side.1 = f32[1024,128]{1,0:T(8,128)} custom-call(s32[1]{0:T(128)} %bitcast.me_s, bf16[128,128]{1,0:T(8,128)(2,1)S(1)} %bitcast.2, bf16[1024,256]{1,0:T(8,128)(2,1)S(1)} %flip.1.c_both), custom_call_target="tpu_custom_call" | custom-call | flops 1000000000 | bytes 3000000 | tf_op jit(solution)/shard_map/user_side/pallas_call | solution.py:446
  (3 shorter events, 0.1 us)
Async XLA Ops:
  0.6 10.1 %collective-permute-start.4 = (bf16[1024,128]{1,0:T(8,128)(2,1)}, bf16[1024,128]{1,0:T(8,128)(2,1)S(1)}, u32[]{:S(2)}, u32[]{:S(2)}) collective-permute-start(bf16[1024,128]{1,0:T(8,128)(2,1)} %refs_4_.7), channel_id=1, source_target_pairs={{0,2},{1,3},{2,0},{3,1},{4,6},{5,7},{6,4},{7,5},{8,10},{9,11},{10,... | collective-permute-start | bytes 786440 | tf_op jit(solution)/shard_map/ppermute | solution.py:488
  3.7 7.9 %collective-permute-start.3 = (bf16[1024,128]{1,0:T(8,128)(2,1)}, bf16[1024,128]{1,0:T(8,128)(2,1)S(1)}, u32[]{:S(2)}, u32[]{:S(2)}) collective-permute-start(bf16[1024,128]{1,0:T(8,128)(2,1)} %refs_4_.7), channel_id=1, source_target_pairs={{0,1},{1,0},{2,3},{3,2},{4,5},{5,4},{6,7},{7,6},{8,9},{9,8},{10,11... | collective-permute-start | bytes 786440 | tf_op jit(solution)/shard_map/ppermute | solution.py:488
  8.6 3.2 %collective-permute-start = (bf16[32,1280]{1,0:T(8,128)(2,1)S(1)}, bf16[32,1280]{1,0:T(8,128)(2,1)S(1)}, u32[]{:S(2)}, u32[]{:S(2)}) collective-permute-start(bf16[32,1280]{1,0:T(8,128)(2,1)S(1)} %get-tuple-element.20), channel_id=1, source_target_pairs={{0,1},{1,0},{2,3},{3,2},{4,5},{5,4},{6,7},{7,6},{8,9},{9,8},{10,11... | collective-permute-start | bytes 245768 | tf_op jit(solution)/shard_map/ppermute | solution.py:488
  9.2 5.3 %collective-permute-start.1 = (bf16[32,1280]{1,0:T(8,128)(2,1)S(1)}, bf16[32,1280]{1,0:T(8,128)(2,1)S(1)}, u32[]{:S(2)}, u32[]{:S(2)}) collective-permute-start(bf16[32,1280]{1,0:T(8,128)(2,1)S(1)} %get-tuple-element.21), channel_id=1, source_target_pairs={{0,2},{1,3},{2,0},{3,1},{4,6},{5,7},{6,4},{7,5},{8,10},{9,11},{10,... | collective-permute-start | bytes 245768 | tf_op jit(solution)/shard_map/ppermute | solution.py:488
  9.2 5.9 %collective-permute-start.2 = (bf16[32,1280]{1,0:T(8,128)(2,1)S(1)}, bf16[32,1280]{1,0:T(8,128)(2,1)S(1)}, u32[]{:S(2)}, u32[]{:S(2)}) collective-permute-start(bf16[32,1280]{1,0:T(8,128)(2,1)S(1)} %get-tuple-element.22), channel_id=1, source_target_pairs={{0,3},{1,2},{2,1},{3,0},{4,7},{5,6},{6,5},{7,4},{8,11},{9,10},{10,... | collective-permute-start | bytes 245768 | tf_op jit(solution)/shard_map/ppermute | solution.py:488
  10.6 1.0 %copy-start = (bf16[1024,128]{1,0:T(8,128)(2,1)S(1)}, bf16[1024,128]{1,0:T(8,128)(2,1)}, u32[]{:S(2)}) copy-start(bf16[1024,128]{1,0:T(8,128)(2,1)} %refs_4_.7) | copy-start | bytes 786436
  10.8 3.3 %collective-permute-start.5 = (bf16[1024,128]{1,0:T(8,128)(2,1)S(1)}, bf16[1024,128]{1,0:T(8,128)(2,1)S(1)}, u32[]{:S(2)}, u32[]{:S(2)}) collective-permute-start(bf16[1024,128]{1,0:T(8,128)(2,1)S(1)} %collective-permute-done.4.refs_2_.refs_1_.refs_4_.refs_6_), channel_id=1, source_target_pairs={{0,1},{1,0},{2,3},{3,2},{4,5},{5,4},{6,7},{7,6},{8,9},{9,8},{10,11... | collective-permute-start | bytes 786440 | tf_op jit(solution)/shard_map/ppermute | solution.py:488
  16.0 6.6 %collective-permute-start.6 = (bf16[2,272,128]{2,1,0:T(8,128)(2,1)S(1)}, bf16[2,272,128]{2,1,0:T(8,128)(2,1)S(1)}, u32[]{:S(2)}, u32[]{:S(2)}) collective-permute-start(bf16[2,272,128]{2,1,0:T(8,128)(2,1)S(1)} %systems.5), channel_id=1, source_target_pairs={{0,4},{1,5},{2,6},{3,7},{4,0},{5,1},{6,2},{7,3},{8,12},{9,13},{10,... | collective-permute-start | bytes 417800 | tf_op jit(solution)/shard_map/ppermute | solution.py:488
  18.8 9.1 %collective-permute-start.7 = (bf16[2,272,128]{2,1,0:T(8,128)(2,1)S(1)}, bf16[2,272,128]{2,1,0:T(8,128)(2,1)S(1)}, u32[]{:S(2)}, u32[]{:S(2)}) collective-permute-start(bf16[2,272,128]{2,1,0:T(8,128)(2,1)S(1)} %systems.6), channel_id=1, source_target_pairs={{0,4},{1,5},{2,6},{3,7},{4,0},{5,1},{6,2},{7,3},{8,12},{9,13},{10,... | collective-permute-start | bytes 417800 | tf_op jit(solution)/shard_map/ppermute | solution.py:488
  22.6 9.4 %collective-permute-start.9 = (bf16[272,128]{1,0:T(8,128)(2,1)S(1)}, bf16[272,128]{1,0:T(8,128)(2,1)S(1)}, u32[]{:S(2)}, u32[]{:S(2)}) collective-permute-start(bf16[272,128]{1,0:T(8,128)(2,1)S(1)} %get-tuple-element.28), channel_id=1, source_target_pairs={{0,16},{1,17},{2,18},{3,19},{4,20},{5,21},{6,22},{7,23},{8,24},{9,... | collective-permute-start | bytes 208904 | tf_op jit(solution)/shard_map/ppermute | solution.py:488
  25.3 6.8 %collective-permute-start.8 = (bf16[272,128]{1,0:T(8,128)(2,1)S(1)}, bf16[272,128]{1,0:T(8,128)(2,1)S(1)}, u32[]{:S(2)}, u32[]{:S(2)}) collective-permute-start(bf16[272,128]{1,0:T(8,128)(2,1)S(1)} %get-tuple-element.31), channel_id=1, source_target_pairs={{0,24},{1,25},{2,26},{3,27},{4,28},{5,29},{6,30},{7,31},{8,16},{9,... | collective-permute-start | bytes 208904 | tf_op jit(solution)/shard_map/ppermute | solution.py:488
  28.0 4.6 %collective-permute-start.10 = (bf16[272,128]{1,0:T(8,128)(2,1)S(1)}, bf16[272,128]{1,0:T(8,128)(2,1)S(1)}, u32[]{:S(2)}, u32[]{:S(2)}) collective-permute-start(bf16[272,128]{1,0:T(8,128)(2,1)S(1)} %merge.3), channel_id=1, source_target_pairs={{0,8},{1,9},{2,10},{3,11},{4,12},{5,13},{6,14},{7,15},{8,0},{9,1},... | collective-permute-start | bytes 208904 | tf_op jit(solution)/shard_map/ppermute | solution.py:488

commit v8 on v7

--- a/solution.py
+++ b/solution.py
@@ -59,7 +59,7 @@
 def histogram_kernel(step, low_part, item_dev, n_grp, n_user, me_s, *refs):
     sources, rest = refs[:6], refs[6:]
     eouts = rest[:n_grp]
-    c_hi, c_lo, prev_here, acc, *here, sem = rest[n_grp:]
+    c_hi, c_lo, prev_here, ut, acc, *here, sem = rest[n_grp:]
     here.append(prev_here)
     copies = [pltpu.make_async_copy(a, b, sem.at[n]) for n, (a, b) in enumerate(zip(sources, here))]
     for copy in copies:
@@ -112,6 +112,7 @@
     lax.fori_loop(0, tiles // step, body, jnp.zeros((kinds, low_part), f32))
     copies[4].wait()
     copies[5].wait()
+    transpose_kernel(u, ut)
     per = num_items // n_grp
     wide = 128 // low_part
 
@@ -143,10 +144,10 @@
     return pl.pallas_call(
         functools.partial(histogram_kernel, step, low_part, item_dev, n_grp, n_user),
         in_specs=[SMEM] + [pl.BlockSpec(memory_space=pltpu.HBM)] * 6,
-        out_specs=[VMEM] * (n_grp + 3),
+        out_specs=[VMEM] * (n_grp + 4),
         out_shape=[struct((num_items // n_grp, block_users + 2 * rank), bf16)] * n_grp
         + [struct((num_items, block_users), bf16)] * 2
-        + [struct(prev.shape, f32)],
+        + [struct(prev.shape, f32), struct((rank, block_users), bf16)],
         scratch_shapes=[
             pltpu.VMEM((num_items * (2 * block_users // low_part + 8), low_part), f32),
             pltpu.SMEM(valid.shape, i32),
@@ -162,40 +163,36 @@
     )(me, *[pltpu.with_memory_space_constraint(v, pltpu.HBM) for v in (valid, item, users, counts, u, prev)])
 
 
-def transpose_kernel(*refs):
-    *us, ut = refs
-    block_users = us[0].shape[0]
-    for b, u in enumerate(us):
-        for c in range(block_users // 128):
-            at = b * block_users + c * 128
-            ut[:, at : at + 128] = u[c * 128 : (c + 1) * 128, :].T
-
-
-def transposed(us):
-    block_users, rank = us[0].shape
+def transpose_kernel(u, ut):
+    for c in range(u.shape[0] // 128):
+        ut[:, c * 128 : (c + 1) * 128] = u[c * 128 : (c + 1) * 128, :].T
+
+
+def transposed(u):
     return pl.pallas_call(
         transpose_kernel,
-        in_specs=[VMEM] * len(us),
+        in_specs=[VMEM],
         out_specs=VMEM,
-        out_shape=struct((rank, block_users * len(us)), bf16),
+        out_shape=struct(u.shape[::-1], bf16),
         compiler_params=params(16),
-        cost_estimate=cost(0.2),
+        cost_estimate=cost(0.1),
         name="transpose",
-    )(*us)
+    )(u)
 
 
 def chunk_rows(item_dev):
     return 64 * item_dev + -(-4 * item_dev // 16) * 16
 
 
-def partial_systems(rows, ut, us, c, item_dev, at):
-    rank = ut.shape[0]
+def partial_systems(rows, uts, us, c, item_dev):
+    rank = uts[0].shape[0]
+    ut = jnp.concatenate([t[...] for t in uts], 1)
     w = []
     for j in range(item_dev):
         one = c * item_dev + j
         e = jnp.concatenate([r[one : one + 1] for r in rows], 1)
         e = jnp.broadcast_to(e, (16, e.shape[1])).astype(bf16)
-        w.append(jnp.concatenate([e] * (rank // 16), 0) * ut[:, at : at + e.shape[1]])
+        w.append(jnp.concatenate([e] * (rank // 16), 0) * ut)
     return jnp.dot(jnp.concatenate(w, 0), jnp.concatenate([u[...] for u in us], 0), preferred_element_type=f32)
 
 
@@ -204,33 +201,34 @@
     return ref[low:high, cols].astype(f32)[first - low : first - low + n]
 
 
-def begun_kernel(first, n_items, item_dev, n, skip, at, *refs):
-    es, us, ut, out = refs[:n], refs[n : 2 * n], refs[2 * n], refs[-1]
-    more = refs[2 * n + 1 : -1]
+def begun_kernel(first, n_items, item_dev, n, at, *refs):
+    es, us, uts, out = refs[:n], refs[n : 2 * n], refs[2 * n : 3 * n], refs[-1]
+    more = refs[3 * n : -1]
     rows = [some_rows(e, first, n_items, slice(0, us[0].shape[0])) for e in es]
     for c in range(n_items // item_dev):
-        total = partial_systems(rows, ut, us, c, item_dev, skip * us[0].shape[0])
+        total = partial_systems(rows, uts, us, c, item_dev)
         out[c] = total + more[0][at + c] if more else total
 
 
-def begun(es, us, ut, first, n_items, item_dev, start=None, skip=0, at=0):
+def begun(es, us, uts, first, n_items, item_dev, start=None, at=0):
     more = [] if start is None else [start]
     n = len(es)
     block_users, rank = us[0].shape
     return pl.pallas_call(
-        functools.partial(begun_kernel, first, n_items, item_dev, n, skip, at),
-        in_specs=[VMEM] * (2 * n + 1 + len(more)),
+        functools.partial(begun_kernel, first, n_items, item_dev, n, at),
+        in_specs=[VMEM] * (3 * n + len(more)),
         out_specs=VMEM,
         out_shape=struct((n_items // item_dev, item_dev * rank, rank), f32),
         compiler_params=params(32),
         cost_estimate=cost(0.082 * n * n_items),
         name="begun",
-    )(*es, *us, ut, *more)
+    )(*es, *us, *uts, *more)
 
 
 def systems_kernel(first, n_items, item_dev, keep, n, done, at, *refs):
-    es, us, ut = refs[:n], refs[n : 2 * n - done], refs[2 * n - done]
-    start = refs[2 * n - done + 1] if done else None
+    m = n - done
+    es, us, uts = refs[:n], refs[n : n + m], refs[n + m : n + 2 * m]
+    start = refs[n + 2 * m] if done else None
     out = refs[-1]
     block_users, rank = us[0].shape
     rows = [some_rows(e, first, n_items, slice(0, block_users)) for e in es[done:]]
@@ -245,7 +243,7 @@
     base = 64 * item_dev
 
     for c in range(n_items // item_dev):
-        total = partial_systems(rows, ut, us, c, item_dev, done * block_users)
+        total = partial_systems(rows, uts, us, c, item_dev)
         if done:
             total = total + start[at + c]
         diag = []
@@ -283,13 +281,13 @@
     more = [] if start is None else [start]
     return pl.pallas_call(
         functools.partial(systems_kernel, first, n_items, item_dev, keep, n, done, at),
-        in_specs=[VMEM] * (2 * n - done + 1 + len(more)),
+        in_specs=[VMEM] * (3 * n - 2 * done + len(more)),
         out_specs=VMEM,
         out_shape=struct((n_items // item_dev, chunk_rows(item_dev), rank), f32 if keep else bf16),
         compiler_params=params(40),
         cost_estimate=cost(0.082 * (n - done) * n_items if us_cost is None else us_cost),
         name="systems",
-    )(*es, *us[done:], ut, *more)
+    )(*es, *us[done:], *ut[done:], *more)
 
 
 def extras(value, item_dev):
@@ -490,7 +488,7 @@
     u0 = user_factors
     u2 = swap(u0, 2)
     u1 = swap(u0, 1)
-    *es, c_hi, c_lo, prev = histogram(
+    *es, c_hi, c_lo, prev, ut0 = histogram(
         me, tile_valid, tile_item, tile_user, tile_count, u0, prev_items, num_items, item_dev, n_grp, n_user
     )
     c_both = flipped(c_hi, c_lo)
@@ -498,28 +496,28 @@
     u3 = swap(u2, 1)
     got = [es[0], swap(es[1], 1), swap(es[2], 2), swap(es[3], 3)]
     us = [u0, u1, u2, u3]
-    ut = transposed(us)
+    ut = [ut0] + [transposed(u) for u in us[1:]]
     n_items = num_items // n_grp
     n_half = n_items // 2
-    start = begun(got[:2], us[:2], transposed(us[:2]), n_half, n_half, item_dev)
+    start = begun(got[:2], us[:2], ut[:2], n_half, n_half, item_dev)
     if n_user == 8:
         n_far = n_half // 2
         chunks = n_far // item_dev
-        first = begun(got[2:3], us[2:3], ut, n_half + n_far, n_far, item_dev, start, 2, chunks)
+        first = begun(got[2:3], us[2:3], ut[2:3], n_half + n_far, n_far, item_dev, start, chunks)
         sent = systems(got, us, ut, n_half + n_far, n_far, item_dev, False, first, 3, 0)
         far_other = swap(sent, n_grp)
-        ut, _ = lax.optimization_barrier((ut, sent))
+        ut[0], _ = lax.optimization_barrier((ut[0], sent))
         sent = systems(got, us, ut, n_half, n_far, item_dev, False, start, 2, 0)
         near_other = swap(sent, n_grp)
-        ut, _ = lax.optimization_barrier((ut, sent))
+        ut[0], _ = lax.optimization_barrier((ut[0], sent))
         own = systems(got, us, ut, n_far, n_far, item_dev, True, us_cost=0.01)
         far = merged(own, far_other, item_dev, 0, True)
         parts = [swap(value, n_grp * 2 * (chunks + n)) for n, value in reversed(list(enumerate(far)))]
-        ut, _ = lax.optimization_barrier((ut, far[0]))
+        ut[0], _ = lax.optimization_barrier((ut[0], far[0]))
         own = systems(got, us, ut, item_dev, n_far - item_dev, item_dev, True)
         near = merged(own, near_other, item_dev, 0, True, 1)
         parts += [swap(value, n_grp * 2 * (n + 1)) for n, value in enumerate(near)]
-        ut, _ = lax.optimization_barrier((ut, own))
+        ut[0], _ = lax.optimization_barrier((ut[0], own))
         own = systems(got, us, ut, 0, item_dev, item_dev, True)
         own = summed(own, [near_other] + parts[:-1])
         parts = parts[-1:]

time: 46.4 us -> 46.2 us (level)
  transfers between devices with their start and end apart: 11 -> 11, of which waited for: 3 -> 4; matrix products, arithmetic and copies ran while one was open for 0% -> 0% of each run, Pallas kernels for 33% -> 33%
where the time goes in v8:
time: 46.2 us; the launch traced here: 46 us
  Pallas kernels  18.4 us (40%)
  starting transfers between devices  12.3 us (27%)
  blocking collectives  10.8 us (23%)
  waiting for transfers between devices  3.79 us (8%)
  between operations  0.78 us (2%)
    ppermute x11, starting transfers between devices, swap(): return lax.ppermute(value, AXES, [(d, d ^ bit) for d in range(devices)])  12.3 us
    all_to_all x1, blocking collectives, shards(): lax.all_to_all(spread, AXES, 0, 0, tiled=True).reshape(num_items, rank)  10.8 us
    pallas_call x5, Pallas kernels, systems(): pl.pallas_call(functools.partial(systems_kernel, first, n_items, item_dev...  7.11 us
    pallas_call x1, Pallas kernels, histogram(): pl.pallas_call(functools.partial(histogram_kernel, step, low_part, item_d...  4.97 us
    ppermute x11, waiting for transfers between devices, swap(): return lax.ppermute(value, AXES, [(d, d ^ bit) for d in range(devices)])  3.79 us
    pallas_call x2, Pallas kernels, begun(): pl.pallas_call(functools.partial(begun_kernel, first, n_items, item_dev,...  3.02 us
    pallas_call x1, Pallas kernels, gradients(): pl.pallas_call(functools.partial(gradients_kernel, item_dev), in_specs=[V...  1.65 us
    pallas_call x1, Pallas kernels, user_side(): pl.pallas_call(functools.partial(user_side_kernel, item_dev, n_grp, n_use...  1.06 us
  transfers between devices with their start and end apart: 11, of which 4 were waited for; matrix products, arithmetic and copies ran while one was open for 0% of the time, Pallas kernels for 33%

profile of v8, /device:TPU:0, one launch (start us, length us, event | category | flops | bytes accessed | tf_op | source)
XLA Modules:
  0.0 46.0 jit_solution(18006904405937568089)
XLA Ops:
  0.6 3.0 %collective-permute-start.4 = (bf16[1024,128]{1,0:T(8,128)(2,1)}, bf16[1024,128]{1,0:T(8,128)(2,1)S(1)}, u32[]{:S(2)}, u32[]{:S(2)}) collective-permute-start(bf16[1024,128]{1,0:T(8,128)(2,1)} %refs_4_.7), channel_id=1, source_target_pairs={{0,2},{1,3},{2,0},{3,1},{4,6},{5,7},{6,4},{7,5},{8,10},{9,11},{10,... | collective-permute-start | bytes 786440 | tf_op jit(solution)/shard_map/ppermute | solution.py:486
  3.7 0.0 collective-permute-start.3
  3.7 5.0 %histogram.1 = (bf16[32,1280]{1,0:T(8,128)(2,1)S(1)}, bf16[32,1280]{1,0:T(8,128)(2,1)S(1)}, bf16[32,1280]{1,0:T(8,128)(2,1)S(1)}, bf16[32,1280]{1,0:T(8,128)(2,1...) custom-call(s32[1]{0:T(128)} %bitcast.me_s, ...), custom_call_target="tpu_custom_call" | custom-call | flops 7000000000 | bytes 21000000 | tf_op jit(solution)/shard_map/histogram/pallas_call | solution.py:144
  8.6 0.6 %collective-permute-start = (bf16[32,1280]{1,0:T(8,128)(2,1)S(1)}, bf16[32,1280]{1,0:T(8,128)(2,1)S(1)}, u32[]{:S(2)}, u32[]{:S(2)}) collective-permute-start(bf16[32,1280]{1,0:T(8,128)(2,1)S(1)} %get-tuple-element.21), channel_id=1, source_target_pairs={{0,1},{1,0},{2,3},{3,2},{4,5},{5,4},{6,7},{7,6},{8,9},{9,8},{10,11... | collective-permute-start | bytes 245768 | tf_op jit(solution)/shard_map/ppermute | solution.py:486
  9.2 0.1 collective-permute-start.1
  9.3 1.4 %collective-permute-start.2 = (bf16[32,1280]{1,0:T(8,128)(2,1)S(1)}, bf16[32,1280]{1,0:T(8,128)(2,1)S(1)}, u32[]{:S(2)}, u32[]{:S(2)}) collective-permute-start(bf16[32,1280]{1,0:T(8,128)(2,1)S(1)} %get-tuple-element.23), channel_id=1, source_target_pairs={{0,3},{1,2},{2,1},{3,0},{4,7},{5,6},{6,5},{7,4},{8,11},{9,10},{10,... | collective-permute-start | bytes 245768 | tf_op jit(solution)/shard_map/ppermute | solution.py:486
  10.6 0.2 flip.1.c_both
  10.8 0.0 copy-start
  10.9 0.0 collective-permute-done.4.u.refs_1_.refs_4_.refs_6_
  10.9 0.8 %collective-permute-start.5 = (bf16[1024,128]{1,0:T(8,128)(2,1)S(1)}, bf16[1024,128]{1,0:T(8,128)(2,1)S(1)}, u32[]{:S(2)}, u32[]{:S(2)}) collective-permute-start(bf16[1024,128]{1,0:T(8,128)(2,1)S(1)} %collective-permute-done.4.u.refs_1_.refs_4_.refs_6_), channel_id=1, source_target_pairs={{0,1},{1,0},{2,3},{3,2},{4,5},{5,4},{6,7},{7,6},{8,9},{9,8},{10,11... | collective-permute-start | bytes 786440 | tf_op jit(solution)/shard_map/ppermute | solution.py:486
  11.6 0.0 collective-permute-done.3.u.refs_3_.refs_5_
  11.6 0.1 transpose.5.refs_5_.refs_9_
  11.8 0.0 collective-permute-done.refs_1_
  11.8 0.0 copy-done
  11.8 2.3 %begun.2.refs_3_.refs_8_ = f32[4,512,128]{2,1,0:T(8,128)S(1)} custom-call(bf16[32,1280]{1,0:T(8,128)(2,1)S(1)} %get-tuple-element.20.refs_0_, bf16[32,1280]{1,0:T(8,128)(2,1)S(1)} %collective-permute-done.refs_1_, bf16[1024,128]{1,0:T(8,128)(2,1)S(1)} %copy-done, bf16[1024,128]{1,0:T(8,128)(2,1)S(1)} %collective-permute-done.3.u.refs_3_.refs_5_, ...), custom_call_target="tpu_custom_call" | custom-call | flops 2624000000 | bytes 7872000 | tf_op jit(solution)/shard_map/begun/pallas_call | solution.py:217
  14.1 0.1 transpose.4.refs_2_.refs_6_.refs_10_
  14.2 0.3 collective-permute-done.1.refs_0_.refs_2_
  14.5 0.7 %begun.3.refs_6_ = f32[2,512,128]{2,1,0:T(8,128)S(1)} custom-call(bf16[32,1280]{1,0:T(8,128)(2,1)S(1)} %collective-permute-done.1.refs_0_.refs_2_, bf16[1024,128]{1,0:T(8,128)(2,1)S(1)} %collective-permute-done.4.u.refs_1_.refs_4_.refs_6_, bf16[128,1024]{1,0:T(8,128)(2,1)S(1)} %transpose.4.refs_2_.refs_6_.refs_10_, f32[4,512,128]{2,1,0:T(8,128)S(1)} %begun.2.refs_3_.refs_8_), custom_call_target="tpu_custom_call" | custom-call | flops 656000000 | bytes 1968000 | tf_op jit(solution)/shard_map/begun/pallas_call | solution.py:217
  15.2 0.0 collective-permute-done.5.u.refs_4_.refs_5_.refs_7_
  15.2 0.1 transpose.3.refs_5_.refs_7_.refs_11_
  15.4 0.0 collective-permute-done.2.refs_3_
  15.4 0.8 %systems.5 = bf16[2,272,128]{2,1,0:T(8,128)(2,1)S(1)} custom-call(bf16[32,1280]{1,0:T(8,128)(2,1)S(1)} %get-tuple-element.20.refs_0_, bf16[32,1280]{1,0:T(8,128)(2,1)S(1)} %collective-permute-done.refs_1_, bf16[32,1280]{1,0:T(8,128)(2,1)S(1)} %collective-permute-done.1.refs_0_.refs_2_, bf16[32,1280]{1,0:T(8,128)(2,1)S(1)} %collective-permute-done.2.refs_3_, ...), custom_call_target="tpu_custom_call" | custom-call | flops 656000000 | bytes 1968000 | tf_op jit(solution)/shard_map/systems/pallas_call | solution.py:282
  16.2 1.6 %collective-permute-start.6 = (bf16[2,272,128]{2,1,0:T(8,128)(2,1)S(1)}, bf16[2,272,128]{2,1,0:T(8,128)(2,1)S(1)}, u32[]{:S(2)}, u32[]{:S(2)}) collective-permute-start(bf16[2,272,128]{2,1,0:T(8,128)(2,1)S(1)} %systems.5), channel_id=1, source_target_pairs={{0,4},{1,5},{2,6},{3,7},{4,0},{5,1},{6,2},{7,3},{8,12},{9,13},{10,... | collective-permute-start | bytes 417800 | tf_op jit(solution)/shard_map/ppermute | solution.py:486
  17.7 1.3 %systems.6 = bf16[2,272,128]{2,1,0:T(8,128)(2,1)S(1)} custom-call(bf16[32,1280]{1,0:T(8,128)(2,1)S(1)} %get-tuple-element.20.refs_0_, bf16[32,1280]{1,0:T(8,128)(2,1)S(1)} %collective-permute-done.refs_1_, bf16[32,1280]{1,0:T(8,128)(2,1)S(1)} %collective-permute-done.1.refs_0_.refs_2_, bf16[32,1280]{1,0:T(8,128)(2,1)S(1)} %collective-permute-done.2.refs_3_, ...), custom_call_target="tpu_custom_call" | custom-call | flops 1312000000 | bytes 3936000 | tf_op jit(solution)/shard_map/systems/pallas_call | solution.py:282
  19.0 0.6 %collective-permute-start.7 = (bf16[2,272,128]{2,1,0:T(8,128)(2,1)S(1)}, bf16[2,272,128]{2,1,0:T(8,128)(2,1)S(1)}, u32[]{:S(2)}, u32[]{:S(2)}) collective-permute-start(bf16[2,272,128]{2,1,0:T(8,128)(2,1)S(1)} %systems.6), channel_id=1, source_target_pairs={{0,4},{1,5},{2,6},{3,7},{4,0},{5,1},{6,2},{7,3},{8,12},{9,13},{10,... | collective-permute-start | bytes 417800 | tf_op jit(solution)/shard_map/ppermute | solution.py:486
  19.6 2.4 %systems.7.own = f32[2,272,128]{2,1,0:T(8,128)S(1)} custom-call(bf16[32,1280]{1,0:T(8,128)(2,1)S(1)} %get-tuple-element.20.refs_0_, bf16[32,1280]{1,0:T(8,128)(2,1)S(1)} %collective-permute-done.refs_1_, bf16[32,1280]{1,0:T(8,128)(2,1)S(1)} %collective-permute-done.1.refs_0_.refs_2_, bf16[32,1280]{1,0:T(8,128)(2,1)S(1)} %collective-permute-done.2.refs_3_, ...), custom_call_target="tpu_custom_call" | custom-call | flops 10000000 | bytes 30000 | tf_op jit(solution)/shard_map/systems/pallas_call | solution.py:282
  22.0 0.5 %collective-permute-done.6.got = bf16[2,272,128]{2,1,0:T(8,128)(2,1)S(1)} collective-permute-done((bf16[2,272,128]{2,1,0:T(8,128)(2,1)S(1)}, bf16[2,272,128]{2,1,0:T(8,128)(2,1)S(1)}, u32[]{:S(2)}, u32[]{:S(2)}) %collective-permute-start.6) | collective-permute-done | bytes 139296 | tf_op jit(solution)/shard_map/ppermute | solution.py:486
  22.6 2.6 %collective-permute-start.9 = (bf16[272,128]{1,0:T(8,128)(2,1)S(1)}, bf16[272,128]{1,0:T(8,128)(2,1)S(1)}, u32[]{:S(2)}, u32[]{:S(2)}) collective-permute-start(bf16[272,128]{1,0:T(8,128)(2,1)S(1)} %get-tuple-element.30), channel_id=1, source_target_pairs={{0,16},{1,17},{2,18},{3,19},{4,20},{5,21},{6,22},{7,23},{8,24},{9,... | collective-permute-start | bytes 208904 | tf_op jit(solution)/shard_map/ppermute | solution.py:486
  25.3 1.3 %collective-permute-start.8 = (bf16[272,128]{1,0:T(8,128)(2,1)S(1)}, bf16[272,128]{1,0:T(8,128)(2,1)S(1)}, u32[]{:S(2)}, u32[]{:S(2)}) collective-permute-start(bf16[272,128]{1,0:T(8,128)(2,1)S(1)} %get-tuple-element.33), channel_id=1, source_target_pairs={{0,24},{1,25},{2,26},{3,27},{4,28},{5,29},{6,30},{7,31},{8,16},{9,... | collective-permute-start | bytes 208904 | tf_op jit(solution)/shard_map/ppermute | solution.py:486
  26.6 1.3 %systems.8.own = f32[1,272,128]{2,1,0:T(8,128)S(1)} custom-call(bf16[32,1280]{1,0:T(8,128)(2,1)S(1)} %get-tuple-element.20.refs_0_, bf16[32,1280]{1,0:T(8,128)(2,1)S(1)} %collective-permute-done.refs_1_, bf16[32,1280]{1,0:T(8,128)(2,1)S(1)} %collective-permute-done.1.refs_0_.refs_2_, bf16[32,1280]{1,0:T(8,128)(2,1)S(1)} %collective-permute-done.2.refs_3_, ...), custom_call_target="tpu_custom_call" | custom-call | flops 1312000000 | bytes 3936000 | tf_op jit(solution)/shard_map/systems/pallas_call | solution.py:282
  27.9 0.0 collective-permute-done.7.refs_0_.got
  28.0 0.3 collective-permute-start.10
  28.3 1.3 %systems.9.own = f32[1,272,128]{2,1,0:T(8,128)S(1)} custom-call(bf16[32,1280]{1,0:T(8,128)(2,1)S(1)} %get-tuple-element.20.refs_0_, bf16[32,1280]{1,0:T(8,128)(2,1)S(1)} %collective-permute-done.refs_1_, bf16[32,1280]{1,0:T(8,128)(2,1)S(1)} %collective-permute-done.1.refs_0_.refs_2_, bf16[32,1280]{1,0:T(8,128)(2,1)S(1)} %collective-permute-done.2.refs_3_, ...), custom_call_target="tpu_custom_call" | custom-call | flops 1312000000 | bytes 3936000 | tf_op jit(solution)/shard_map/systems/pallas_call | solution.py:282
  29.6 2.6 %collective-permute-done.8.refs_1_ = bf16[272,128]{1,0:T(8,128)(2,1)S(1)} collective-permute-done((bf16[272,128]{1,0:T(8,128)(2,1)S(1)}, bf16[272,128]{1,0:T(8,128)(2,1)S(1)}, u32[]{:S(2)}, u32[]{:S(2)}) %collective-permute-start.8) | collective-permute-done | bytes 69664 | tf_op jit(solution)/shard_map/ppermute | solution.py:486
  32.2 0.0 collective-permute-done.9.refs_2_
  32.2 0.4 collective-permute-done.10.refs_0_
  32.6 1.6 %gradients.1 = (f32[4,128]{1,0:T(4,128)}, bf16[32,4,128]{2,1,0:T(4,128)(2,1)S(1)}) custom-call(f32[1,272,128]{2,1,0:T(8,128)S(1)} %summed.1.own, bf16[272,128]{1,0:T(8,128)(2,1)S(1)} %collective-permute-done.10.refs_0_, f32[4,128]{1,0:T(4,128)S(1)} %get-tuple-element.34.refs_1_), custom_call_target="tpu_custom_call" | custom-call | flops 2000000000 | bytes 6000000 | tf_op jit(solution)/shard_map/gradients/pallas_call | solution.py:391
  34.2 10.8 %all_to_all.5 = bf16[32,4,128]{2,1,0:T(4,128)(2,1)S(1)} all-to-all(bf16[32,4,128]{2,1,0:T(4,128)(2,1)S(1)} %get-tuple-element.36), channel_id=1, replica_groups=mesh['user'=8,'grp'=4] {'user','grp'}, dimensions={0} | all-to-all | bytes 65536 | tf_op jit(solution)/shard_map/all_to_all | solution.py:537
  45.0 1.1 %user_side.1 = f32[1024,128]{1,0:T(8,128)} custom-call(s32[1]{0:T(128)} %bitcast.me_s, bf16[128,128]{1,0:T(8,128)(2,1)S(1)} %bitcast.2, bf16[1024,256]{1,0:T(8,128)(2,1)S(1)} %flip.1.c_both), custom_call_target="tpu_custom_call" | custom-call | flops 1000000000 | bytes 3000000 | tf_op jit(solution)/shard_map/user_side/pallas_call | solution.py:444
  (3 shorter events, 0.1 us)
Async XLA Ops:
  0.6 10.2 %collective-permute-start.4 = (bf16[1024,128]{1,0:T(8,128)(2,1)}, bf16[1024,128]{1,0:T(8,128)(2,1)S(1)}, u32[]{:S(2)}, u32[]{:S(2)}) collective-permute-start(bf16[1024,128]{1,0:T(8,128)(2,1)} %refs_4_.7), channel_id=1, source_target_pairs={{0,2},{1,3},{2,0},{3,1},{4,6},{5,7},{6,4},{7,5},{8,10},{9,11},{10,... | collective-permute-start | bytes 786440 | tf_op jit(solution)/shard_map/ppermute | solution.py:486
  3.7 8.0 %collective-permute-start.3 = (bf16[1024,128]{1,0:T(8,128)(2,1)}, bf16[1024,128]{1,0:T(8,128)(2,1)S(1)}, u32[]{:S(2)}, u32[]{:S(2)}) collective-permute-start(bf16[1024,128]{1,0:T(8,128)(2,1)} %refs_4_.7), channel_id=1, source_target_pairs={{0,1},{1,0},{2,3},{3,2},{4,5},{5,4},{6,7},{7,6},{8,9},{9,8},{10,11... | collective-permute-start | bytes 786440 | tf_op jit(solution)/shard_map/ppermute | solution.py:486
  8.6 3.1 %collective-permute-start = (bf16[32,1280]{1,0:T(8,128)(2,1)S(1)}, bf16[32,1280]{1,0:T(8,128)(2,1)S(1)}, u32[]{:S(2)}, u32[]{:S(2)}) collective-permute-start(bf16[32,1280]{1,0:T(8,128)(2,1)S(1)} %get-tuple-element.21), channel_id=1, source_target_pairs={{0,1},{1,0},{2,3},{3,2},{4,5},{5,4},{6,7},{7,6},{8,9},{9,8},{10,11... | collective-permute-start | bytes 245768 | tf_op jit(solution)/shard_map/ppermute | solution.py:486
  9.2 5.3 %collective-permute-start.1 = (bf16[32,1280]{1,0:T(8,128)(2,1)S(1)}, bf16[32,1280]{1,0:T(8,128)(2,1)S(1)}, u32[]{:S(2)}, u32[]{:S(2)}) collective-permute-start(bf16[32,1280]{1,0:T(8,128)(2,1)S(1)} %get-tuple-element.22), channel_id=1, source_target_pairs={{0,2},{1,3},{2,0},{3,1},{4,6},{5,7},{6,4},{7,5},{8,10},{9,11},{10,... | collective-permute-start | bytes 245768 | tf_op jit(solution)/shard_map/ppermute | solution.py:486
  9.3 6.1 %collective-permute-start.2 = (bf16[32,1280]{1,0:T(8,128)(2,1)S(1)}, bf16[32,1280]{1,0:T(8,128)(2,1)S(1)}, u32[]{:S(2)}, u32[]{:S(2)}) collective-permute-start(bf16[32,1280]{1,0:T(8,128)(2,1)S(1)} %get-tuple-element.23), channel_id=1, source_target_pairs={{0,3},{1,2},{2,1},{3,0},{4,7},{5,6},{6,5},{7,4},{8,11},{9,10},{10,... | collective-permute-start | bytes 245768 | tf_op jit(solution)/shard_map/ppermute | solution.py:486
  10.8 1.0 %copy-start = (bf16[1024,128]{1,0:T(8,128)(2,1)S(1)}, bf16[1024,128]{1,0:T(8,128)(2,1)}, u32[]{:S(2)}) copy-start(bf16[1024,128]{1,0:T(8,128)(2,1)} %refs_4_.7) | copy-start | bytes 786436
  10.9 4.4 %collective-permute-start.5 = (bf16[1024,128]{1,0:T(8,128)(2,1)S(1)}, bf16[1024,128]{1,0:T(8,128)(2,1)S(1)}, u32[]{:S(2)}, u32[]{:S(2)}) collective-permute-start(bf16[1024,128]{1,0:T(8,128)(2,1)S(1)} %collective-permute-done.4.u.refs_1_.refs_4_.refs_6_), channel_id=1, source_target_pairs={{0,1},{1,0},{2,3},{3,2},{4,5},{5,4},{6,7},{7,6},{8,9},{9,8},{10,11... | collective-permute-start | bytes 786440 | tf_op jit(solution)/shard_map/ppermute | solution.py:486
  16.2 6.4 %collective-permute-start.6 = (bf16[2,272,128]{2,1,0:T(8,128)(2,1)S(1)}, bf16[2,272,128]{2,1,0:T(8,128)(2,1)S(1)}, u32[]{:S(2)}, u32[]{:S(2)}) collective-permute-start(bf16[2,272,128]{2,1,0:T(8,128)(2,1)S(1)} %systems.5), channel_id=1, source_target_pairs={{0,4},{1,5},{2,6},{3,7},{4,0},{5,1},{6,2},{7,3},{8,12},{9,13},{10,... | collective-permute-start | bytes 417800 | tf_op jit(solution)/shard_map/ppermute | solution.py:486
  19.0 8.9 %collective-permute-start.7 = (bf16[2,272,128]{2,1,0:T(8,128)(2,1)S(1)}, bf16[2,272,128]{2,1,0:T(8,128)(2,1)S(1)}, u32[]{:S(2)}, u32[]{:S(2)}) collective-permute-start(bf16[2,272,128]{2,1,0:T(8,128)(2,1)S(1)} %systems.6), channel_id=1, source_target_pairs={{0,4},{1,5},{2,6},{3,7},{4,0},{5,1},{6,2},{7,3},{8,12},{9,13},{10,... | collective-permute-start | bytes 417800 | tf_op jit(solution)/shard_map/ppermute | solution.py:486
  22.6 9.5 %collective-permute-start.9 = (bf16[272,128]{1,0:T(8,128)(2,1)S(1)}, bf16[272,128]{1,0:T(8,128)(2,1)S(1)}, u32[]{:S(2)}, u32[]{:S(2)}) collective-permute-start(bf16[272,128]{1,0:T(8,128)(2,1)S(1)} %get-tuple-element.30), channel_id=1, source_target_pairs={{0,16},{1,17},{2,18},{3,19},{4,20},{5,21},{6,22},{7,23},{8,24},{9,... | collective-permute-start | bytes 208904 | tf_op jit(solution)/shard_map/ppermute | solution.py:486
  25.3 6.9 %collective-permute-start.8 = (bf16[272,128]{1,0:T(8,128)(2,1)S(1)}, bf16[272,128]{1,0:T(8,128)(2,1)S(1)}, u32[]{:S(2)}, u32[]{:S(2)}) collective-permute-start(bf16[272,128]{1,0:T(8,128)(2,1)S(1)} %get-tuple-element.33), channel_id=1, source_target_pairs={{0,24},{1,25},{2,26},{3,27},{4,28},{5,29},{6,30},{7,31},{8,16},{9,... | collective-permute-start | bytes 208904 | tf_op jit(solution)/shard_map/ppermute | solution.py:486
  28.0 4.6 %collective-permute-start.10 = (bf16[272,128]{1,0:T(8,128)(2,1)S(1)}, bf16[272,128]{1,0:T(8,128)(2,1)S(1)}, u32[]{:S(2)}, u32[]{:S(2)}) collective-permute-start(bf16[272,128]{1,0:T(8,128)(2,1)S(1)} %merge.3), channel_id=1, source_target_pairs={{0,8},{1,9},{2,10},{3,11},{4,12},{5,13},{6,14},{7,15},{8,0},{9,1},... | collective-permute-start | bytes 208904 | tf_op jit(solution)/shard_map/ppermute | solution.py:486

commit v9 on v8

--- a/solution.py
+++ b/solution.py
@@ -440,7 +440,7 @@
 
 def user_side(me, returned, c_both, item_dev, n_grp, n_user):
     num_items, rank = returned.shape
-    pieces = 4
+    pieces = 8
     return pl.pallas_call(
         functools.partial(user_side_kernel, item_dev, n_grp, n_user),
         in_specs=[SMEM, VMEM, VMEM],

time: 46.2 us -> 46.2 us (level)
  no operation moved by 1% of the time
where the time goes in v9:
time: 46.2 us; the launch traced here: 46 us
  Pallas kernels  18.4 us (40%)
  starting transfers between devices  12.3 us (27%)
  blocking collectives  10.8 us (23%)
  waiting for transfers between devices  3.79 us (8%)
  between operations  0.78 us (2%)
    ppermute x11, starting transfers between devices, swap(): return lax.ppermute(value, AXES, [(d, d ^ bit) for d in range(devices)])  12.3 us
    all_to_all x1, blocking collectives, shards(): lax.all_to_all(spread, AXES, 0, 0, tiled=True).reshape(num_items, rank)  10.8 us
    pallas_call x5, Pallas kernels, systems(): pl.pallas_call(functools.partial(systems_kernel, first, n_items, item_dev...  7.11 us
    pallas_call x1, Pallas kernels, histogram(): pl.pallas_call(functools.partial(histogram_kernel, step, low_part, item_d...  4.97 us
    ppermute x11, waiting for transfers between devices, swap(): return lax.ppermute(value, AXES, [(d, d ^ bit) for d in range(devices)])  3.79 us
    pallas_call x2, Pallas kernels, begun(): pl.pallas_call(functools.partial(begun_kernel, first, n_items, item_dev,...  3.02 us
    pallas_call x1, Pallas kernels, gradients(): pl.pallas_call(functools.partial(gradients_kernel, item_dev), in_specs=[V...  1.65 us
    pallas_call x1, Pallas kernels, user_side(): pl.pallas_call(functools.partial(user_side_kernel, item_dev, n_grp, n_use...  1.05 us
  transfers between devices with their start and end apart: 11, of which 4 were waited for; matrix products, arithmetic and copies ran while one was open for 0% of the time, Pallas kernels for 33%

profile of v9, /device:TPU:0, one launch (start us, length us, event | category | flops | bytes accessed | tf_op | source)
XLA Modules:
  0.0 46.0 jit_solution(12092622158440063435)
XLA Ops:
  0.6 3.0 %collective-permute-start.4 = (bf16[1024,128]{1,0:T(8,128)(2,1)}, bf16[1024,128]{1,0:T(8,128)(2,1)S(1)}, u32[]{:S(2)}, u32[]{:S(2)}) collective-permute-start(bf16[1024,128]{1,0:T(8,128)(2,1)} %refs_4_.7), channel_id=1, source_target_pairs={{0,2},{1,3},{2,0},{3,1},{4,6},{5,7},{6,4},{7,5},{8,10},{9,11},{10,... | collective-permute-start | bytes 786440 | tf_op jit(solution)/shard_map/ppermute | solution.py:486
  3.7 0.0 collective-permute-start.3
  3.7 5.0 %histogram.1 = (bf16[32,1280]{1,0:T(8,128)(2,1)S(1)}, bf16[32,1280]{1,0:T(8,128)(2,1)S(1)}, bf16[32,1280]{1,0:T(8,128)(2,1)S(1)}, bf16[32,1280]{1,0:T(8,128)(2,1...) custom-call(s32[1]{0:T(128)} %bitcast.me_s, ...), custom_call_target="tpu_custom_call" | custom-call | flops 7000000000 | bytes 21000000 | tf_op jit(solution)/shard_map/histogram/pallas_call | solution.py:144
  8.6 0.6 %collective-permute-start = (bf16[32,1280]{1,0:T(8,128)(2,1)S(1)}, bf16[32,1280]{1,0:T(8,128)(2,1)S(1)}, u32[]{:S(2)}, u32[]{:S(2)}) collective-permute-start(bf16[32,1280]{1,0:T(8,128)(2,1)S(1)} %get-tuple-element.21), channel_id=1, source_target_pairs={{0,1},{1,0},{2,3},{3,2},{4,5},{5,4},{6,7},{7,6},{8,9},{9,8},{10,11... | collective-permute-start | bytes 245768 | tf_op jit(solution)/shard_map/ppermute | solution.py:486
  9.2 0.1 collective-permute-start.1
  9.3 1.4 %collective-permute-start.2 = (bf16[32,1280]{1,0:T(8,128)(2,1)S(1)}, bf16[32,1280]{1,0:T(8,128)(2,1)S(1)}, u32[]{:S(2)}, u32[]{:S(2)}) collective-permute-start(bf16[32,1280]{1,0:T(8,128)(2,1)S(1)} %get-tuple-element.23), channel_id=1, source_target_pairs={{0,3},{1,2},{2,1},{3,0},{4,7},{5,6},{6,5},{7,4},{8,11},{9,10},{10,... | collective-permute-start | bytes 245768 | tf_op jit(solution)/shard_map/ppermute | solution.py:486
  10.6 0.2 flip.1.c_both
  10.8 0.0 copy-start
  10.9 0.0 collective-permute-done.4.u.refs_1_.refs_4_.refs_6_
  10.9 0.8 %collective-permute-start.5 = (bf16[1024,128]{1,0:T(8,128)(2,1)S(1)}, bf16[1024,128]{1,0:T(8,128)(2,1)S(1)}, u32[]{:S(2)}, u32[]{:S(2)}) collective-permute-start(bf16[1024,128]{1,0:T(8,128)(2,1)S(1)} %collective-permute-done.4.u.refs_1_.refs_4_.refs_6_), channel_id=1, source_target_pairs={{0,1},{1,0},{2,3},{3,2},{4,5},{5,4},{6,7},{7,6},{8,9},{9,8},{10,11... | collective-permute-start | bytes 786440 | tf_op jit(solution)/shard_map/ppermute | solution.py:486
  11.6 0.0 collective-permute-done.3.u.refs_3_.refs_5_
  11.6 0.1 transpose.5.refs_5_.refs_9_
  11.8 0.0 collective-permute-done.refs_1_
  11.8 0.0 copy-done
  11.8 2.3 %begun.2.refs_3_.refs_8_ = f32[4,512,128]{2,1,0:T(8,128)S(1)} custom-call(bf16[32,1280]{1,0:T(8,128)(2,1)S(1)} %get-tuple-element.20.refs_0_, bf16[32,1280]{1,0:T(8,128)(2,1)S(1)} %collective-permute-done.refs_1_, bf16[1024,128]{1,0:T(8,128)(2,1)S(1)} %copy-done, bf16[1024,128]{1,0:T(8,128)(2,1)S(1)} %collective-permute-done.3.u.refs_3_.refs_5_, ...), custom_call_target="tpu_custom_call" | custom-call | flops 2624000000 | bytes 7872000 | tf_op jit(solution)/shard_map/begun/pallas_call | solution.py:217
  14.1 0.1 transpose.4.refs_2_.refs_6_.refs_10_
  14.2 0.3 collective-permute-done.1.refs_0_.refs_2_
  14.5 0.7 %begun.3.refs_6_ = f32[2,512,128]{2,1,0:T(8,128)S(1)} custom-call(bf16[32,1280]{1,0:T(8,128)(2,1)S(1)} %collective-permute-done.1.refs_0_.refs_2_, bf16[1024,128]{1,0:T(8,128)(2,1)S(1)} %collective-permute-done.4.u.refs_1_.refs_4_.refs_6_, bf16[128,1024]{1,0:T(8,128)(2,1)S(1)} %transpose.4.refs_2_.refs_6_.refs_10_, f32[4,512,128]{2,1,0:T(8,128)S(1)} %begun.2.refs_3_.refs_8_), custom_call_target="tpu_custom_call" | custom-call | flops 656000000 | bytes 1968000 | tf_op jit(solution)/shard_map/begun/pallas_call | solution.py:217
  15.2 0.0 collective-permute-done.5.u.refs_4_.refs_5_.refs_7_
  15.2 0.1 transpose.3.refs_5_.refs_7_.refs_11_
  15.4 0.0 collective-permute-done.2.refs_3_
  15.4 0.8 %systems.5 = bf16[2,272,128]{2,1,0:T(8,128)(2,1)S(1)} custom-call(bf16[32,1280]{1,0:T(8,128)(2,1)S(1)} %get-tuple-element.20.refs_0_, bf16[32,1280]{1,0:T(8,128)(2,1)S(1)} %collective-permute-done.refs_1_, bf16[32,1280]{1,0:T(8,128)(2,1)S(1)} %collective-permute-done.1.refs_0_.refs_2_, bf16[32,1280]{1,0:T(8,128)(2,1)S(1)} %collective-permute-done.2.refs_3_, ...), custom_call_target="tpu_custom_call" | custom-call | flops 656000000 | bytes 1968000 | tf_op jit(solution)/shard_map/systems/pallas_call | solution.py:282
  16.2 1.6 %collective-permute-start.6 = (bf16[2,272,128]{2,1,0:T(8,128)(2,1)S(1)}, bf16[2,272,128]{2,1,0:T(8,128)(2,1)S(1)}, u32[]{:S(2)}, u32[]{:S(2)}) collective-permute-start(bf16[2,272,128]{2,1,0:T(8,128)(2,1)S(1)} %systems.5), channel_id=1, source_target_pairs={{0,4},{1,5},{2,6},{3,7},{4,0},{5,1},{6,2},{7,3},{8,12},{9,13},{10,... | collective-permute-start | bytes 417800 | tf_op jit(solution)/shard_map/ppermute | solution.py:486
  17.7 1.3 %systems.6 = bf16[2,272,128]{2,1,0:T(8,128)(2,1)S(1)} custom-call(bf16[32,1280]{1,0:T(8,128)(2,1)S(1)} %get-tuple-element.20.refs_0_, bf16[32,1280]{1,0:T(8,128)(2,1)S(1)} %collective-permute-done.refs_1_, bf16[32,1280]{1,0:T(8,128)(2,1)S(1)} %collective-permute-done.1.refs_0_.refs_2_, bf16[32,1280]{1,0:T(8,128)(2,1)S(1)} %collective-permute-done.2.refs_3_, ...), custom_call_target="tpu_custom_call" | custom-call | flops 1312000000 | bytes 3936000 | tf_op jit(solution)/shard_map/systems/pallas_call | solution.py:282
  19.0 0.6 %collective-permute-start.7 = (bf16[2,272,128]{2,1,0:T(8,128)(2,1)S(1)}, bf16[2,272,128]{2,1,0:T(8,128)(2,1)S(1)}, u32[]{:S(2)}, u32[]{:S(2)}) collective-permute-start(bf16[2,272,128]{2,1,0:T(8,128)(2,1)S(1)} %systems.6), channel_id=1, source_target_pairs={{0,4},{1,5},{2,6},{3,7},{4,0},{5,1},{6,2},{7,3},{8,12},{9,13},{10,... | collective-permute-start | bytes 417800 | tf_op jit(solution)/shard_map/ppermute | solution.py:486
  19.6 2.4 %systems.7.own = f32[2,272,128]{2,1,0:T(8,128)S(1)} custom-call(bf16[32,1280]{1,0:T(8,128)(2,1)S(1)} %get-tuple-element.20.refs_0_, bf16[32,1280]{1,0:T(8,128)(2,1)S(1)} %collective-permute-done.refs_1_, bf16[32,1280]{1,0:T(8,128)(2,1)S(1)} %collective-permute-done.1.refs_0_.refs_2_, bf16[32,1280]{1,0:T(8,128)(2,1)S(1)} %collective-permute-done.2.refs_3_, ...), custom_call_target="tpu_custom_call" | custom-call | flops 10000000 | bytes 30000 | tf_op jit(solution)/shard_map/systems/pallas_call | solution.py:282
  22.0 0.5 %collective-permute-done.6.got = bf16[2,272,128]{2,1,0:T(8,128)(2,1)S(1)} collective-permute-done((bf16[2,272,128]{2,1,0:T(8,128)(2,1)S(1)}, bf16[2,272,128]{2,1,0:T(8,128)(2,1)S(1)}, u32[]{:S(2)}, u32[]{:S(2)}) %collective-permute-start.6) | collective-permute-done | bytes 139296 | tf_op jit(solution)/shard_map/ppermute | solution.py:486
  22.6 2.6 %collective-permute-start.9 = (bf16[272,128]{1,0:T(8,128)(2,1)S(1)}, bf16[272,128]{1,0:T(8,128)(2,1)S(1)}, u32[]{:S(2)}, u32[]{:S(2)}) collective-permute-start(bf16[272,128]{1,0:T(8,128)(2,1)S(1)} %get-tuple-element.30), channel_id=1, source_target_pairs={{0,16},{1,17},{2,18},{3,19},{4,20},{5,21},{6,22},{7,23},{8,24},{9,... | collective-permute-start | bytes 208904 | tf_op jit(solution)/shard_map/ppermute | solution.py:486
  25.3 1.3 %collective-permute-start.8 = (bf16[272,128]{1,0:T(8,128)(2,1)S(1)}, bf16[272,128]{1,0:T(8,128)(2,1)S(1)}, u32[]{:S(2)}, u32[]{:S(2)}) collective-permute-start(bf16[272,128]{1,0:T(8,128)(2,1)S(1)} %get-tuple-element.33), channel_id=1, source_target_pairs={{0,24},{1,25},{2,26},{3,27},{4,28},{5,29},{6,30},{7,31},{8,16},{9,... | collective-permute-start | bytes 208904 | tf_op jit(solution)/shard_map/ppermute | solution.py:486
  26.6 1.3 %systems.8.own = f32[1,272,128]{2,1,0:T(8,128)S(1)} custom-call(bf16[32,1280]{1,0:T(8,128)(2,1)S(1)} %get-tuple-element.20.refs_0_, bf16[32,1280]{1,0:T(8,128)(2,1)S(1)} %collective-permute-done.refs_1_, bf16[32,1280]{1,0:T(8,128)(2,1)S(1)} %collective-permute-done.1.refs_0_.refs_2_, bf16[32,1280]{1,0:T(8,128)(2,1)S(1)} %collective-permute-done.2.refs_3_, ...), custom_call_target="tpu_custom_call" | custom-call | flops 1312000000 | bytes 3936000 | tf_op jit(solution)/shard_map/systems/pallas_call | solution.py:282
  27.9 0.0 collective-permute-done.7.refs_0_.got
  28.0 0.3 collective-permute-start.10
  28.3 1.3 %systems.9.own = f32[1,272,128]{2,1,0:T(8,128)S(1)} custom-call(bf16[32,1280]{1,0:T(8,128)(2,1)S(1)} %get-tuple-element.20.refs_0_, bf16[32,1280]{1,0:T(8,128)(2,1)S(1)} %collective-permute-done.refs_1_, bf16[32,1280]{1,0:T(8,128)(2,1)S(1)} %collective-permute-done.1.refs_0_.refs_2_, bf16[32,1280]{1,0:T(8,128)(2,1)S(1)} %collective-permute-done.2.refs_3_, ...), custom_call_target="tpu_custom_call" | custom-call | flops 1312000000 | bytes 3936000 | tf_op jit(solution)/shard_map/systems/pallas_call | solution.py:282
  29.6 2.6 %collective-permute-done.8.refs_1_ = bf16[272,128]{1,0:T(8,128)(2,1)S(1)} collective-permute-done((bf16[272,128]{1,0:T(8,128)(2,1)S(1)}, bf16[272,128]{1,0:T(8,128)(2,1)S(1)}, u32[]{:S(2)}, u32[]{:S(2)}) %collective-permute-start.8) | collective-permute-done | bytes 69664 | tf_op jit(solution)/shard_map/ppermute | solution.py:486
  32.2 0.0 collective-permute-done.9.refs_2_
  32.2 0.4 collective-permute-done.10.refs_0_
  32.6 1.6 %gradients.1 = (f32[4,128]{1,0:T(4,128)}, bf16[32,4,128]{2,1,0:T(4,128)(2,1)S(1)}) custom-call(f32[1,272,128]{2,1,0:T(8,128)S(1)} %summed.1.own, bf16[272,128]{1,0:T(8,128)(2,1)S(1)} %collective-permute-done.10.refs_0_, f32[4,128]{1,0:T(4,128)S(1)} %get-tuple-element.34.refs_1_), custom_call_target="tpu_custom_call" | custom-call | flops 2000000000 | bytes 6000000 | tf_op jit(solution)/shard_map/gradients/pallas_call | solution.py:391
  34.2 10.8 %all_to_all.5 = bf16[32,4,128]{2,1,0:T(4,128)(2,1)S(1)} all-to-all(bf16[32,4,128]{2,1,0:T(4,128)(2,1)S(1)} %get-tuple-element.36), channel_id=1, replica_groups=mesh['user'=8,'grp'=4] {'user','grp'}, dimensions={0} | all-to-all | bytes 65536 | tf_op jit(solution)/shard_map/all_to_all | solution.py:537
  45.0 1.1 %user_side.1 = f32[1024,128]{1,0:T(8,128)} custom-call(s32[1]{0:T(128)} %bitcast.me_s, bf16[128,128]{1,0:T(8,128)(2,1)S(1)} %bitcast.2, bf16[1024,256]{1,0:T(8,128)(2,1)S(1)} %flip.1.c_both), custom_call_target="tpu_custom_call" | custom-call | flops 1000000000 | bytes 3000000 | tf_op jit(solution)/shard_map/user_side/pallas_call | solution.py:444
  (3 shorter events, 0.1 us)
Async XLA Ops:
  0.6 10.2 %collective-permute-start.4 = (bf16[1024,128]{1,0:T(8,128)(2,1)}, bf16[1024,128]{1,0:T(8,128)(2,1)S(1)}, u32[]{:S(2)}, u32[]{:S(2)}) collective-permute-start(bf16[1024,128]{1,0:T(8,128)(2,1)} %refs_4_.7), channel_id=1, source_target_pairs={{0,2},{1,3},{2,0},{3,1},{4,6},{5,7},{6,4},{7,5},{8,10},{9,11},{10,... | collective-permute-start | bytes 786440 | tf_op jit(solution)/shard_map/ppermute | solution.py:486
  3.7 8.0 %collective-permute-start.3 = (bf16[1024,128]{1,0:T(8,128)(2,1)}, bf16[1024,128]{1,0:T(8,128)(2,1)S(1)}, u32[]{:S(2)}, u32[]{:S(2)}) collective-permute-start(bf16[1024,128]{1,0:T(8,128)(2,1)} %refs_4_.7), channel_id=1, source_target_pairs={{0,1},{1,0},{2,3},{3,2},{4,5},{5,4},{6,7},{7,6},{8,9},{9,8},{10,11... | collective-permute-start | bytes 786440 | tf_op jit(solution)/shard_map/ppermute | solution.py:486
  8.6 3.1 %collective-permute-start = (bf16[32,1280]{1,0:T(8,128)(2,1)S(1)}, bf16[32,1280]{1,0:T(8,128)(2,1)S(1)}, u32[]{:S(2)}, u32[]{:S(2)}) collective-permute-start(bf16[32,1280]{1,0:T(8,128)(2,1)S(1)} %get-tuple-element.21), channel_id=1, source_target_pairs={{0,1},{1,0},{2,3},{3,2},{4,5},{5,4},{6,7},{7,6},{8,9},{9,8},{10,11... | collective-permute-start | bytes 245768 | tf_op jit(solution)/shard_map/ppermute | solution.py:486
  9.2 5.3 %collective-permute-start.1 = (bf16[32,1280]{1,0:T(8,128)(2,1)S(1)}, bf16[32,1280]{1,0:T(8,128)(2,1)S(1)}, u32[]{:S(2)}, u32[]{:S(2)}) collective-permute-start(bf16[32,1280]{1,0:T(8,128)(2,1)S(1)} %get-tuple-element.22), channel_id=1, source_target_pairs={{0,2},{1,3},{2,0},{3,1},{4,6},{5,7},{6,4},{7,5},{8,10},{9,11},{10,... | collective-permute-start | bytes 245768 | tf_op jit(solution)/shard_map/ppermute | solution.py:486
  9.3 6.1 %collective-permute-start.2 = (bf16[32,1280]{1,0:T(8,128)(2,1)S(1)}, bf16[32,1280]{1,0:T(8,128)(2,1)S(1)}, u32[]{:S(2)}, u32[]{:S(2)}) collective-permute-start(bf16[32,1280]{1,0:T(8,128)(2,1)S(1)} %get-tuple-element.23), channel_id=1, source_target_pairs={{0,3},{1,2},{2,1},{3,0},{4,7},{5,6},{6,5},{7,4},{8,11},{9,10},{10,... | collective-permute-start | bytes 245768 | tf_op jit(solution)/shard_map/ppermute | solution.py:486
  10.8 1.0 %copy-start = (bf16[1024,128]{1,0:T(8,128)(2,1)S(1)}, bf16[1024,128]{1,0:T(8,128)(2,1)}, u32[]{:S(2)}) copy-start(bf16[1024,128]{1,0:T(8,128)(2,1)} %refs_4_.7) | copy-start | bytes 786436
  10.9 4.4 %collective-permute-start.5 = (bf16[1024,128]{1,0:T(8,128)(2,1)S(1)}, bf16[1024,128]{1,0:T(8,128)(2,1)S(1)}, u32[]{:S(2)}, u32[]{:S(2)}) collective-permute-start(bf16[1024,128]{1,0:T(8,128)(2,1)S(1)} %collective-permute-done.4.u.refs_1_.refs_4_.refs_6_), channel_id=1, source_target_pairs={{0,1},{1,0},{2,3},{3,2},{4,5},{5,4},{6,7},{7,6},{8,9},{9,8},{10,11... | collective-permute-start | bytes 786440 | tf_op jit(solution)/shard_map/ppermute | solution.py:486
  16.2 6.4 %collective-permute-start.6 = (bf16[2,272,128]{2,1,0:T(8,128)(2,1)S(1)}, bf16[2,272,128]{2,1,0:T(8,128)(2,1)S(1)}, u32[]{:S(2)}, u32[]{:S(2)}) collective-permute-start(bf16[2,272,128]{2,1,0:T(8,128)(2,1)S(1)} %systems.5), channel_id=1, source_target_pairs={{0,4},{1,5},{2,6},{3,7},{4,0},{5,1},{6,2},{7,3},{8,12},{9,13},{10,... | collective-permute-start | bytes 417800 | tf_op jit(solution)/shard_map/ppermute | solution.py:486
  19.0 8.9 %collective-permute-start.7 = (bf16[2,272,128]{2,1,0:T(8,128)(2,1)S(1)}, bf16[2,272,128]{2,1,0:T(8,128)(2,1)S(1)}, u32[]{:S(2)}, u32[]{:S(2)}) collective-permute-start(bf16[2,272,128]{2,1,0:T(8,128)(2,1)S(1)} %systems.6), channel_id=1, source_target_pairs={{0,4},{1,5},{2,6},{3,7},{4,0},{5,1},{6,2},{7,3},{8,12},{9,13},{10,... | collective-permute-start | bytes 417800 | tf_op jit(solution)/shard_map/ppermute | solution.py:486
  22.6 9.5 %collective-permute-start.9 = (bf16[272,128]{1,0:T(8,128)(2,1)S(1)}, bf16[272,128]{1,0:T(8,128)(2,1)S(1)}, u32[]{:S(2)}, u32[]{:S(2)}) collective-permute-start(bf16[272,128]{1,0:T(8,128)(2,1)S(1)} %get-tuple-element.30), channel_id=1, source_target_pairs={{0,16},{1,17},{2,18},{3,19},{4,20},{5,21},{6,22},{7,23},{8,24},{9,... | collective-permute-start | bytes 208904 | tf_op jit(solution)/shard_map/ppermute | solution.py:486
  25.3 6.9 %collective-permute-start.8 = (bf16[272,128]{1,0:T(8,128)(2,1)S(1)}, bf16[272,128]{1,0:T(8,128)(2,1)S(1)}, u32[]{:S(2)}, u32[]{:S(2)}) collective-permute-start(bf16[272,128]{1,0:T(8,128)(2,1)S(1)} %get-tuple-element.33), channel_id=1, source_target_pairs={{0,24},{1,25},{2,26},{3,27},{4,28},{5,29},{6,30},{7,31},{8,16},{9,... | collective-permute-start | bytes 208904 | tf_op jit(solution)/shard_map/ppermute | solution.py:486
  28.0 4.6 %collective-permute-start.10 = (bf16[272,128]{1,0:T(8,128)(2,1)S(1)}, bf16[272,128]{1,0:T(8,128)(2,1)S(1)}, u32[]{:S(2)}, u32[]{:S(2)}) collective-permute-start(bf16[272,128]{1,0:T(8,128)(2,1)S(1)} %merge.3), channel_id=1, source_target_pairs={{0,8},{1,9},{2,10},{3,11},{4,12},{5,13},{6,14},{7,15},{8,0},{9,1},... | collective-permute-start | bytes 208904 | tf_op jit(solution)/shard_map/ppermute | solution.py:486
